TPU v7x, 32 devices: a whole 2x2x4 slice. The times are simulated.
32 devices in a mesh: grp: 2 (over y), tm: 4 (over x, core), chan: 4 (over z).
Axes of the slice: x: 2, y: 2, z: 4, core: 2. Of those that a mesh axis runs over, the one named last changes fastest.
Arguments:
- records: bfloat16 [512, 3, 1024], P(('grp', 'tm', 'chan')), parts along dimension 0, may hold values from -6 to 6
- templates: bfloat16 [256, 3, 200, 256], P(('tm', 'chan')), may hold values from -6 to 6
- moveouts: int32 [256, 3], P(('tm', 'chan')), may hold values from 0 to 999
- uptime: int32 [512, 2], P(('grp', 'tm', 'chan')), parts along dimension 0, may hold values from 0 to 512
Outputs:
- cccsum: float32 [256, 2048], P(None, ('grp', 'tm', 'chan')), parts along dimension 1
There are 2 independent parts, one for each index of `grp`. A program takes and returns all parts, laid end to end along the dimension named above; an argument that names none is the same for every part. Nothing has to cross between parts.
All inputs are finite; a program needn't handle non-finite values.
Results may differ from a plain program's by a relative error of at most 0.0041.
Values may be sent and summed in bfloat16 or wider, within the bound.
No kernel may reach another device: no remote copies, remote signals or barrier semaphores. Data moves between devices by JAX's collectives and lax.ppermute only.
A program may use at most 64 MiB of HBM per device.

v0:
```python
import jax
import jax.numpy as jnp
from jax import lax
from jax.sharding import PartitionSpec as P

MAXMO = 1000


def sender_prep(records, moveouts, uptime):
    stations, components, length = records.shape
    block_count = uptime.shape[1]
    offsets = lax.broadcasted_iota(jnp.int32, (block_count, length // block_count), 1)
    live_mask = (offsets[None, :, :] < uptime[:, :, None]).reshape(stations, 1, length)
    masked = jnp.where(live_mask, records, jnp.zeros((), records.dtype))
    padded = jnp.concatenate(
        [masked, jnp.zeros((stations, components, MAXMO), records.dtype)], axis=2
    )
    flat_rows = padded.reshape(stations * components, length + MAXMO)
    starts = moveouts.reshape(stations * components)

    def slice_row(record_row, start_at):
        return lax.dynamic_slice_in_dim(record_row, start_at, length)

    shifted = jax.vmap(slice_row)(flat_rows, starts)
    return shifted.reshape(stations, components, length)


def normalize_templates(templates):
    values = templates.astype(jnp.float32)
    squares = jnp.sum(values * values, axis=2, keepdims=True)
    return (values * lax.rsqrt(squares + 1e-06)).astype(jnp.bfloat16)


def correlate_station(station_rows, unit_rows):
    channels, length = station_rows.shape
    window_len = unit_rows.shape[1]
    out_len = length - window_len + 1
    tiled_rows = jnp.tile(station_rows, (1, window_len + 1))[:, : window_len * (length + 1)]
    windows = tiled_rows.reshape(channels, window_len, length + 1)[:, :, :out_len]
    energy = jnp.sum(jnp.square(windows.astype(jnp.float32)), axis=1)
    factor = lax.rsqrt(jnp.maximum(energy, 1.0))
    scaled = (windows.astype(jnp.float32) * factor[:, None, :]).astype(jnp.bfloat16)
    unit_flat = unit_rows.reshape(channels * window_len, unit_rows.shape[2])
    return jnp.dot(
        unit_flat.T,
        scaled.reshape(channels * window_len, out_len),
        preferred_element_type=jnp.float32,
    )


def margin_blocks(signal, block_len, window_len):
    lead_shape = signal.shape[:-1]
    length = signal.shape[-1]
    block_count = length // block_len
    padded = jnp.concatenate([signal, jnp.zeros(lead_shape + (block_len,), signal.dtype)], axis=-1)
    grid = padded.reshape(lead_shape + (block_count + 1, block_len))
    main_part = grid[..., :block_count, :]
    rim_part = grid[..., 1:, : window_len - 1]
    return jnp.concatenate([main_part, rim_part], axis=-1)


def body(records, templates, moveouts, uptime):
    shifted = sender_prep(records, moveouts, uptime)
    unit_bank = normalize_templates(templates)
    window_len = unit_bank.shape[2]
    time_groups = lax.axis_size("tm")
    blocks = margin_blocks(shifted, shifted.shape[2] // time_groups, window_len)
    extended = lax.all_to_all(blocks, "tm", split_axis=2, concat_axis=0, tiled=True)[:, :, 0, :]
    initial = jnp.zeros((unit_bank.shape[3], extended.shape[2] - window_len + 1), jnp.float32)
    piece_rows = lax.all_gather(unit_bank, "tm", axis=0, tiled=True)

    def one_station(station, running_sum):
        station_rows = lax.dynamic_index_in_dim(extended, station, 0, keepdims=False)
        unit_rows = lax.dynamic_index_in_dim(piece_rows, station, 0, keepdims=False)
        return running_sum + correlate_station(station_rows, unit_rows)

    partial_value = lax.fori_loop(0, piece_rows.shape[0], one_station, initial)
    return lax.psum_scatter(partial_value, "chan", scatter_dimension=1, tiled=True)


def solution(mesh):
    placed = (
        P(("grp", "tm", "chan"), None, None),
        P(("tm", "chan"), None, None, None),
        P(("tm", "chan"), None),
        P(("grp", "tm", "chan"), None),
    )
    return jax.shard_map(
        body, mesh=mesh, in_specs=placed, out_specs=P(None, ("grp", "tm", "chan")), check_vma=False
    )
```

profile of v0, /device:TPU:0, one launch (start us, length us, event | category | flops | bytes accessed | tf_op | source)
XLA Modules:
  0.0 490.9 jit_solution(4632010004564827906)
XLA Ops:
  6.5 3.5 fusion.2
  10.1 5.8 %fusion.3 = bf16[16,3,200,256]{3,2,1,0:T(8,128)(2,1)} fusion(bf16[16,3,200,256]{3,2,1,0:T(8,128)(2,1)} %param.7, f32[16,3,256]{2,1,0:T(4,128)S(1)} %add_rsqrt_fusion), kind=kLoop, calls=%fused_computation.12 | loop fusion | flops 7372800 | bytes 9879552 | tf_op jit(solution)/shard_map/convert_element_type | solution.py:31
  16.8 99.4 %while.15 = (s32[]{:T(128)}, bf16[48,2024]{1,0:T(8,128)(2,1)S(1)}, s32[48,2]{0,1:T(2,128)S(1)}, bf16[48,1024]{1,0:T(8,128)(2,1)S(1)}, s32[]{:T(128)}, /*index=5*/s32[]{:T(128)}) while((s32[]{:T(128)}, bf16[48,2024]{1,0:T(8,128)(2,1)S(1)}, s32[48,2]{0,1:T(2,128)S(1)}, bf16[48,1024]{1,0:T(8,128)(2,1)S(1)}, s32[]{:T(128)}, /*index=5*/s32[]{:T(128)}) %tuple.49), condition=%wide.while_cond, body=%wide.while_body.sunk | while | flops 2 | bytes 8305 | solution.py:22
  117.4 4.2 all-to-all-start
  121.6 7.8 %all-to-all-done = bf16[16,3,4,455]{3,0,1,2:T(8,128)(2,1)S(1)} async-done(((bf16[16,3,4,455]{3,0,1,2:T(8,128)(2,1)}), bf16[16,3,4,455]{3,0,1,2:T(8,128)(2,1)S(1)}, u32[]{:S(2)}, u32[]{:S(2)}) %all-to-all-start) | async-done | bytes 174752 | tf_op jit(solution)/shard_map/all_to_all | solution.py:68
  129.6 15.6 %all-gather.2.cloned.1.call-done = bf16[64,3,200,256]{3,2,1,0:T(8,128)(2,1)} async-done(((bf16[16,3,200,256]{3,2,1,0:T(8,128)(2,1)}), bf16[64,3,200,256]{3,2,1,0:T(8,128)(2,1)}) %all-gather.2.cloned.1.call-update) | async-done | bytes 19660816 | tf_op jit(solution)/shard_map/all_gather | solution.py:70
  145.2 318.2 %while.16 = (s32[]{:T(128)}, f32[256,256]{1,0:T(8,128)S(1)}, bf16[64,3,200,256]{3,2,1,0:T(8,128)(2,1)}, bf16[64,3,455]{2,1,0:T(4,128)(2,1)S(1)}, s32[]{:T(128)}, /*index=5*/s32[]{:T(128)}) while((s32[]{:T(128)}, f32[256,256]{1,0:T(8,128)S(1)}, bf16[64,3,200,256]{3,2,1,0:T(8,128)(2,1)}, bf16[64,3,455]{2,1,0:T(4,128)(2,1)S(1)}, ...), condition=%wide.region_3.4_spmd.clone, body=%wide.region_1.3_spmd.clone.sunk | while | flops 79695872 | bytes 6530243 | solution.py:77
  145.3 1.6 tile.29
  150.3 1.6 tile.29
  155.2 1.6 tile.29
  160.2 1.6 tile.29
  165.2 1.6 tile.29
  170.1 1.6 tile.29
  180.1 1.6 tile.29
  185.1 1.6 tile.29
  190.0 1.6 tile.29
  195.0 1.6 tile.29
  200.0 1.6 tile.29
  204.9 1.6 tile.29
  209.9 1.6 tile.29
  214.9 1.6 tile.29
  219.9 1.6 tile.29
  224.8 1.6 tile.29
  229.8 1.6 tile.29
  234.8 1.6 tile.29
  239.7 1.6 tile.29
  244.7 1.6 tile.29
  249.7 1.6 tile.29
  254.7 1.6 tile.29
  259.6 1.6 tile.29
  269.6 1.6 tile.29
  464.3 19.8 %reduce-scatter.2.cloned.1.call-done = f32[256,64]{0,1:T(8,128)} async-done(((f32[256,256]{0,1:T(8,128)}), f32[256,64]{0,1:T(8,128)}) %reduce-scatter.2.cloned.1.call-update) | async-done | bytes 65552 | tf_op jit(solution)/shard_map/reduce_scatter | solution.py:78
  (847 shorter events, 376.5 us)
Async XLA Ops:
  6.5 9.4 %copy-start.2 = (s32[16,2]{0,1:T(2,128)S(1)}, s32[16,2]{0,1:T(2,128)}, u32[]{:S(2)}) copy-start(s32[16,2]{0,1:T(2,128)} %param.9) | copy-start | bytes 388
  6.5 9.6 %copy-start = (bf16[16,3,1024]{2,0,1:T(8,128)(2,1)S(1)}, bf16[16,3,1024]{2,0,1:T(8,128)(2,1)}, u32[]{:S(2)}) copy-start(bf16[16,3,1024]{2,0,1:T(8,128)(2,1)} %param.6) | copy-start | bytes 294916
  6.5 10.0 %copy-start.1 = (s32[16,3]{0,1:T(4,128)S(1)}, s32[16,3]{0,1:T(4,128)}, u32[]{:S(2)}) copy-start(s32[16,3]{0,1:T(4,128)} %param.8) | copy-start | bytes 580
  6.5 138.7 %all-gather.2.cloned.1.call-start = ((), (), s32[]{:S(2)}) async-start(), calls=%async_computation.2 | async-start | bytes 24576000 | tf_op jit(solution)/shard_map/all_gather | solution.py:70
  117.4 12.0 %all-to-all-start = ((bf16[16,3,4,455]{3,0,1,2:T(8,128)(2,1)}), bf16[16,3,4,455]{3,0,1,2:T(8,128)(2,1)S(1)}, u32[]{:S(2)}, u32[]{:S(2)}) async-start(bf16[16,3,4,455]{3,0,1,2:T(8,128)(2,1)} %copy.33), calls=%async_computation | async-start | bytes 393216 | tf_op jit(solution)/shard_map/all_to_all | solution.py:68
  121.6 362.5 %reduce-scatter.2.cloned.1.call-start = ((), (), s32[]{:S(2)}) async-start(), calls=%async_computation.3 | async-start | bytes 327680 | tf_op jit(solution)/shard_map/reduce_scatter | solution.py:78
Sparse Core Ops, SparseCore 0:
  16.0 129.1 all-gather.1
  464.4 19.6 reduce-scatter.1
where the time goes:
time: 494 us; the launch traced here: 491 us
  local copies, waits for them, and re-layouts  382 us (77%)
  waiting for transfers between devices  43.3 us (9%)
  matrix products  22.9 us (5%)
  other arithmetic  19 us (4%)
  between operations  13.6 us (3%)
  loops' own time  6.32 us (1%)
    another operation x192, local copies, waits for them, and re-layouts, correlate_station(): jnp.tile(station_rows, (1, window_len + 1))[:, :window_len * (length + 1)]  104 us
    gather x192, local copies, waits for them, and re-layouts  98.2 us
    reshape x64, local copies, waits for them, and re-layouts, correlate_station(): tiled_rows.reshape(channels, window_len, length + 1)[:, :, :out_len]  96.7 us
    dynamic_slice x64, local copies, waits for them, and re-layouts, one_station(): unit_rows = lax.dynamic_index_in_dim(piece_rows, station, 0, keepdims=False)  63.6 us
    dot_general x64, matrix products, correlate_station(): jnp.dot(unit_flat.T, scaled.reshape(channels * window_len, out_len), pref...  22.9 us
    reduce_scatter x1, waiting for transfers between devices, body(): lax.psum_scatter(partial_value, 'chan', scatter_dimension=1, tiled=True)  19.8 us
    slice x64, local copies, waits for them, and re-layouts, correlate_station(): jnp.tile(station_rows, (1, window_len + 1))[:, :window_len * (length + 1)]  16.2 us
    all_gather x1, waiting for transfers between devices, body(): piece_rows = lax.all_gather(unit_bank, 'tm', axis=0, tiled=True)  15.6 us
  transfers between devices with their start and end apart: 3, of which 3 were waited for; matrix products, arithmetic and copies ran while one was open for 20% of the time, Pallas kernels for 0%

commit v1 on v0

v1 whole, which is shorter than its diff:
```python
import functools

import jax
import jax.numpy as jnp
from jax import lax
from jax.experimental import pallas as pl
from jax.experimental.pallas import tpu as pltpu
from jax.sharding import PartitionSpec as P

MAXMO = 1000
LANES = 128
GROUP = 16


def up(value, unit):
    return -(-value // unit) * unit


def window_sum(values, window):
    width = values.shape[1]

    def ahead(array, by):
        return array if by == 0 else pltpu.roll(array, width - by, 1)

    total, offset, size, run = None, 0, 1, values
    while size <= window:
        if window & size:
            piece = ahead(run, offset)
            total = piece if total is None else total + piece
            offset += size
        size *= 2
        if size <= window:
            run = run + ahead(run, size // 2)
    return total


def correlate_kernel(
    core_ref, moveouts_ref, uptime_ref, records_ref, templates_ref,
    send_ref, keep_ref,
    masked, shifted, factor, columns, hankel, bank, total,
    *, stations, components, length, window, block_count,
):
    station = pl.program_id(0)
    channels = stations * components
    rows = masked.shape[0]
    tiles = length // LANES
    depth_tiles = up(window, LANES) // LANES
    block_len = length // block_count
    span = shifted.shape[1]

    @pl.when(station == 0)
    def prologue():
        masked[...] = jnp.zeros(masked.shape, jnp.float32)
        offsets = lax.broadcasted_iota(jnp.int32, (components, block_len), 1)
        for s in range(stations):
            for b in range(block_count):
                part = slice(b * block_len, (b + 1) * block_len)
                values = records_ref[s, :, part].astype(jnp.float32)
                live = offsets < uptime_ref[s * block_count + b]
                masked[s * components:(s + 1) * components, part] = jnp.where(live, values, 0.0)
        shifted[...] = jnp.zeros(shifted.shape, jnp.float32)

        def shift_one(c, carry):
            moveout = moveouts_ref[c]
            base = pl.multiple_of(moveout // LANES * LANES, LANES)
            row = masked[pl.ds(c, 1), pl.ds(base, span)]
            shifted[pl.ds(c, 1), :] = pltpu.roll(row, span - (moveout - base), 1)
            return carry

        lax.fori_loop(0, channels, shift_one, 0)
        factor[...] = jnp.zeros(factor.shape, jnp.float32)
        for g in range(0, rows, 8):
            values = shifted[g:g + 8, :]
            energy = window_sum(values * values, window)[:, :length]
            factor[g:g + 8, :] = lax.rsqrt(jnp.maximum(energy, 1.0))
        source = lax.broadcasted_iota(jnp.int32, (LANES, LANES), 1)
        target = lax.broadcasted_iota(jnp.int32, (LANES, LANES), 0)
        mirrored = target // GROUP * GROUP + (GROUP - 1 - target % GROUP)
        swap = jnp.where(source == mirrored, 1.0, 0.0).astype(jnp.float32)
        for i in range(tiles):
            columns[i * LANES:(i + 1) * LANES, :] = lax.dot_general(
                swap, factor[:, i * LANES:(i + 1) * LANES],
                (((1,), (1,)), ((), ())),
                precision=lax.Precision.HIGHEST,
                preferred_element_type=jnp.float32,
            )
        bank[...] = jnp.zeros(bank.shape, bank.dtype)
        total[...] = jnp.zeros(total.shape, total.dtype)

    for j in range(components):
        values = templates_ref[0, j].astype(jnp.float32)
        squares = jnp.sum(values * values, axis=0, keepdims=True)
        unit = (values * lax.rsqrt(squares + 1e-06)).astype(jnp.bfloat16)
        bank[j * depth_tiles * LANES:j * depth_tiles * LANES + window, :] = unit

    for j in range(components):
        c = station * components + j
        half = jnp.broadcast_to(shifted[pl.ds(c, 1), :], (8, span))
        strip = jnp.concatenate(
            [pltpu.roll(half, span - GROUP + 1 + b, 1, stride=1, stride_axis=0) for b in (0, 8)],
            axis=0,
        ).astype(jnp.bfloat16)
        for a in range(LANES // GROUP):
            rolled = strip if a == 0 else pltpu.roll(strip, span - a * GROUP, 1)
            for i in range(tiles + depth_tiles - 1):
                hankel[j, i, a * GROUP:(a + 1) * GROUP, :] = rolled[:, i * LANES:(i + 1) * LANES]

    def one_tile(i, carry):
        at = pl.multiple_of(i * LANES, LANES)
        column = columns[pl.ds(at, LANES), :]
        parts = []
        for j in range(components):
            lane = jnp.full((LANES, LANES), station * components + j, jnp.int32)
            scale = jnp.take_along_axis(column, lane, axis=1).astype(jnp.bfloat16)
            for d in range(depth_tiles):
                parts.append(hankel[j, i + d] * scale)
        total[pl.ds(at, LANES), :] += jnp.dot(
            jnp.concatenate(parts, axis=1), bank[...], preferred_element_type=jnp.float32
        )
        return carry

    lax.fori_loop(0, tiles, one_tile, 0, unroll=tiles <= 8)

    @pl.when(station == stations - 1)
    def finish():
        core = core_ref[0]
        hops, region = keep_ref.shape[0], keep_ref.shape[1]
        for x in range(hops):
            own = pl.multiple_of((2 * x + core) * region, region)
            other = pl.multiple_of((2 * x + 1 - core) * region, region)
            keep_ref[x] = total[pl.ds(own, region), :]
            send_ref[x] = total[pl.ds(other, region), :].astype(send_ref.dtype)


def correlate(core, records, templates, moveouts, uptime, hops):
    stations, components, length = records.shape
    window, bank_size = templates.shape[2:]
    block_count = uptime.shape[1]
    depth = up(window, LANES)
    rows = up(stations * components, 8)
    reach = length + depth + LANES + up(MAXMO, LANES)
    region = length // (2 * hops)
    body = functools.partial(
        correlate_kernel, stations=stations, components=components, length=length,
        window=window, block_count=block_count,
    )
    whole = lambda s, *_: (0, 0, 0)
    return pl.pallas_call(
        body,
        grid_spec=pltpu.PrefetchScalarGridSpec(
            num_scalar_prefetch=3,
            grid=(stations,),
            in_specs=[
                pl.BlockSpec(records.shape, whole),
                pl.BlockSpec((1,) + templates.shape[1:], lambda s, *_: (s, 0, 0, 0)),
            ],
            out_specs=[
                pl.BlockSpec((hops, region, bank_size), whole),
                pl.BlockSpec((hops, region, bank_size), whole),
            ],
            scratch_shapes=[
                pltpu.VMEM((rows, reach), jnp.float32),
                pltpu.VMEM((rows, length + depth + LANES), jnp.float32),
                pltpu.VMEM((up(rows, LANES), length), jnp.float32),
                pltpu.VMEM((length, up(rows, LANES)), jnp.float32),
                pltpu.VMEM((components, (length + depth) // LANES - 1, LANES, LANES), jnp.bfloat16),
                pltpu.VMEM((components * depth, bank_size), jnp.bfloat16),
                pltpu.VMEM((length, bank_size), jnp.float32),
            ],
        ),
        out_shape=[
            jax.ShapeDtypeStruct((hops, region, bank_size), jnp.bfloat16),
            jax.ShapeDtypeStruct((hops, region, bank_size), jnp.float32),
        ],
        compiler_params=pltpu.CompilerParams(vmem_limit_bytes=48 * 2**20),
        name="correlate",
    )(core, moveouts.reshape(-1), uptime.reshape(-1), records, templates)


def body(records, templates, moveouts, uptime):
    tm, chan = lax.axis_size("tm"), lax.axis_size("chan")
    hops = tm // 2
    t, z = lax.axis_index("tm"), lax.axis_index("chan")
    x, core = t // 2, t % 2
    send, keep = correlate(core.reshape(1), records, templates, moveouts, uptime, hops)
    got = lax.ppermute(send, "tm", [(i, i ^ 1) for i in range(tm)])
    mine = keep + got.astype(jnp.float32)
    result = lax.dynamic_index_in_dim(mine, x, 0, keepdims=False)
    for step in range(1, hops):
        block = lax.dynamic_index_in_dim(mine, (x + step) % hops, 0, keepdims=False)
        perm = [(i, ((i // 2 + step) % hops) * 2 + i % 2) for i in range(tm)]
        result = result + lax.ppermute(block.astype(jnp.bfloat16), "tm", perm).astype(jnp.float32)
    mine = result.reshape(chan, result.shape[0] // chan, result.shape[1])
    result = lax.dynamic_index_in_dim(mine, z, 0, keepdims=False)
    for step in range(1, chan):
        block = lax.dynamic_index_in_dim(mine, (z + step) % chan, 0, keepdims=False)
        perm = [(i, (i + step) % chan) for i in range(chan)]
        result = result + lax.ppermute(block.astype(jnp.bfloat16), "chan", perm).astype(jnp.float32)
    samples, bank_size = result.shape
    result = result.reshape(samples // GROUP, GROUP, bank_size)[:, ::-1, :]
    return result.reshape(samples, bank_size).T


def solution(mesh):
    placed = (
        P(("grp", "tm", "chan"), None, None),
        P(("tm", "chan"), None, None, None),
        P(("tm", "chan"), None),
        P(("grp", "tm", "chan"), None),
    )
    return jax.shard_map(
        body, mesh=mesh, in_specs=placed, out_specs=P(None, ("grp", "tm", "chan")), check_vma=False
    )
```

time: 494 us -> 48.4 us (0.10)
  local copies, waits for them, and re-layouts: 382 us -> 5.77 us
  waiting for transfers between devices: 43.3 us -> 7.53 us
  Pallas kernels: 0 us -> 25.5 us
  matrix products: 22.9 us -> 0 us
  other arithmetic: 19 us -> 0.09 us
  between operations: 13.6 us -> 0.07 us
  loops' own time: 6.32 us -> 0 us
  starting transfers between devices: 4.21 us -> 9.25 us
    another operation x192 -> x0, local copies, waits for them, and re-layouts: 104 us -> none  [correlate_station(): jnp.tile(station_rows, (1, window_len + 1))[:, :window_len * (length + 1)]]
    gather x192 -> x0, local copies, waits for them, and re-layouts: 98.2 us -> none
    reshape x68 -> x2, local copies, waits for them, and re-layouts: 97.2 us -> 0.17 us  [the longest x1 0.09 us: correlate(): moveouts.reshape(-1)]
    dynamic_slice x64 -> x0, local copies, waits for them, and re-layouts: 63.6 us -> none  [one_station(): unit_rows = lax.dynamic_index_in_dim(piece_rows, station, 0, keepdims=False)]
    pallas_call x0 -> x1, Pallas kernels: none -> 25.5 us  [correlate(): pl.pallas_call(body, grid_spec=pltpu.PrefetchScalarGridSpec(num_scalar_pr...]
    dot_general x64 -> x0, matrix products: 22.9 us -> none  [correlate_station(): jnp.dot(unit_flat.T, scaled.reshape(channels * window_len, out_len), pref...]
    reduce_scatter x1 -> x0, waiting for transfers between devices: 19.8 us -> none  [body(): lax.psum_scatter(partial_value, 'chan', scatter_dimension=1, tiled=True)]
    slice x66 -> x0, local copies, waits for them, and re-layouts: 16.3 us -> none  [the longest x64 16.2 us: correlate_station(): jnp.tile(station_rows, (1, window_len + 1))[:, :window_len * (length + 1)]]
  transfers between devices with their start and end apart: 3 -> 5, of which waited for: 3 -> 5; matrix products, arithmetic and copies ran while one was open for 20% -> 0% of each run, Pallas kernels for 0% -> 0%
where the time goes in v1:
time: 48.4 us; the launch traced here: 48.2 us
  Pallas kernels  25.5 us (53%)
  starting transfers between devices  9.25 us (19%)
  waiting for transfers between devices  7.53 us (16%)
  local copies, waits for them, and re-layouts  5.77 us (12%)
    pallas_call x1, Pallas kernels, correlate(): pl.pallas_call(body, grid_spec=pltpu.PrefetchScalarGridSpec(num_scalar_pr...  25.5 us
    ppermute x3, starting transfers between devices, body(): lax.ppermute(block.astype(jnp.bfloat16), 'chan', perm).astype(jnp.float32)  5.81 us
    unnamed x5, local copies, waits for them, and re-layouts  4.89 us
    ppermute x1, waiting for transfers between devices, body(): lax.ppermute(block.astype(jnp.bfloat16), 'tm', perm).astype(jnp.float32)  3.8 us
    ppermute x1, starting transfers between devices, body(): lax.ppermute(block.astype(jnp.bfloat16), 'tm', perm).astype(jnp.float32)  2.93 us
    ppermute x3, waiting for transfers between devices, body(): lax.ppermute(block.astype(jnp.bfloat16), 'chan', perm).astype(jnp.float32)  2.57 us
    ppermute x1, waiting for transfers between devices, body(): got = lax.ppermute(send, 'tm', [(i, i ^ 1) for i in range(tm)])  1.16 us
  transfers between devices with their start and end apart: 5, of which 5 were waited for; matrix products, arithmetic and copies ran while one was open for 0% of the time, Pallas kernels for 0%

profile of v1, /device:TPU:0, one launch (start us, length us, event | category | flops | bytes accessed | tf_op | source)
XLA Modules:
  0.0 48.2 jit_solution(13002754687255599177)
XLA Ops:
  0.0 1.0 %copy.10.records_ref = bf16[16,3,1024]{2,1,0:T(4,128)(2,1)S(1)} copy(bf16[16,3,1024]{2,0,1:T(8,128)(2,1)} %param.4) | data formatting | bytes 196608 | tf_op args[0]
  1.0 0.8 %copy.8 = s32[16,3]{1,0:T(8,128)S(1)} copy(s32[16,3]{0,1:T(4,128)} %param.6) | data formatting | bytes 384 | tf_op args[2]
  1.7 0.1 reshape.23.moveouts_ref
  1.8 0.8 %copy.9 = s32[16,2]{1,0:T(8,128)S(1)} copy(s32[16,2]{0,1:T(2,128)} %param.7) | data formatting | bytes 256 | tf_op args[3]
  2.6 0.1 reshape.24.uptime_ref
  2.7 0.0 copy-start
  2.7 2.4 %copy-done = bf16[16,3,200,256]{3,2,1,0:T(8,128)(2,1)S(1)} copy-done((bf16[16,3,200,256]{3,2,1,0:T(8,128)(2,1)S(1)}, bf16[16,3,200,256]{3,2,1,0:T(8,128)(2,1)}, u32[]{:S(2)}) %copy-start) | copy-done | bytes 4915224
  5.1 25.5 %correlate.1 = (bf16[2,256,256]{2,1,0:T(8,128)(2,1)S(1)}, f32[2,256,256]{2,1,0:T(8,128)S(1)}) custom-call(s32[1]{0:T(128)} %bitcast.core_ref, s32[48]{0:T(128)S(1)} %reshape.23.moveouts_ref, s32[32]{0:T(128)S(1)} %reshape.24.uptime_ref, bf16[16,3,1024]{2,1,0:T(4,128)(2,1)S(1)} %copy.10.records_ref, bf16[16,3,200,256]{3,2,1,0:T(8,128)(2,1)S(1)} %copy-done), custom_call_target="tpu_custom_call" | custom-call | tf_op jit(solution)/shard_map/correlate/pallas_call | solution.py:148
  30.6 0.5 %collective-permute-start = (bf16[2,256,256]{2,1,0:T(8,128)(2,1)S(1)}, bf16[2,256,256]{2,1,0:T(8,128)(2,1)S(1)}, u32[]{:S(2)}, u32[]{:S(2)}) collective-permute-start(bf16[2,256,256]{2,1,0:T(8,128)(2,1)S(1)} %get-tuple-element.8), channel_id=1, source_target_pairs={{0,4},{4,0},{8,12},{12,8},{1,5},{5,1},{9,13},{13,9},{2,6},{6,2},{1... | collective-permute-start | bytes 786440 | tf_op jit(solution)/shard_map/ppermute | solution.py:186
  31.1 1.2 %collective-permute-done = bf16[2,256,256]{2,1,0:T(8,128)(2,1)S(1)} collective-permute-done((bf16[2,256,256]{2,1,0:T(8,128)(2,1)S(1)}, bf16[2,256,256]{2,1,0:T(8,128)(2,1)S(1)}, u32[]{:S(2)}, u32[]{:S(2)}) %collective-permute-start) | collective-permute-done | bytes 262176 | tf_op jit(solution)/shard_map/ppermute | solution.py:186
  32.3 0.1 convert_add_fusion
  32.4 2.9 %collective-permute-start.1 = (bf16[256,256]{1,0:T(8,128)(2,1)S(1)}, bf16[256,256]{1,0:T(8,128)(2,1)S(1)}, u32[]{:S(2)}, u32[]{:S(2)}) collective-permute-start(bf16[256,256]{1,0:T(8,128)(2,1)S(1)} %fusion), channel_id=1, source_target_pairs={{0,8},{4,12},{8,0},{12,4},{1,9},{5,13},{9,1},{13,5},{2,10},{6,14},... | collective-permute-start | bytes 393224 | tf_op jit(solution)/shard_map/ppermute | solution.py:192
  35.3 3.8 %collective-permute-done.1 = bf16[256,256]{1,0:T(8,128)(2,1)S(1)} collective-permute-done((bf16[256,256]{1,0:T(8,128)(2,1)S(1)}, bf16[256,256]{1,0:T(8,128)(2,1)S(1)}, u32[]{:S(2)}, u32[]{:S(2)}) %collective-permute-start.1) | collective-permute-done | bytes 131104 | tf_op jit(solution)/shard_map/ppermute | solution.py:192
  39.2 1.9 %collective-permute-start.2 = (bf16[64,256]{1,0:T(8,128)(2,1)S(1)}, bf16[64,256]{1,0:T(8,128)(2,1)S(1)}, u32[]{:S(2)}, u32[]{:S(2)}) collective-permute-start(bf16[64,256]{1,0:T(8,128)(2,1)S(1)} %get-tuple-element.9), channel_id=1, source_target_pairs={{0,1},{1,2},{2,3},{3,0},{4,5},{5,6},{6,7},{7,4},{8,9},{9,10},{10,1... | collective-permute-start | bytes 98312 | tf_op jit(solution)/shard_map/ppermute | solution.py:198
  41.0 2.6 %collective-permute-start.3 = (bf16[64,256]{1,0:T(8,128)(2,1)S(1)}, bf16[64,256]{1,0:T(8,128)(2,1)S(1)}, u32[]{:S(2)}, u32[]{:S(2)}) collective-permute-start(bf16[64,256]{1,0:T(8,128)(2,1)S(1)} %get-tuple-element.11), channel_id=1, source_target_pairs={{0,2},{1,3},{2,0},{3,1},{4,6},{5,7},{6,4},{7,5},{8,10},{9,11},{10,... | collective-permute-start | bytes 98312 | tf_op jit(solution)/shard_map/ppermute | solution.py:198
  43.6 1.3 %collective-permute-start.4 = (bf16[64,256]{1,0:T(8,128)(2,1)S(1)}, bf16[64,256]{1,0:T(8,128)(2,1)S(1)}, u32[]{:S(2)}, u32[]{:S(2)}) collective-permute-start(bf16[64,256]{1,0:T(8,128)(2,1)S(1)} %get-tuple-element.10), channel_id=1, source_target_pairs={{0,3},{1,0},{2,1},{3,2},{4,7},{5,4},{6,5},{7,6},{8,11},{9,8},{10,9... | collective-permute-start | bytes 98312 | tf_op jit(solution)/shard_map/ppermute | solution.py:198
  45.0 0.4 collective-permute-done.2
  45.4 0.6 %collective-permute-done.3 = bf16[64,256]{1,0:T(8,128)(2,1)S(1)} collective-permute-done((bf16[64,256]{1,0:T(8,128)(2,1)S(1)}, bf16[64,256]{1,0:T(8,128)(2,1)S(1)}, u32[]{:S(2)}, u32[]{:S(2)}) %collective-permute-start.3) | collective-permute-done | bytes 32800 | tf_op jit(solution)/shard_map/ppermute | solution.py:198
  46.0 1.6 %collective-permute-done.4 = bf16[64,256]{1,0:T(8,128)(2,1)S(1)} collective-permute-done((bf16[64,256]{1,0:T(8,128)(2,1)S(1)}, bf16[64,256]{1,0:T(8,128)(2,1)S(1)}, u32[]{:S(2)}, u32[]{:S(2)}) %collective-permute-start.4) | collective-permute-done | bytes 32800 | tf_op jit(solution)/shard_map/ppermute | solution.py:198
  47.6 0.7 %rev.3 = f32[4,16,256]{2,1,0:T(8,128)} reverse(f32[4,16,256]{2,1,0:T(8,128)S(1)} %bitcast.24), dimensions={1} | reverse | bytes 131072 | tf_op jit(solution)/shard_map/rev | solution.py:200
  (4 shorter events, 0.1 us)
Async XLA Ops:
  2.7 2.4 %copy-start = (bf16[16,3,200,256]{3,2,1,0:T(8,128)(2,1)S(1)}, bf16[16,3,200,256]{3,2,1,0:T(8,128)(2,1)}, u32[]{:S(2)}) copy-start(bf16[16,3,200,256]{3,2,1,0:T(8,128)(2,1)} %templates_ref.1) | copy-start | bytes 14745604
  30.6 1.7 %collective-permute-start = (bf16[2,256,256]{2,1,0:T(8,128)(2,1)S(1)}, bf16[2,256,256]{2,1,0:T(8,128)(2,1)S(1)}, u32[]{:S(2)}, u32[]{:S(2)}) collective-permute-start(bf16[2,256,256]{2,1,0:T(8,128)(2,1)S(1)} %get-tuple-element.8), channel_id=1, source_target_pairs={{0,4},{4,0},{8,12},{12,8},{1,5},{5,1},{9,13},{13,9},{2,6},{6,2},{1... | collective-permute-start | bytes 786440 | tf_op jit(solution)/shard_map/ppermute | solution.py:186
  32.4 6.7 %collective-permute-start.1 = (bf16[256,256]{1,0:T(8,128)(2,1)S(1)}, bf16[256,256]{1,0:T(8,128)(2,1)S(1)}, u32[]{:S(2)}, u32[]{:S(2)}) collective-permute-start(bf16[256,256]{1,0:T(8,128)(2,1)S(1)} %fusion), channel_id=1, source_target_pairs={{0,8},{4,12},{8,0},{12,4},{1,9},{5,13},{9,1},{13,5},{2,10},{6,14},... | collective-permute-start | bytes 393224 | tf_op jit(solution)/shard_map/ppermute | solution.py:192
  39.2 6.3 %collective-permute-start.2 = (bf16[64,256]{1,0:T(8,128)(2,1)S(1)}, bf16[64,256]{1,0:T(8,128)(2,1)S(1)}, u32[]{:S(2)}, u32[]{:S(2)}) collective-permute-start(bf16[64,256]{1,0:T(8,128)(2,1)S(1)} %get-tuple-element.9), channel_id=1, source_target_pairs={{0,1},{1,2},{2,3},{3,0},{4,5},{5,6},{6,7},{7,4},{8,9},{9,10},{10,1... | collective-permute-start | bytes 98312 | tf_op jit(solution)/shard_map/ppermute | solution.py:198
  41.0 4.9 %collective-permute-start.3 = (bf16[64,256]{1,0:T(8,128)(2,1)S(1)}, bf16[64,256]{1,0:T(8,128)(2,1)S(1)}, u32[]{:S(2)}, u32[]{:S(2)}) collective-permute-start(bf16[64,256]{1,0:T(8,128)(2,1)S(1)} %get-tuple-element.11), channel_id=1, source_target_pairs={{0,2},{1,3},{2,0},{3,1},{4,6},{5,7},{6,4},{7,5},{8,10},{9,11},{10,... | collective-permute-start | bytes 98312 | tf_op jit(solution)/shard_map/ppermute | solution.py:198
  43.6 3.9 %collective-permute-start.4 = (bf16[64,256]{1,0:T(8,128)(2,1)S(1)}, bf16[64,256]{1,0:T(8,128)(2,1)S(1)}, u32[]{:S(2)}, u32[]{:S(2)}) collective-permute-start(bf16[64,256]{1,0:T(8,128)(2,1)S(1)} %get-tuple-element.10), channel_id=1, source_target_pairs={{0,3},{1,0},{2,1},{3,2},{4,7},{5,4},{6,5},{7,6},{8,11},{9,8},{10,9... | collective-permute-start | bytes 98312 | tf_op jit(solution)/shard_map/ppermute | solution.py:198

commit v2 on v1

v2 whole, which is shorter than its diff:
```python
import functools

import jax
import jax.numpy as jnp
from jax import lax
from jax.experimental import pallas as pl
from jax.experimental.pallas import tpu as pltpu
from jax.sharding import PartitionSpec as P

MAXMO = 1000
LANES = 128
GROUP = 16


def up(value, unit):
    return -(-value // unit) * unit


def window_sum(values, window):
    width = values.shape[1]

    def ahead(array, by):
        return array if by == 0 else pltpu.roll(array, width - by, 1)

    total, offset, size, run = None, 0, 1, values
    while size <= window:
        if window & size:
            piece = ahead(run, offset)
            total = piece if total is None else total + piece
            offset += size
        size *= 2
        if size <= window:
            run = run + ahead(run, size // 2)
    return total


def correlate_kernel(
    core_ref, moveouts_ref, uptime_ref, records_ref, templates_ref,
    send_ref, keep_ref,
    masked, shifted, factor, columns, strips, windows_a, windows_b, bank_a, bank_b, total,
    *, stations, components, length, window, block_count,
):
    step = pl.program_id(0)
    channels = stations * components
    rows = masked.shape[0]
    tiles = length // LANES
    depth_tiles = up(window, LANES) // LANES
    depth = depth_tiles * LANES
    block_len = length // block_count
    span = shifted.shape[1]

    def prologue():
        masked[...] = jnp.zeros(masked.shape, jnp.float32)
        offsets = lax.broadcasted_iota(jnp.int32, (stations, block_len), 1)
        which = lax.broadcasted_iota(jnp.int32, (stations, block_len), 0)
        for b in range(block_count):
            limit = jnp.zeros((stations, block_len), jnp.int32)
            for s in range(stations):
                limit = jnp.where(which == s, uptime_ref[b, s], limit)
            part = slice(b * block_len, (b + 1) * block_len)
            for j in range(components):
                values = records_ref[j, :, part].astype(jnp.float32)
                masked[j * stations:(j + 1) * stations, part] = jnp.where(offsets < limit, values, 0.0)
        shifted[...] = jnp.zeros(shifted.shape, jnp.float32)

        def shift_one(s, carry):
            for j in range(components):
                c = j * stations + s
                moveout = moveouts_ref[j, s]
                base = pl.multiple_of(moveout // LANES * LANES, LANES)
                row = masked[pl.ds(c, 1), pl.ds(base, span)]
                shifted[pl.ds(c, 1), :] = pltpu.roll(row, span - (moveout - base), 1)
            return carry

        lax.fori_loop(0, stations, shift_one, 0)
        factor[...] = jnp.zeros(factor.shape, jnp.float32)
        for g in range(0, rows, 8):
            values = shifted[g:g + 8, :]
            energy = window_sum(values * values, window)[:, :length]
            factor[g:g + 8, :] = lax.rsqrt(jnp.maximum(energy, 1.0))
        source = lax.broadcasted_iota(jnp.int32, (LANES, LANES), 1)
        target = lax.broadcasted_iota(jnp.int32, (LANES, LANES), 0)
        mirrored = target // GROUP * GROUP + (GROUP - 1 - target % GROUP)
        swap = jnp.where(source == mirrored, 1.0, 0.0).astype(jnp.float32)
        for i in range(tiles):
            columns[i * LANES:(i + 1) * LANES, :] = lax.dot_general(
                swap, factor[:, i * LANES:(i + 1) * LANES],
                (((1,), (1,)), ((), ())),
                precision=lax.Precision.HIGHEST,
                preferred_element_type=jnp.float32,
            )
        bank_a[...] = jnp.zeros(bank_a.shape, bank_a.dtype)
        bank_b[...] = jnp.zeros(bank_b.shape, bank_b.dtype)
        total[...] = jnp.zeros(total.shape, total.dtype)

    def build(windows, bank):
        for j in range(components):
            values = templates_ref[0, j].astype(jnp.float32)
            squares = jnp.sum(values * values, axis=0, keepdims=True)
            unit = (values * lax.rsqrt(squares + 1e-06)).astype(jnp.bfloat16)
            bank[j * depth:j * depth + window, :] = unit
        for j in range(components):
            c = j * stations + step
            half = jnp.broadcast_to(shifted[pl.ds(c, 1), :], (8, span))
            strip = jnp.concatenate(
                [pltpu.roll(half, span - GROUP + 1 + b, 1, stride=1, stride_axis=0) for b in (0, 8)],
                axis=0,
            ).astype(jnp.bfloat16)
            lane = jnp.full((GROUP, LANES), c, jnp.int32)
            for a in range(LANES // GROUP):
                rolled = strip if a == 0 else pltpu.roll(strip, span - a * GROUP, 1)
                for i in range(tiles):
                    at = i * LANES + a * GROUP
                    scale = jnp.take_along_axis(columns[at:at + GROUP, :], lane, axis=1)
                    scale = scale.astype(jnp.bfloat16)
                    for d in range(depth_tiles):
                        piece = rolled[:, (i + d) * LANES:(i + d + 1) * LANES]
                        windows[at:at + GROUP, j * depth + d * LANES:j * depth + (d + 1) * LANES] = piece * scale

    def multiply(windows, bank):
        total[...] += jnp.dot(windows[...], bank[...], preferred_element_type=jnp.float32)

    @pl.when(step == 0)
    def first():
        prologue()
        build(windows_a, bank_a)

    @pl.when((step > 0) & (step < stations) & (step % 2 == 1))
    def odd():
        build(windows_b, bank_b)
        multiply(windows_a, bank_a)

    @pl.when((step > 0) & (step < stations) & (step % 2 == 0))
    def even():
        build(windows_a, bank_a)
        multiply(windows_b, bank_b)

    @pl.when(step == stations)
    def last():
        if stations % 2:
            multiply(windows_a, bank_a)
        else:
            multiply(windows_b, bank_b)
        core = core_ref[0]
        hops, region = keep_ref.shape[0], keep_ref.shape[1]
        turned = 7 - lax.broadcasted_iota(jnp.int32, (8, LANES), 0)
        for h in range(0, total.shape[1], LANES):
            for r in range(0, length, 8):
                source = r // GROUP * GROUP + (GROUP - 8 - r % GROUP)
                strips[r:r + 8, h:h + LANES] = jnp.take_along_axis(
                    total[source:source + 8, h:h + LANES], turned, axis=0)
        for x in range(hops):
            own = pl.multiple_of((2 * x + core) * region, region)
            other = pl.multiple_of((2 * x + 1 - core) * region, region)
            keep_ref[x] = strips[pl.ds(own, region), :]
            send_ref[x] = strips[pl.ds(other, region), :].astype(send_ref.dtype)


def correlate(core, records, templates, moveouts, uptime, hops):
    components, stations, length = records.shape
    window, bank_size = templates.shape[2:]
    block_count = uptime.shape[0]
    depth = up(window, LANES)
    rows = up(stations * components, 8)
    reach = length + depth + LANES + up(MAXMO, LANES)
    region = length // (2 * hops)
    body = functools.partial(
        correlate_kernel, stations=stations, components=components, length=length,
        window=window, block_count=block_count,
    )
    whole = lambda s, *_: (0, 0, 0)
    return pl.pallas_call(
        body,
        grid_spec=pltpu.PrefetchScalarGridSpec(
            num_scalar_prefetch=3,
            grid=(stations + 1,),
            in_specs=[
                pl.BlockSpec(records.shape, whole),
                pl.BlockSpec(
                    (1,) + templates.shape[1:],
                    lambda s, *_: (jnp.minimum(s, stations - 1), 0, 0, 0),
                ),
            ],
            out_specs=[
                pl.BlockSpec((hops, region, bank_size), whole),
                pl.BlockSpec((hops, region, bank_size), whole),
            ],
            scratch_shapes=[
                pltpu.VMEM((rows, reach), jnp.float32),
                pltpu.VMEM((rows, length + depth + LANES), jnp.float32),
                pltpu.VMEM((up(rows, LANES), length), jnp.float32),
                pltpu.VMEM((length, up(rows, LANES)), jnp.float32),
                pltpu.VMEM((length, bank_size), jnp.float32),
                pltpu.VMEM((length, components * depth), jnp.bfloat16),
                pltpu.VMEM((length, components * depth), jnp.bfloat16),
                pltpu.VMEM((components * depth, bank_size), jnp.bfloat16),
                pltpu.VMEM((components * depth, bank_size), jnp.bfloat16),
                pltpu.VMEM((length, bank_size), jnp.float32),
            ],
        ),
        out_shape=[
            jax.ShapeDtypeStruct((hops, region, bank_size), jnp.bfloat16),
            jax.ShapeDtypeStruct((hops, region, bank_size), jnp.float32),
        ],
        compiler_params=pltpu.CompilerParams(vmem_limit_bytes=60 * 2**20),
        name="correlate",
    )(core, moveouts, uptime, records, templates)


def body(records, templates, moveouts, uptime):
    tm, chan = lax.axis_size("tm"), lax.axis_size("chan")
    hops = tm // 2
    t, z = lax.axis_index("tm"), lax.axis_index("chan")
    x, core = t // 2, t % 2
    send, keep = correlate(
        core.reshape(1), records.transpose(1, 0, 2), templates, moveouts.T, uptime.T, hops
    )
    got = lax.ppermute(send, "tm", [(i, i ^ 1) for i in range(tm)])
    mine = keep + got.astype(jnp.float32)
    result = lax.dynamic_index_in_dim(mine, x, 0, keepdims=False)
    for step in range(1, hops):
        block = lax.dynamic_index_in_dim(mine, (x + step) % hops, 0, keepdims=False)
        perm = [(i, ((i // 2 + step) % hops) * 2 + i % 2) for i in range(tm)]
        result = result + lax.ppermute(block.astype(jnp.bfloat16), "tm", perm).astype(jnp.float32)
    mine = result.reshape(chan, result.shape[0] // chan, result.shape[1])
    result = lax.dynamic_index_in_dim(mine, z, 0, keepdims=False)
    for step in range(1, chan):
        block = lax.dynamic_index_in_dim(mine, (z + step) % chan, 0, keepdims=False)
        perm = [(i, (i + step) % chan) for i in range(chan)]
        result = result + lax.ppermute(block.astype(jnp.bfloat16), "chan", perm).astype(jnp.float32)
    return result.T


def solution(mesh):
    placed = (
        P(("grp", "tm", "chan"), None, None),
        P(("tm", "chan"), None, None, None),
        P(("tm", "chan"), None),
        P(("grp", "tm", "chan"), None),
    )
    return jax.shard_map(
        body, mesh=mesh, in_specs=placed, out_specs=P(None, ("grp", "tm", "chan")), check_vma=False
    )
```

time: 48.4 us -> 40.8 us (0.84)
  local copies, waits for them, and re-layouts: 5.77 us -> 0.04 us
  Pallas kernels: 25.5 us -> 21.6 us
  other arithmetic: 0.09 us -> 1.76 us
    unnamed x5 -> x0, local copies, waits for them, and re-layouts: 4.89 us -> none
    pallas_call x1, Pallas kernels: 25.5 us -> 21.6 us  [correlate(): pl.pallas_call(body, grid_spec=pltpu.PrefetchScalarGridSpec(num_scalar_pr...]
    add x1, other arithmetic: 0.05 us -> 1.09 us  [body(): mine = keep + got.astype(jnp.float32)]
    rev x1 -> x0, local copies, waits for them, and re-layouts: 0.67 us -> none  [body(): result = result.reshape(samples // GROUP, GROUP, bank_size)[:, ::-1, :]]
    transpose x0 -> x1, other arithmetic: none -> 0.65 us  [body(): return result.T]
where the time goes in v2:
time: 40.8 us; the launch traced here: 40.4 us
  Pallas kernels  21.6 us (53%)
  starting transfers between devices  9.2 us (23%)
  waiting for transfers between devices  7.74 us (19%)
  other arithmetic  1.76 us (4%)
    pallas_call x1, Pallas kernels, correlate(): pl.pallas_call(body, grid_spec=pltpu.PrefetchScalarGridSpec(num_scalar_pr...  21.6 us
    ppermute x3, starting transfers between devices, body(): lax.ppermute(block.astype(jnp.bfloat16), 'chan', perm).astype(jnp.float32)  5.82 us
    ppermute x1, waiting for transfers between devices, body(): lax.ppermute(block.astype(jnp.bfloat16), 'tm', perm).astype(jnp.float32)  3.8 us
    ppermute x1, starting transfers between devices, body(): lax.ppermute(block.astype(jnp.bfloat16), 'tm', perm).astype(jnp.float32)  2.92 us
    ppermute x3, waiting for transfers between devices, body(): lax.ppermute(block.astype(jnp.bfloat16), 'chan', perm).astype(jnp.float32)  2.57 us
    ppermute x1, waiting for transfers between devices, body(): got = lax.ppermute(send, 'tm', [(i, i ^ 1) for i in range(tm)])  1.37 us
    add x1, other arithmetic, body(): mine = keep + got.astype(jnp.float32)  1.09 us
  transfers between devices with their start and end apart: 5, of which 5 were waited for; matrix products, arithmetic and copies ran while one was open for 0% of the time, Pallas kernels for 0%

profile of v2, /device:TPU:0, one launch (start us, length us, event | category | flops | bytes accessed | tf_op | source)
XLA Modules:
  0.0 40.4 jit_solution(10188950179052422037)
XLA Ops:
  0.0 21.6 %correlate.1 = (bf16[2,256,256]{2,1,0:T(8,128)(2,1)}, f32[2,256,256]{2,1,0:T(8,128)}) custom-call(s32[1]{0:T(128)} %bitcast.core_ref, s32[3,16]{1,0:T(4,128)} %bitcast.28, s32[2,16]{1,0:T(2,128)} %bitcast.29, bf16[3,16,1024]{2,1,0:T(8,128)(2,1)} %bitcast.27, bf16[16,3,200,256]{3,2,1,0:T(8,128)(2,1)} %templates_ref.1), custom_call_target="tpu_custom_call" | custom-call | tf_op jit(solution)/shard_map/correlate/pallas_call | solution.py:172
  21.6 0.5 %collective-permute-start = (bf16[2,256,256]{2,1,0:T(8,128)(2,1)}, bf16[2,256,256]{2,1,0:T(8,128)(2,1)S(1)}, u32[]{:S(2)}, u32[]{:S(2)}) collective-permute-start(bf16[2,256,256]{2,1,0:T(8,128)(2,1)} %get-tuple-element.8), channel_id=1, source_target_pairs={{0,4},{4,0},{8,12},{12,8},{1,5},{5,1},{9,13},{13,9},{2,6},{6,2},{1... | collective-permute-start | bytes 786440 | tf_op jit(solution)/shard_map/ppermute | solution.py:218
  22.0 1.4 %collective-permute-done = bf16[2,256,256]{2,1,0:T(8,128)(2,1)S(1)} collective-permute-done((bf16[2,256,256]{2,1,0:T(8,128)(2,1)}, bf16[2,256,256]{2,1,0:T(8,128)(2,1)S(1)}, u32[]{:S(2)}, u32[]{:S(2)}) %collective-permute-start) | collective-permute-done | bytes 262176 | tf_op jit(solution)/shard_map/ppermute | solution.py:218
  23.4 1.1 %convert_add_fusion = f32[2,256,256]{2,1,0:T(8,128)S(1)} fusion(f32[2,256,256]{2,1,0:T(8,128)} %get-tuple-element.7, bf16[2,256,256]{2,1,0:T(8,128)(2,1)S(1)} %collective-permute-done), kind=kLoop, calls=%fused_computation | loop fusion | flops 262144 | bytes 1310720 | tf_op jit(solution)/shard_map/add | solution.py:219
  24.5 2.9 %collective-permute-start.1 = (bf16[256,256]{1,0:T(8,128)(2,1)S(1)}, bf16[256,256]{1,0:T(8,128)(2,1)S(1)}, u32[]{:S(2)}, u32[]{:S(2)}) collective-permute-start(bf16[256,256]{1,0:T(8,128)(2,1)S(1)} %fusion), channel_id=1, source_target_pairs={{0,8},{4,12},{8,0},{12,4},{1,9},{5,13},{9,1},{13,5},{2,10},{6,14},... | collective-permute-start | bytes 393224 | tf_op jit(solution)/shard_map/ppermute | solution.py:224
  27.5 3.8 %collective-permute-done.1 = bf16[256,256]{1,0:T(8,128)(2,1)S(1)} collective-permute-done((bf16[256,256]{1,0:T(8,128)(2,1)S(1)}, bf16[256,256]{1,0:T(8,128)(2,1)S(1)}, u32[]{:S(2)}, u32[]{:S(2)}) %collective-permute-start.1) | collective-permute-done | bytes 131104 | tf_op jit(solution)/shard_map/ppermute | solution.py:224
  31.3 1.9 %collective-permute-start.2 = (bf16[64,256]{1,0:T(8,128)(2,1)S(1)}, bf16[64,256]{1,0:T(8,128)(2,1)S(1)}, u32[]{:S(2)}, u32[]{:S(2)}) collective-permute-start(bf16[64,256]{1,0:T(8,128)(2,1)S(1)} %get-tuple-element.9), channel_id=1, source_target_pairs={{0,1},{1,2},{2,3},{3,0},{4,5},{5,6},{6,7},{7,4},{8,9},{9,10},{10,1... | collective-permute-start | bytes 98312 | tf_op jit(solution)/shard_map/ppermute | solution.py:230
  33.2 2.6 %collective-permute-start.3 = (bf16[64,256]{1,0:T(8,128)(2,1)S(1)}, bf16[64,256]{1,0:T(8,128)(2,1)S(1)}, u32[]{:S(2)}, u32[]{:S(2)}) collective-permute-start(bf16[64,256]{1,0:T(8,128)(2,1)S(1)} %get-tuple-element.11), channel_id=1, source_target_pairs={{0,2},{1,3},{2,0},{3,1},{4,6},{5,7},{6,4},{7,5},{8,10},{9,11},{10,... | collective-permute-start | bytes 98312 | tf_op jit(solution)/shard_map/ppermute | solution.py:230
  35.8 1.3 %collective-permute-start.4 = (bf16[64,256]{1,0:T(8,128)(2,1)S(1)}, bf16[64,256]{1,0:T(8,128)(2,1)S(1)}, u32[]{:S(2)}, u32[]{:S(2)}) collective-permute-start(bf16[64,256]{1,0:T(8,128)(2,1)S(1)} %get-tuple-element.10), channel_id=1, source_target_pairs={{0,3},{1,0},{2,1},{3,2},{4,7},{5,4},{6,5},{7,6},{8,11},{9,8},{10,9... | collective-permute-start | bytes 98312 | tf_op jit(solution)/shard_map/ppermute | solution.py:230
  37.1 0.4 %collective-permute-done.2 = bf16[64,256]{1,0:T(8,128)(2,1)S(1)} collective-permute-done((bf16[64,256]{1,0:T(8,128)(2,1)S(1)}, bf16[64,256]{1,0:T(8,128)(2,1)S(1)}, u32[]{:S(2)}, u32[]{:S(2)}) %collective-permute-start.2) | collective-permute-done | bytes 32800 | tf_op jit(solution)/shard_map/ppermute | solution.py:230
  37.6 0.6 %collective-permute-done.3 = bf16[64,256]{1,0:T(8,128)(2,1)S(1)} collective-permute-done((bf16[64,256]{1,0:T(8,128)(2,1)S(1)}, bf16[64,256]{1,0:T(8,128)(2,1)S(1)}, u32[]{:S(2)}, u32[]{:S(2)}) %collective-permute-start.3) | collective-permute-done | bytes 32800 | tf_op jit(solution)/shard_map/ppermute | solution.py:230
  38.1 1.6 %collective-permute-done.4 = bf16[64,256]{1,0:T(8,128)(2,1)S(1)} collective-permute-done((bf16[64,256]{1,0:T(8,128)(2,1)S(1)}, bf16[64,256]{1,0:T(8,128)(2,1)S(1)}, u32[]{:S(2)}, u32[]{:S(2)}) %collective-permute-start.4) | collective-permute-done | bytes 32800 | tf_op jit(solution)/shard_map/ppermute | solution.py:230
  39.7 0.6 %fusion.3 = f32[256,64]{0,1:T(8,128)} fusion(bf16[64,256]{1,0:T(8,128)(2,1)S(1)} %collective-permute-done.4, bf16[64,256]{1,0:T(8,128)(2,1)S(1)} %collective-permute-done.3, bf16[64,256]{1,0:T(8,128)(2,1)S(1)} %collective-permute-done.2, f32[4,64,256]{2,1,0:T(8,128)S(1)} %bitcast.26, s32[]{:T(128)S(6)} %select_n.52), kind=kLoop, calls=%fused_computation.7 | loop fusion | flops 98304 | bytes 229380 | tf_op jit(solution)/shard_map/transpose | solution.py:231
  (3 shorter events, 0.1 us)
Async XLA Ops:
  21.6 1.8 %collective-permute-start = (bf16[2,256,256]{2,1,0:T(8,128)(2,1)}, bf16[2,256,256]{2,1,0:T(8,128)(2,1)S(1)}, u32[]{:S(2)}, u32[]{:S(2)}) collective-permute-start(bf16[2,256,256]{2,1,0:T(8,128)(2,1)} %get-tuple-element.8), channel_id=1, source_target_pairs={{0,4},{4,0},{8,12},{12,8},{1,5},{5,1},{9,13},{13,9},{2,6},{6,2},{1... | collective-permute-start | bytes 786440 | tf_op jit(solution)/shard_map/ppermute | solution.py:218
  24.5 6.7 %collective-permute-start.1 = (bf16[256,256]{1,0:T(8,128)(2,1)S(1)}, bf16[256,256]{1,0:T(8,128)(2,1)S(1)}, u32[]{:S(2)}, u32[]{:S(2)}) collective-permute-start(bf16[256,256]{1,0:T(8,128)(2,1)S(1)} %fusion), channel_id=1, source_target_pairs={{0,8},{4,12},{8,0},{12,4},{1,9},{5,13},{9,1},{13,5},{2,10},{6,14},... | collective-permute-start | bytes 393224 | tf_op jit(solution)/shard_map/ppermute | solution.py:224
  31.3 6.3 %collective-permute-start.2 = (bf16[64,256]{1,0:T(8,128)(2,1)S(1)}, bf16[64,256]{1,0:T(8,128)(2,1)S(1)}, u32[]{:S(2)}, u32[]{:S(2)}) collective-permute-start(bf16[64,256]{1,0:T(8,128)(2,1)S(1)} %get-tuple-element.9), channel_id=1, source_target_pairs={{0,1},{1,2},{2,3},{3,0},{4,5},{5,6},{6,7},{7,4},{8,9},{9,10},{10,1... | collective-permute-start | bytes 98312 | tf_op jit(solution)/shard_map/ppermute | solution.py:230
  33.2 4.9 %collective-permute-start.3 = (bf16[64,256]{1,0:T(8,128)(2,1)S(1)}, bf16[64,256]{1,0:T(8,128)(2,1)S(1)}, u32[]{:S(2)}, u32[]{:S(2)}) collective-permute-start(bf16[64,256]{1,0:T(8,128)(2,1)S(1)} %get-tuple-element.11), channel_id=1, source_target_pairs={{0,2},{1,3},{2,0},{3,1},{4,6},{5,7},{6,4},{7,5},{8,10},{9,11},{10,... | collective-permute-start | bytes 98312 | tf_op jit(solution)/shard_map/ppermute | solution.py:230
  35.8 3.9 %collective-permute-start.4 = (bf16[64,256]{1,0:T(8,128)(2,1)S(1)}, bf16[64,256]{1,0:T(8,128)(2,1)S(1)}, u32[]{:S(2)}, u32[]{:S(2)}) collective-permute-start(bf16[64,256]{1,0:T(8,128)(2,1)S(1)} %get-tuple-element.10), channel_id=1, source_target_pairs={{0,3},{1,0},{2,1},{3,2},{4,7},{5,4},{6,5},{7,6},{8,11},{9,8},{10,9... | collective-permute-start | bytes 98312 | tf_op jit(solution)/shard_map/ppermute | solution.py:230

commit v3 on v2

v3 whole, which is shorter than its diff:
```python
import functools

import jax
import jax.numpy as jnp
from jax import lax
from jax.experimental import pallas as pl
from jax.experimental.pallas import tpu as pltpu
from jax.sharding import PartitionSpec as P

MAXMO = 1000
LANES = 128
GROUP = 16


def up(value, unit):
    return -(-value // unit) * unit


def window_sum(values, window):
    def behind(array, by):
        return array if by == 0 else pltpu.roll(array, by, 1)

    total, offset, size, run = None, 0, 1, values
    while size <= window:
        if window & size:
            piece = behind(run, offset)
            total = piece if total is None else total + piece
            offset += size
        size *= 2
        if size <= window:
            run = run + behind(run, size // 2)
    return total


def correlate_kernel(
    core_ref, moveouts_ref, uptime_ref, records_ref, templates_ref,
    send_ref, keep_ref,
    masked, shifted, factor, bank, windows_a, windows_b, bank_a, bank_b, total,
    *, stations, components, length, window, block_count, batch,
):
    step = pl.program_id(0)
    steps = stations // batch
    rows = masked.shape[0]
    tiles = length // LANES
    groups = up(window, GROUP) // GROUP
    margin = up(window, LANES)
    block_len = length // block_count
    span = shifted.shape[1]
    lead = masked.shape[1] - length

    def prologue():
        masked[...] = jnp.zeros(masked.shape, jnp.float32)
        offsets = lax.broadcasted_iota(jnp.int32, (stations, LANES), 1)
        which = lax.broadcasted_iota(jnp.int32, (stations, LANES), 0)
        for b in range(block_count):
            limit = jnp.zeros((stations, LANES), jnp.int32)
            for s in range(stations):
                limit = jnp.where(which == s, uptime_ref[b, s], limit)
            for i in range(block_len // LANES):
                at = b * block_len + i * LANES
                live = offsets + i * LANES < limit
                for j in range(components):
                    values = records_ref[j, :, at:at + LANES].astype(jnp.float32)
                    factor[j * stations:(j + 1) * stations, at:at + LANES] = jnp.where(live, values, 0.0)
        mirror = LANES - 1 - lax.broadcasted_iota(jnp.int32, (8, LANES), 1)
        for g in range(0, rows, 8):
            for at in range(0, length, LANES):
                to = lead + length - LANES - at
                masked[g:g + 8, to:to + LANES] = jnp.take_along_axis(
                    factor[g:g + 8, at:at + LANES], mirror, axis=1)
        shifted[...] = jnp.zeros(shifted.shape, jnp.float32)

        def shift_one(s, carry):
            for j in range(components):
                c = j * stations + s
                moveout = moveouts_ref[j, s]
                whole = moveout // LANES * LANES
                base = pl.multiple_of(lead - margin - LANES - whole, LANES)
                row = masked[pl.ds(c, 1), pl.ds(base, span + LANES)]
                row = pltpu.roll(row, moveout - whole, 1)
                shifted[pl.ds(c, 1), :] = row[:, LANES:]
            return carry

        lax.fori_loop(0, stations, shift_one, 0)
        for g in range(0, rows, 8):
            values = shifted[g:g + 8, :]
            energy = window_sum(values * values, window)[:, margin:]
            factor[g:g + 8, :] = lax.rsqrt(jnp.maximum(energy, 1.0))
        bank[...] = jnp.zeros(bank.shape, bank.dtype)
        total[...] = jnp.zeros(total.shape, total.dtype)

    def build(windows, turned):
        for u in range(batch):
            for j in range(components):
                values = templates_ref[u, j].astype(jnp.float32)
                squares = jnp.sum(values * values, axis=0, keepdims=True)
                unit = (values * lax.rsqrt(squares + 1e-06)).astype(jnp.bfloat16)
                at = (u * components + j) * groups * GROUP
                bank[at:at + window, :] = unit
        turned[...] = bank[...].T
        for u in range(batch):
            for j in range(components):
                c = j * stations + step * batch + u
                half = jnp.broadcast_to(shifted[pl.ds(c, 1), :], (8, span))
                strip = jnp.concatenate(
                    [pltpu.roll(half, b, 1, stride=1, stride_axis=0) for b in (0, 8)], axis=0
                ).astype(jnp.bfloat16)
                scale = jnp.broadcast_to(factor[pl.ds(c, 1), :], (GROUP, length))
                scale = scale.astype(jnp.bfloat16)
                for a in range(min(groups, LANES // GROUP)):
                    rolled = strip if a == 0 else pltpu.roll(strip, a * GROUP, 1)
                    for g in range(a, groups, LANES // GROUP):
                        begin = margin - (g - a) * GROUP
                        at = ((u * components + j) * groups + g) * GROUP
                        windows[at:at + GROUP, :] = rolled[:, begin:begin + length] * scale

    def multiply(windows, turned):
        total[...] += jnp.dot(turned[:, :windows.shape[0]], windows[...],
                              preferred_element_type=jnp.float32)

    @pl.when(step == 0)
    def first():
        prologue()
        build(windows_a, bank_a)

    @pl.when((step > 0) & (step < steps) & (step % 2 == 1))
    def odd():
        build(windows_b, bank_b)
        multiply(windows_a, bank_a)

    @pl.when((step > 0) & (step < steps) & (step % 2 == 0))
    def even():
        build(windows_a, bank_a)
        multiply(windows_b, bank_b)

    @pl.when(step == steps)
    def last():
        if steps % 2:
            multiply(windows_a, bank_a)
        else:
            multiply(windows_b, bank_b)
        core = core_ref[0]
        hops, region = keep_ref.shape[0], keep_ref.shape[1]
        flip = LANES - 1 - lax.broadcasted_iota(jnp.int32, (LANES, LANES), 1)

        def ordered(begin, h):
            at = pl.multiple_of(length - LANES - begin, LANES)
            block = total[h:h + LANES, pl.ds(at, LANES)]
            return jnp.take_along_axis(block, flip, axis=1).T

        for x in range(hops):
            for r in range(0, region, LANES):
                for h in range(0, total.shape[0], LANES):
                    own = (2 * x + core) * region + r
                    other = (2 * x + 1 - core) * region + r
                    keep_ref[x, r:r + LANES, h:h + LANES] = ordered(own, h)
                    send_ref[x, r:r + LANES, h:h + LANES] = ordered(other, h).astype(send_ref.dtype)


def correlate(core, records, templates, moveouts, uptime, hops):
    components, stations, length = records.shape
    window, bank_size = templates.shape[2:]
    block_count = uptime.shape[0]
    margin = up(window, LANES)
    rows = up(stations * components, 8)
    region = length // (2 * hops)
    batch = 2 if stations % 2 == 0 else 1
    depth = batch * components * up(window, GROUP)
    body = functools.partial(
        correlate_kernel, stations=stations, components=components, length=length,
        window=window, block_count=block_count, batch=batch,
    )
    whole = lambda s, *_: (0, 0, 0)
    return pl.pallas_call(
        body,
        grid_spec=pltpu.PrefetchScalarGridSpec(
            num_scalar_prefetch=3,
            grid=(stations // batch + 1,),
            in_specs=[
                pl.BlockSpec(records.shape, whole),
                pl.BlockSpec(
                    (batch,) + templates.shape[1:],
                    lambda s, *_: (jnp.minimum(s, stations // batch - 1), 0, 0, 0),
                ),
            ],
            out_specs=[
                pl.BlockSpec((hops, region, bank_size), whole),
                pl.BlockSpec((hops, region, bank_size), whole),
            ],
            scratch_shapes=[
                pltpu.VMEM((rows, length + margin + LANES + up(MAXMO, LANES)), jnp.float32),
                pltpu.VMEM((rows, length + margin), jnp.float32),
                pltpu.VMEM((rows, length), jnp.float32),
                pltpu.VMEM((up(depth, LANES), bank_size), jnp.bfloat16),
                pltpu.VMEM((depth, length), jnp.bfloat16),
                pltpu.VMEM((depth, length), jnp.bfloat16),
                pltpu.VMEM((bank_size, up(depth, LANES)), jnp.bfloat16),
                pltpu.VMEM((bank_size, up(depth, LANES)), jnp.bfloat16),
                pltpu.VMEM((bank_size, length), jnp.float32),
            ],
        ),
        out_shape=[
            jax.ShapeDtypeStruct((hops, region, bank_size), jnp.bfloat16),
            jax.ShapeDtypeStruct((hops, region, bank_size), jnp.float32),
        ],
        compiler_params=pltpu.CompilerParams(vmem_limit_bytes=60 * 2**20),
        name="correlate",
    )(core, moveouts, uptime, records, templates)


def body(records, templates, moveouts, uptime):
    tm, chan = lax.axis_size("tm"), lax.axis_size("chan")
    hops = tm // 2
    t, z = lax.axis_index("tm"), lax.axis_index("chan")
    x, core = t // 2, t % 2
    send, keep = correlate(
        core.reshape(1), records.transpose(1, 0, 2), templates, moveouts.T, uptime.T, hops
    )
    got = lax.ppermute(send, "tm", [(i, i ^ 1) for i in range(tm)])
    mine = keep + got.astype(jnp.float32)
    result = lax.dynamic_index_in_dim(mine, x, 0, keepdims=False)
    for step in range(1, hops):
        block = lax.dynamic_index_in_dim(mine, (x + step) % hops, 0, keepdims=False)
        perm = [(i, ((i // 2 + step) % hops) * 2 + i % 2) for i in range(tm)]
        result = result + lax.ppermute(block.astype(jnp.bfloat16), "tm", perm).astype(jnp.float32)
    mine = result.reshape(chan, result.shape[0] // chan, result.shape[1])
    result = lax.dynamic_index_in_dim(mine, z, 0, keepdims=False)
    for step in range(1, chan):
        block = lax.dynamic_index_in_dim(mine, (z + step) % chan, 0, keepdims=False)
        perm = [(i, (i + step) % chan) for i in range(chan)]
        result = result + lax.ppermute(block.astype(jnp.bfloat16), "chan", perm).astype(jnp.float32)
    return result.T


def solution(mesh):
    placed = (
        P(("grp", "tm", "chan"), None, None),
        P(("tm", "chan"), None, None, None),
        P(("tm", "chan"), None),
        P(("grp", "tm", "chan"), None),
    )
    return jax.shard_map(
        body, mesh=mesh, in_specs=placed, out_specs=P(None, ("grp", "tm", "chan")), check_vma=False
    )
```

time: 40.8 us -> 36.8 us (0.902)
  Pallas kernels: 21.6 us -> 17.8 us
    pallas_call x1, Pallas kernels: 21.6 us -> 17.8 us  [correlate(): pl.pallas_call(body, grid_spec=pltpu.PrefetchScalarGridSpec(num_scalar_pr...]
where the time goes in v3:
time: 36.8 us; the launch traced here: 36.6 us
  Pallas kernels  17.8 us (48%)
  starting transfers between devices  9.19 us (25%)
  waiting for transfers between devices  7.74 us (21%)
  other arithmetic  1.76 us (5%)
    pallas_call x1, Pallas kernels, correlate(): pl.pallas_call(body, grid_spec=pltpu.PrefetchScalarGridSpec(num_scalar_pr...  17.8 us
    ppermute x3, starting transfers between devices, body(): lax.ppermute(block.astype(jnp.bfloat16), 'chan', perm).astype(jnp.float32)  5.82 us
    ppermute x1, waiting for transfers between devices, body(): lax.ppermute(block.astype(jnp.bfloat16), 'tm', perm).astype(jnp.float32)  3.8 us
    ppermute x1, starting transfers between devices, body(): lax.ppermute(block.astype(jnp.bfloat16), 'tm', perm).astype(jnp.float32)  2.93 us
    ppermute x3, waiting for transfers between devices, body(): lax.ppermute(block.astype(jnp.bfloat16), 'chan', perm).astype(jnp.float32)  2.57 us
    ppermute x1, waiting for transfers between devices, body(): got = lax.ppermute(send, 'tm', [(i, i ^ 1) for i in range(tm)])  1.37 us
    add x1, other arithmetic, body(): mine = keep + got.astype(jnp.float32)  1.09 us
  transfers between devices with their start and end apart: 5, of which 5 were waited for; matrix products, arithmetic and copies ran while one was open for 0% of the time, Pallas kernels for 0%

profile of v3, /device:TPU:0, one launch (start us, length us, event | category | flops | bytes accessed | tf_op | source)
XLA Modules:
  0.0 36.6 jit_solution(15410488276513908606)
XLA Ops:
  0.0 17.8 %correlate.1 = (bf16[2,256,256]{2,1,0:T(8,128)(2,1)}, f32[2,256,256]{2,1,0:T(8,128)}) custom-call(s32[1]{0:T(128)} %bitcast.core_ref, s32[3,16]{1,0:T(4,128)} %bitcast.28, s32[2,16]{1,0:T(2,128)} %bitcast.29, bf16[3,16,1024]{2,1,0:T(8,128)(2,1)} %bitcast.27, bf16[16,3,200,256]{3,2,1,0:T(8,128)(2,1)} %templates_ref.1), custom_call_target="tpu_custom_call" | custom-call | tf_op jit(solution)/shard_map/correlate/pallas_call | solution.py:174
  17.8 0.4 %collective-permute-start = (bf16[2,256,256]{2,1,0:T(8,128)(2,1)}, bf16[2,256,256]{2,1,0:T(8,128)(2,1)S(1)}, u32[]{:S(2)}, u32[]{:S(2)}) collective-permute-start(bf16[2,256,256]{2,1,0:T(8,128)(2,1)} %get-tuple-element.8), channel_id=1, source_target_pairs={{0,4},{4,0},{8,12},{12,8},{1,5},{5,1},{9,13},{13,9},{2,6},{6,2},{1... | collective-permute-start | bytes 786440 | tf_op jit(solution)/shard_map/ppermute | solution.py:219
  18.3 1.4 %collective-permute-done = bf16[2,256,256]{2,1,0:T(8,128)(2,1)S(1)} collective-permute-done((bf16[2,256,256]{2,1,0:T(8,128)(2,1)}, bf16[2,256,256]{2,1,0:T(8,128)(2,1)S(1)}, u32[]{:S(2)}, u32[]{:S(2)}) %collective-permute-start) | collective-permute-done | bytes 262176 | tf_op jit(solution)/shard_map/ppermute | solution.py:219
  19.6 1.1 %convert_add_fusion = f32[2,256,256]{2,1,0:T(8,128)S(1)} fusion(f32[2,256,256]{2,1,0:T(8,128)} %get-tuple-element.7, bf16[2,256,256]{2,1,0:T(8,128)(2,1)S(1)} %collective-permute-done), kind=kLoop, calls=%fused_computation | loop fusion | flops 262144 | bytes 1310720 | tf_op jit(solution)/shard_map/add | solution.py:220
  20.8 2.9 %collective-permute-start.1 = (bf16[256,256]{1,0:T(8,128)(2,1)S(1)}, bf16[256,256]{1,0:T(8,128)(2,1)S(1)}, u32[]{:S(2)}, u32[]{:S(2)}) collective-permute-start(bf16[256,256]{1,0:T(8,128)(2,1)S(1)} %fusion), channel_id=1, source_target_pairs={{0,8},{4,12},{8,0},{12,4},{1,9},{5,13},{9,1},{13,5},{2,10},{6,14},... | collective-permute-start | bytes 393224 | tf_op jit(solution)/shard_map/ppermute | solution.py:225
  23.7 3.8 %collective-permute-done.1 = bf16[256,256]{1,0:T(8,128)(2,1)S(1)} collective-permute-done((bf16[256,256]{1,0:T(8,128)(2,1)S(1)}, bf16[256,256]{1,0:T(8,128)(2,1)S(1)}, u32[]{:S(2)}, u32[]{:S(2)}) %collective-permute-start.1) | collective-permute-done | bytes 131104 | tf_op jit(solution)/shard_map/ppermute | solution.py:225
  27.6 1.9 %collective-permute-start.2 = (bf16[64,256]{1,0:T(8,128)(2,1)S(1)}, bf16[64,256]{1,0:T(8,128)(2,1)S(1)}, u32[]{:S(2)}, u32[]{:S(2)}) collective-permute-start(bf16[64,256]{1,0:T(8,128)(2,1)S(1)} %get-tuple-element.9), channel_id=1, source_target_pairs={{0,1},{1,2},{2,3},{3,0},{4,5},{5,6},{6,7},{7,4},{8,9},{9,10},{10,1... | collective-permute-start | bytes 98312 | tf_op jit(solution)/shard_map/ppermute | solution.py:231
  29.4 2.6 %collective-permute-start.3 = (bf16[64,256]{1,0:T(8,128)(2,1)S(1)}, bf16[64,256]{1,0:T(8,128)(2,1)S(1)}, u32[]{:S(2)}, u32[]{:S(2)}) collective-permute-start(bf16[64,256]{1,0:T(8,128)(2,1)S(1)} %get-tuple-element.11), channel_id=1, source_target_pairs={{0,2},{1,3},{2,0},{3,1},{4,6},{5,7},{6,4},{7,5},{8,10},{9,11},{10,... | collective-permute-start | bytes 98312 | tf_op jit(solution)/shard_map/ppermute | solution.py:231
  32.0 1.3 %collective-permute-start.4 = (bf16[64,256]{1,0:T(8,128)(2,1)S(1)}, bf16[64,256]{1,0:T(8,128)(2,1)S(1)}, u32[]{:S(2)}, u32[]{:S(2)}) collective-permute-start(bf16[64,256]{1,0:T(8,128)(2,1)S(1)} %get-tuple-element.10), channel_id=1, source_target_pairs={{0,3},{1,0},{2,1},{3,2},{4,7},{5,4},{6,5},{7,6},{8,11},{9,8},{10,9... | collective-permute-start | bytes 98312 | tf_op jit(solution)/shard_map/ppermute | solution.py:231
  33.4 0.4 %collective-permute-done.2 = bf16[64,256]{1,0:T(8,128)(2,1)S(1)} collective-permute-done((bf16[64,256]{1,0:T(8,128)(2,1)S(1)}, bf16[64,256]{1,0:T(8,128)(2,1)S(1)}, u32[]{:S(2)}, u32[]{:S(2)}) %collective-permute-start.2) | collective-permute-done | bytes 32800 | tf_op jit(solution)/shard_map/ppermute | solution.py:231
  33.8 0.6 %collective-permute-done.3 = bf16[64,256]{1,0:T(8,128)(2,1)S(1)} collective-permute-done((bf16[64,256]{1,0:T(8,128)(2,1)S(1)}, bf16[64,256]{1,0:T(8,128)(2,1)S(1)}, u32[]{:S(2)}, u32[]{:S(2)}) %collective-permute-start.3) | collective-permute-done | bytes 32800 | tf_op jit(solution)/shard_map/ppermute | solution.py:231
  34.4 1.6 %collective-permute-done.4 = bf16[64,256]{1,0:T(8,128)(2,1)S(1)} collective-permute-done((bf16[64,256]{1,0:T(8,128)(2,1)S(1)}, bf16[64,256]{1,0:T(8,128)(2,1)S(1)}, u32[]{:S(2)}, u32[]{:S(2)}) %collective-permute-start.4) | collective-permute-done | bytes 32800 | tf_op jit(solution)/shard_map/ppermute | solution.py:231
  36.0 0.6 %fusion.3 = f32[256,64]{0,1:T(8,128)} fusion(bf16[64,256]{1,0:T(8,128)(2,1)S(1)} %collective-permute-done.4, bf16[64,256]{1,0:T(8,128)(2,1)S(1)} %collective-permute-done.3, bf16[64,256]{1,0:T(8,128)(2,1)S(1)} %collective-permute-done.2, f32[4,64,256]{2,1,0:T(8,128)S(1)} %bitcast.26, s32[]{:T(128)S(6)} %select_n.52), kind=kLoop, calls=%fused_computation.7 | loop fusion | flops 98304 | bytes 229380 | tf_op jit(solution)/shard_map/transpose | solution.py:232
  (3 shorter events, 0.1 us)
Async XLA Ops:
  17.8 1.8 %collective-permute-start = (bf16[2,256,256]{2,1,0:T(8,128)(2,1)}, bf16[2,256,256]{2,1,0:T(8,128)(2,1)S(1)}, u32[]{:S(2)}, u32[]{:S(2)}) collective-permute-start(bf16[2,256,256]{2,1,0:T(8,128)(2,1)} %get-tuple-element.8), channel_id=1, source_target_pairs={{0,4},{4,0},{8,12},{12,8},{1,5},{5,1},{9,13},{13,9},{2,6},{6,2},{1... | collective-permute-start | bytes 786440 | tf_op jit(solution)/shard_map/ppermute | solution.py:219
  20.8 6.7 %collective-permute-start.1 = (bf16[256,256]{1,0:T(8,128)(2,1)S(1)}, bf16[256,256]{1,0:T(8,128)(2,1)S(1)}, u32[]{:S(2)}, u32[]{:S(2)}) collective-permute-start(bf16[256,256]{1,0:T(8,128)(2,1)S(1)} %fusion), channel_id=1, source_target_pairs={{0,8},{4,12},{8,0},{12,4},{1,9},{5,13},{9,1},{13,5},{2,10},{6,14},... | collective-permute-start | bytes 393224 | tf_op jit(solution)/shard_map/ppermute | solution.py:225
  27.6 6.3 %collective-permute-start.2 = (bf16[64,256]{1,0:T(8,128)(2,1)S(1)}, bf16[64,256]{1,0:T(8,128)(2,1)S(1)}, u32[]{:S(2)}, u32[]{:S(2)}) collective-permute-start(bf16[64,256]{1,0:T(8,128)(2,1)S(1)} %get-tuple-element.9), channel_id=1, source_target_pairs={{0,1},{1,2},{2,3},{3,0},{4,5},{5,6},{6,7},{7,4},{8,9},{9,10},{10,1... | collective-permute-start | bytes 98312 | tf_op jit(solution)/shard_map/ppermute | solution.py:231
  29.4 4.9 %collective-permute-start.3 = (bf16[64,256]{1,0:T(8,128)(2,1)S(1)}, bf16[64,256]{1,0:T(8,128)(2,1)S(1)}, u32[]{:S(2)}, u32[]{:S(2)}) collective-permute-start(bf16[64,256]{1,0:T(8,128)(2,1)S(1)} %get-tuple-element.11), channel_id=1, source_target_pairs={{0,2},{1,3},{2,0},{3,1},{4,6},{5,7},{6,4},{7,5},{8,10},{9,11},{10,... | collective-permute-start | bytes 98312 | tf_op jit(solution)/shard_map/ppermute | solution.py:231
  32.0 3.9 %collective-permute-start.4 = (bf16[64,256]{1,0:T(8,128)(2,1)S(1)}, bf16[64,256]{1,0:T(8,128)(2,1)S(1)}, u32[]{:S(2)}, u32[]{:S(2)}) collective-permute-start(bf16[64,256]{1,0:T(8,128)(2,1)S(1)} %get-tuple-element.10), channel_id=1, source_target_pairs={{0,3},{1,0},{2,1},{3,2},{4,7},{5,4},{6,5},{7,6},{8,11},{9,8},{10,9... | collective-permute-start | bytes 98312 | tf_op jit(solution)/shard_map/ppermute | solution.py:231

commit v4 on v3

v4 whole, which is shorter than its diff:
```python
import functools

import jax
import jax.numpy as jnp
from jax import lax
from jax.experimental import pallas as pl
from jax.experimental.pallas import tpu as pltpu
from jax.sharding import PartitionSpec as P

MAXMO = 1000
LANES = 128
GROUP = 16


def up(value, unit):
    return -(-value // unit) * unit


def window_sum(values, window):
    def behind(array, by):
        return array if by == 0 else pltpu.roll(array, by, 1)

    total, offset, size, run = None, 0, 1, values
    while size <= window:
        if window & size:
            piece = behind(run, offset)
            total = piece if total is None else total + piece
            offset += size
        size *= 2
        if size <= window:
            run = run + behind(run, size // 2)
    return total


def correlate_kernel(
    core_ref, moveouts_ref, uptime_ref, records_ref, templates_ref,
    send_ref, keep_ref,
    masked, shifted, factor, loaded, bank, windows_a, windows_b, bank_a, bank_b, total, arrived,
    *, window, batch,
):
    components, stations, length = records_ref.shape
    block_count = uptime_ref.shape[0]
    batches = stations // batch
    rows = masked.shape[0]
    groups = up(window, GROUP) // GROUP
    margin = up(window, LANES)
    block_len = length // block_count
    span = shifted.shape[1]
    lead = masked.shape[1] - length

    def fetch(i):
        at = pl.ds(i * batch, batch)
        return pltpu.make_async_copy(templates_ref.at[at], loaded.at[at], arrived.at[i])

    for i in range(batches):
        fetch(i).start()

    masked[...] = jnp.zeros(masked.shape, jnp.float32)
    offsets = lax.broadcasted_iota(jnp.int32, (stations, LANES), 1)
    which = lax.broadcasted_iota(jnp.int32, (stations, LANES), 0)
    for b in range(block_count):
        limit = jnp.zeros((stations, LANES), jnp.int32)
        for s in range(stations):
            limit = jnp.where(which == s, uptime_ref[b, s], limit)
        for i in range(block_len // LANES):
            at = b * block_len + i * LANES
            live = offsets + i * LANES < limit
            for j in range(components):
                values = records_ref[j, :, at:at + LANES].astype(jnp.float32)
                factor[j * stations:(j + 1) * stations, at:at + LANES] = jnp.where(live, values, 0.0)
    mirror = LANES - 1 - lax.broadcasted_iota(jnp.int32, (8, LANES), 1)
    for g in range(0, rows, 8):
        for at in range(0, length, LANES):
            to = lead + length - LANES - at
            masked[g:g + 8, to:to + LANES] = jnp.take_along_axis(
                factor[g:g + 8, at:at + LANES], mirror, axis=1)
    shifted[...] = jnp.zeros(shifted.shape, jnp.float32)
    for j in range(components):
        for s in range(stations):
            c = j * stations + s
            moveout = moveouts_ref[j, s]
            whole = moveout // LANES * LANES
            base = pl.multiple_of(lead - margin - LANES - whole, LANES)
            row = masked[c:c + 1, pl.ds(base, span + LANES)]
            row = pltpu.roll(row, moveout - whole, 1)
            shifted[c:c + 1, :] = row[:, LANES:]
    for g in range(0, rows, 8):
        values = shifted[g:g + 8, :]
        energy = window_sum(values * values, window)[:, margin:]
        factor[g:g + 8, :] = lax.rsqrt(jnp.maximum(energy, 1.0))
    bank[...] = jnp.zeros(bank.shape, bank.dtype)
    total[...] = jnp.zeros(total.shape, total.dtype)
    depth = batch * components * groups * GROUP
    for windows in (windows_a, windows_b):
        if windows.shape[0] > depth:
            windows[depth:, :] = jnp.zeros((windows.shape[0] - depth, length), windows.dtype)

    def build(i, windows, turned):
        fetch(i).wait()
        for u in range(batch):
            for j in range(components):
                values = loaded[i * batch + u, j].astype(jnp.float32)
                squares = jnp.sum(values * values, axis=0, keepdims=True)
                unit = (values * lax.rsqrt(squares + 1e-06)).astype(jnp.bfloat16)
                at = (u * components + j) * groups * GROUP
                bank[at:at + window, :] = unit
        turned[...] = bank[...].T
        for u in range(batch):
            for j in range(components):
                c = j * stations + i * batch + u
                half = jnp.broadcast_to(shifted[pl.ds(c, 1), :], (8, span))
                strip = jnp.concatenate(
                    [pltpu.roll(half, b, 1, stride=1, stride_axis=0) for b in (0, 8)], axis=0
                ).astype(jnp.bfloat16)
                scale = jnp.broadcast_to(factor[pl.ds(c, 1), :], (GROUP, length))
                scale = scale.astype(jnp.bfloat16)
                for a in range(min(groups, LANES // GROUP)):
                    rolled = strip if a == 0 else pltpu.roll(strip, a * GROUP, 1)
                    for g in range(a, groups, LANES // GROUP):
                        begin = margin - (g - a) * GROUP
                        at = ((u * components + j) * groups + g) * GROUP
                        windows[at:at + GROUP, :] = rolled[:, begin:begin + length] * scale

    def multiply(windows, turned):
        width = min(2 * LANES, length)
        for n in range(0, length, width):
            total[:, n:n + width] += jnp.dot(
                turned[...], windows[:, n:n + width], preferred_element_type=jnp.float32)

    build(0, windows_a, bank_a)

    def two_batches(i, carry):
        build(2 * i + 1, windows_b, bank_b)
        multiply(windows_a, bank_a)
        build(2 * i + 2, windows_a, bank_a)
        multiply(windows_b, bank_b)
        return carry

    if batches > 2:
        lax.fori_loop(0, (batches - 1) // 2, two_batches, 0)
    if batches % 2 == 0:
        build(batches - 1, windows_b, bank_b)
        multiply(windows_a, bank_a)
        multiply(windows_b, bank_b)
    else:
        multiply(windows_a, bank_a)

    core = core_ref[0]
    hops, region = keep_ref.shape[0], keep_ref.shape[1]
    flip = LANES - 1 - lax.broadcasted_iota(jnp.int32, (LANES, LANES), 1)

    def ordered(begin, h):
        at = pl.multiple_of(length - LANES - begin, LANES)
        block = total[h:h + LANES, pl.ds(at, LANES)]
        return jnp.take_along_axis(block, flip, axis=1).T

    for x in range(hops):
        for r in range(0, region, LANES):
            for h in range(0, total.shape[0], LANES):
                own = (2 * x + core) * region + r
                other = (2 * x + 1 - core) * region + r
                keep_ref[x, r:r + LANES, h:h + LANES] = ordered(own, h)
                send_ref[x, r:r + LANES, h:h + LANES] = ordered(other, h).astype(send_ref.dtype)


def correlate(core, records, templates, moveouts, uptime, hops):
    components, stations, length = records.shape
    window, bank_size = templates.shape[2:]
    margin = up(window, LANES)
    rows = up(stations * components, 8)
    region = length // (2 * hops)
    batch = 2 if stations % 2 == 0 else 1
    depth = up(batch * components * up(window, GROUP), LANES)
    scalars = pl.BlockSpec(memory_space=pltpu.SMEM)
    vectors = pl.BlockSpec(memory_space=pltpu.VMEM)
    return pl.pallas_call(
        functools.partial(correlate_kernel, window=window, batch=batch),
        in_specs=[scalars, scalars, scalars, vectors, pl.BlockSpec(memory_space=pl.ANY)],
        out_specs=[vectors, vectors],
        scratch_shapes=[
            pltpu.VMEM((rows, length + margin + LANES + up(MAXMO, LANES)), jnp.float32),
            pltpu.VMEM((rows, length + margin), jnp.float32),
            pltpu.VMEM((rows, length), jnp.float32),
            pltpu.VMEM(templates.shape, templates.dtype),
            pltpu.VMEM((depth, bank_size), jnp.bfloat16),
            pltpu.VMEM((depth, length), jnp.bfloat16),
            pltpu.VMEM((depth, length), jnp.bfloat16),
            pltpu.VMEM((bank_size, depth), jnp.bfloat16),
            pltpu.VMEM((bank_size, depth), jnp.bfloat16),
            pltpu.VMEM((bank_size, length), jnp.float32),
            pltpu.SemaphoreType.DMA((stations // batch,)),
        ],
        out_shape=[
            jax.ShapeDtypeStruct((hops, region, bank_size), jnp.bfloat16),
            jax.ShapeDtypeStruct((hops, region, bank_size), jnp.float32),
        ],
        compiler_params=pltpu.CompilerParams(vmem_limit_bytes=60 * 2**20),
        name="correlate",
    )(core, moveouts, uptime, records, templates)


def body(records, templates, moveouts, uptime):
    tm, chan = lax.axis_size("tm"), lax.axis_size("chan")
    hops = tm // 2
    t, z = lax.axis_index("tm"), lax.axis_index("chan")
    x, core = t // 2, t % 2
    send, keep = correlate(
        core.reshape(1), records.transpose(1, 0, 2), templates, moveouts.T, uptime.T, hops
    )
    got = lax.ppermute(send, "tm", [(i, i ^ 1) for i in range(tm)])
    mine = keep + got.astype(jnp.float32)
    result = lax.dynamic_index_in_dim(mine, x, 0, keepdims=False)
    for step in range(1, hops):
        block = lax.dynamic_index_in_dim(mine, (x + step) % hops, 0, keepdims=False)
        perm = [(i, ((i // 2 + step) % hops) * 2 + i % 2) for i in range(tm)]
        result = result + lax.ppermute(block.astype(jnp.bfloat16), "tm", perm).astype(jnp.float32)
    mine = result.reshape(chan, result.shape[0] // chan, result.shape[1])
    result = lax.dynamic_index_in_dim(mine, z, 0, keepdims=False)
    for step in range(1, chan):
        block = lax.dynamic_index_in_dim(mine, (z + step) % chan, 0, keepdims=False)
        perm = [(i, (i + step) % chan) for i in range(chan)]
        result = result + lax.ppermute(block.astype(jnp.bfloat16), "chan", perm).astype(jnp.float32)
    return result.T


def solution(mesh):
    placed = (
        P(("grp", "tm", "chan"), None, None),
        P(("tm", "chan"), None, None, None),
        P(("tm", "chan"), None),
        P(("grp", "tm", "chan"), None),
    )
    return jax.shard_map(
        body, mesh=mesh, in_specs=placed, out_specs=P(None, ("grp", "tm", "chan")), check_vma=False
    )
```

time: 36.8 us -> 34.8 us (0.946)
  Pallas kernels: 17.8 us -> 15.8 us
    pallas_call x1, Pallas kernels: 17.8 us -> 15.8 us  [correlate(): pl.pallas_call(functools.partial(correlate_kernel, window=window, batch=b...]
where the time goes in v4:
time: 34.8 us; the launch traced here: 34.6 us
  Pallas kernels  15.8 us (45%)
  starting transfers between devices  9.25 us (27%)
  waiting for transfers between devices  7.75 us (22%)
  other arithmetic  1.76 us (5%)
    pallas_call x1, Pallas kernels, correlate(): pl.pallas_call(functools.partial(correlate_kernel, window=window, batch=b...  15.8 us
    ppermute x3, starting transfers between devices, body(): lax.ppermute(block.astype(jnp.bfloat16), 'chan', perm).astype(jnp.float32)  5.82 us
    ppermute x1, waiting for transfers between devices, body(): lax.ppermute(block.astype(jnp.bfloat16), 'tm', perm).astype(jnp.float32)  3.8 us
    ppermute x1, starting transfers between devices, body(): lax.ppermute(block.astype(jnp.bfloat16), 'tm', perm).astype(jnp.float32)  2.91 us
    ppermute x3, waiting for transfers between devices, body(): lax.ppermute(block.astype(jnp.bfloat16), 'chan', perm).astype(jnp.float32)  2.57 us
    ppermute x1, waiting for transfers between devices, body(): got = lax.ppermute(send, 'tm', [(i, i ^ 1) for i in range(tm)])  1.37 us
    add x1, other arithmetic, body(): mine = keep + got.astype(jnp.float32)  1.09 us
  transfers between devices with their start and end apart: 5, of which 5 were waited for; matrix products, arithmetic and copies ran while one was open for 0% of the time, Pallas kernels for 0%

profile of v4, /device:TPU:0, one launch (start us, length us, event | category | flops | bytes accessed | tf_op | source)
XLA Modules:
  0.0 34.6 jit_solution(17149126427449530995)
XLA Ops:
  0.0 15.8 %correlate.1 = (bf16[2,256,256]{2,1,0:T(8,128)(2,1)}, f32[2,256,256]{2,1,0:T(8,128)}) custom-call(s32[1]{0:T(128)} %bitcast.core_ref, s32[3,16]{1,0:T(4,128)} %bitcast.28, s32[2,16]{1,0:T(2,128)} %bitcast.29, bf16[3,16,1024]{2,1,0:T(8,128)(2,1)} %bitcast.27, bf16[16,3,200,256]{3,2,1,0:T(8,128)(2,1)} %templates_ref.1), custom_call_target="tpu_custom_call" | custom-call | tf_op jit(solution)/shard_map/correlate/pallas_call | solution.py:176
  15.8 0.5 %collective-permute-start = (bf16[2,256,256]{2,1,0:T(8,128)(2,1)}, bf16[2,256,256]{2,1,0:T(8,128)(2,1)S(1)}, u32[]{:S(2)}, u32[]{:S(2)}) collective-permute-start(bf16[2,256,256]{2,1,0:T(8,128)(2,1)} %get-tuple-element.8), channel_id=1, source_target_pairs={{0,4},{4,0},{8,12},{12,8},{1,5},{5,1},{9,13},{13,9},{2,6},{6,2},{1... | collective-permute-start | bytes 786440 | tf_op jit(solution)/shard_map/ppermute | solution.py:210
  16.3 1.4 %collective-permute-done = bf16[2,256,256]{2,1,0:T(8,128)(2,1)S(1)} collective-permute-done((bf16[2,256,256]{2,1,0:T(8,128)(2,1)}, bf16[2,256,256]{2,1,0:T(8,128)(2,1)S(1)}, u32[]{:S(2)}, u32[]{:S(2)}) %collective-permute-start) | collective-permute-done | bytes 262176 | tf_op jit(solution)/shard_map/ppermute | solution.py:210
  17.7 1.1 %convert_add_fusion = f32[2,256,256]{2,1,0:T(8,128)S(1)} fusion(f32[2,256,256]{2,1,0:T(8,128)} %get-tuple-element.7, bf16[2,256,256]{2,1,0:T(8,128)(2,1)S(1)} %collective-permute-done), kind=kLoop, calls=%fused_computation | loop fusion | flops 262144 | bytes 1310720 | tf_op jit(solution)/shard_map/add | solution.py:211
  18.8 2.9 %collective-permute-start.1 = (bf16[256,256]{1,0:T(8,128)(2,1)S(1)}, bf16[256,256]{1,0:T(8,128)(2,1)S(1)}, u32[]{:S(2)}, u32[]{:S(2)}) collective-permute-start(bf16[256,256]{1,0:T(8,128)(2,1)S(1)} %fusion), channel_id=1, source_target_pairs={{0,8},{4,12},{8,0},{12,4},{1,9},{5,13},{9,1},{13,5},{2,10},{6,14},... | collective-permute-start | bytes 393224 | tf_op jit(solution)/shard_map/ppermute | solution.py:216
  21.7 3.8 %collective-permute-done.1 = bf16[256,256]{1,0:T(8,128)(2,1)S(1)} collective-permute-done((bf16[256,256]{1,0:T(8,128)(2,1)S(1)}, bf16[256,256]{1,0:T(8,128)(2,1)S(1)}, u32[]{:S(2)}, u32[]{:S(2)}) %collective-permute-start.1) | collective-permute-done | bytes 131104 | tf_op jit(solution)/shard_map/ppermute | solution.py:216
  25.6 1.9 %collective-permute-start.2 = (bf16[64,256]{1,0:T(8,128)(2,1)S(1)}, bf16[64,256]{1,0:T(8,128)(2,1)S(1)}, u32[]{:S(2)}, u32[]{:S(2)}) collective-permute-start(bf16[64,256]{1,0:T(8,128)(2,1)S(1)} %get-tuple-element.9), channel_id=1, source_target_pairs={{0,1},{1,2},{2,3},{3,0},{4,5},{5,6},{6,7},{7,4},{8,9},{9,10},{10,1... | collective-permute-start | bytes 98312 | tf_op jit(solution)/shard_map/ppermute | solution.py:222
  27.5 2.6 %collective-permute-start.3 = (bf16[64,256]{1,0:T(8,128)(2,1)S(1)}, bf16[64,256]{1,0:T(8,128)(2,1)S(1)}, u32[]{:S(2)}, u32[]{:S(2)}) collective-permute-start(bf16[64,256]{1,0:T(8,128)(2,1)S(1)} %get-tuple-element.11), channel_id=1, source_target_pairs={{0,2},{1,3},{2,0},{3,1},{4,6},{5,7},{6,4},{7,5},{8,10},{9,11},{10,... | collective-permute-start | bytes 98312 | tf_op jit(solution)/shard_map/ppermute | solution.py:222
  30.1 1.3 %collective-permute-start.4 = (bf16[64,256]{1,0:T(8,128)(2,1)S(1)}, bf16[64,256]{1,0:T(8,128)(2,1)S(1)}, u32[]{:S(2)}, u32[]{:S(2)}) collective-permute-start(bf16[64,256]{1,0:T(8,128)(2,1)S(1)} %get-tuple-element.10), channel_id=1, source_target_pairs={{0,3},{1,0},{2,1},{3,2},{4,7},{5,4},{6,5},{7,6},{8,11},{9,8},{10,9... | collective-permute-start | bytes 98312 | tf_op jit(solution)/shard_map/ppermute | solution.py:222
  31.4 0.4 %collective-permute-done.2 = bf16[64,256]{1,0:T(8,128)(2,1)S(1)} collective-permute-done((bf16[64,256]{1,0:T(8,128)(2,1)S(1)}, bf16[64,256]{1,0:T(8,128)(2,1)S(1)}, u32[]{:S(2)}, u32[]{:S(2)}) %collective-permute-start.2) | collective-permute-done | bytes 32800 | tf_op jit(solution)/shard_map/ppermute | solution.py:222
  31.9 0.6 %collective-permute-done.3 = bf16[64,256]{1,0:T(8,128)(2,1)S(1)} collective-permute-done((bf16[64,256]{1,0:T(8,128)(2,1)S(1)}, bf16[64,256]{1,0:T(8,128)(2,1)S(1)}, u32[]{:S(2)}, u32[]{:S(2)}) %collective-permute-start.3) | collective-permute-done | bytes 32800 | tf_op jit(solution)/shard_map/ppermute | solution.py:222
  32.4 1.6 %collective-permute-done.4 = bf16[64,256]{1,0:T(8,128)(2,1)S(1)} collective-permute-done((bf16[64,256]{1,0:T(8,128)(2,1)S(1)}, bf16[64,256]{1,0:T(8,128)(2,1)S(1)}, u32[]{:S(2)}, u32[]{:S(2)}) %collective-permute-start.4) | collective-permute-done | bytes 32800 | tf_op jit(solution)/shard_map/ppermute | solution.py:222
  34.0 0.6 %fusion.3 = f32[256,64]{0,1:T(8,128)} fusion(bf16[64,256]{1,0:T(8,128)(2,1)S(1)} %collective-permute-done.4, bf16[64,256]{1,0:T(8,128)(2,1)S(1)} %collective-permute-done.3, bf16[64,256]{1,0:T(8,128)(2,1)S(1)} %collective-permute-done.2, f32[4,64,256]{2,1,0:T(8,128)S(1)} %bitcast.26, s32[]{:T(128)S(6)} %select_n.52), kind=kLoop, calls=%fused_computation.7 | loop fusion | flops 98304 | bytes 229380 | tf_op jit(solution)/shard_map/transpose | solution.py:223
  (3 shorter events, 0.1 us)
Async XLA Ops:
  15.8 1.9 %collective-permute-start = (bf16[2,256,256]{2,1,0:T(8,128)(2,1)}, bf16[2,256,256]{2,1,0:T(8,128)(2,1)S(1)}, u32[]{:S(2)}, u32[]{:S(2)}) collective-permute-start(bf16[2,256,256]{2,1,0:T(8,128)(2,1)} %get-tuple-element.8), channel_id=1, source_target_pairs={{0,4},{4,0},{8,12},{12,8},{1,5},{5,1},{9,13},{13,9},{2,6},{6,2},{1... | collective-permute-start | bytes 786440 | tf_op jit(solution)/shard_map/ppermute | solution.py:210
  18.8 6.7 %collective-permute-start.1 = (bf16[256,256]{1,0:T(8,128)(2,1)S(1)}, bf16[256,256]{1,0:T(8,128)(2,1)S(1)}, u32[]{:S(2)}, u32[]{:S(2)}) collective-permute-start(bf16[256,256]{1,0:T(8,128)(2,1)S(1)} %fusion), channel_id=1, source_target_pairs={{0,8},{4,12},{8,0},{12,4},{1,9},{5,13},{9,1},{13,5},{2,10},{6,14},... | collective-permute-start | bytes 393224 | tf_op jit(solution)/shard_map/ppermute | solution.py:216
  25.6 6.3 %collective-permute-start.2 = (bf16[64,256]{1,0:T(8,128)(2,1)S(1)}, bf16[64,256]{1,0:T(8,128)(2,1)S(1)}, u32[]{:S(2)}, u32[]{:S(2)}) collective-permute-start(bf16[64,256]{1,0:T(8,128)(2,1)S(1)} %get-tuple-element.9), channel_id=1, source_target_pairs={{0,1},{1,2},{2,3},{3,0},{4,5},{5,6},{6,7},{7,4},{8,9},{9,10},{10,1... | collective-permute-start | bytes 98312 | tf_op jit(solution)/shard_map/ppermute | solution.py:222
  27.5 4.9 %collective-permute-start.3 = (bf16[64,256]{1,0:T(8,128)(2,1)S(1)}, bf16[64,256]{1,0:T(8,128)(2,1)S(1)}, u32[]{:S(2)}, u32[]{:S(2)}) collective-permute-start(bf16[64,256]{1,0:T(8,128)(2,1)S(1)} %get-tuple-element.11), channel_id=1, source_target_pairs={{0,2},{1,3},{2,0},{3,1},{4,6},{5,7},{6,4},{7,5},{8,10},{9,11},{10,... | collective-permute-start | bytes 98312 | tf_op jit(solution)/shard_map/ppermute | solution.py:222
  30.1 3.9 %collective-permute-start.4 = (bf16[64,256]{1,0:T(8,128)(2,1)S(1)}, bf16[64,256]{1,0:T(8,128)(2,1)S(1)}, u32[]{:S(2)}, u32[]{:S(2)}) collective-permute-start(bf16[64,256]{1,0:T(8,128)(2,1)S(1)} %get-tuple-element.10), channel_id=1, source_target_pairs={{0,3},{1,0},{2,1},{3,2},{4,7},{5,4},{6,5},{7,6},{8,11},{9,8},{10,9... | collective-permute-start | bytes 98312 | tf_op jit(solution)/shard_map/ppermute | solution.py:222

commit v5 on v4

--- a/solution.py
+++ b/solution.py
@@ -95,8 +95,16 @@
         if windows.shape[0] > depth:
             windows[depth:, :] = jnp.zeros((windows.shape[0] - depth, length), windows.dtype)
 
-    def build(i, windows, turned):
+    width = min(2 * LANES, length)
+
+    def multiply(n, windows, turned):
+        total[:, n:n + width] += jnp.dot(
+            turned[...], windows[:, n:n + width], preferred_element_type=jnp.float32)
+
+    def build(i, windows, turned, pending=None):
         fetch(i).wait()
+        left = list(range(0, length, width)) if pending else []
+        share = up(len(left), batch * components) // (batch * components)
         for u in range(batch):
             for j in range(components):
                 values = loaded[i * batch + u, j].astype(jnp.float32)
@@ -120,30 +128,31 @@
                         begin = margin - (g - a) * GROUP
                         at = ((u * components + j) * groups + g) * GROUP
                         windows[at:at + GROUP, :] = rolled[:, begin:begin + length] * scale
-
-    def multiply(windows, turned):
-        width = min(2 * LANES, length)
+                for n in left[:share]:
+                    multiply(n, *pending)
+                left = left[share:]
+        for n in left:
+            multiply(n, *pending)
+
+    def finish(windows, turned):
         for n in range(0, length, width):
-            total[:, n:n + width] += jnp.dot(
-                turned[...], windows[:, n:n + width], preferred_element_type=jnp.float32)
-
-    build(0, windows_a, bank_a)
+            multiply(n, windows, turned)
+
+    a, b = (windows_a, bank_a), (windows_b, bank_b)
+    build(0, *a)
 
     def two_batches(i, carry):
-        build(2 * i + 1, windows_b, bank_b)
-        multiply(windows_a, bank_a)
-        build(2 * i + 2, windows_a, bank_a)
-        multiply(windows_b, bank_b)
+        build(2 * i + 1, *b, a)
+        build(2 * i + 2, *a, b)
         return carry
 
     if batches > 2:
         lax.fori_loop(0, (batches - 1) // 2, two_batches, 0)
     if batches % 2 == 0:
-        build(batches - 1, windows_b, bank_b)
-        multiply(windows_a, bank_a)
-        multiply(windows_b, bank_b)
+        build(batches - 1, *b, a)
+        finish(*b)
     else:
-        multiply(windows_a, bank_a)
+        finish(*a)
 
     core = core_ref[0]
     hops, region = keep_ref.shape[0], keep_ref.shape[1]

time: 34.8 us -> 34.8 us (level)
  no operation moved by 1% of the time
where the time goes in v5:
time: 34.8 us; the launch traced here: 34.6 us
  Pallas kernels  15.8 us (45%)
  starting transfers between devices  9.27 us (27%)
  waiting for transfers between devices  7.74 us (22%)
  other arithmetic  1.76 us (5%)
    pallas_call x1, Pallas kernels, correlate(): pl.pallas_call(functools.partial(correlate_kernel, window=window, batch=b...  15.8 us
    ppermute x3, starting transfers between devices, body(): lax.ppermute(block.astype(jnp.bfloat16), 'chan', perm).astype(jnp.float32)  5.83 us
    ppermute x1, waiting for transfers between devices, body(): lax.ppermute(block.astype(jnp.bfloat16), 'tm', perm).astype(jnp.float32)  3.8 us
    ppermute x1, starting transfers between devices, body(): lax.ppermute(block.astype(jnp.bfloat16), 'tm', perm).astype(jnp.float32)  2.93 us
    ppermute x3, waiting for transfers between devices, body(): lax.ppermute(block.astype(jnp.bfloat16), 'chan', perm).astype(jnp.float32)  2.57 us
    ppermute x1, waiting for transfers between devices, body(): got = lax.ppermute(send, 'tm', [(i, i ^ 1) for i in range(tm)])  1.37 us
    add x1, other arithmetic, body(): mine = keep + got.astype(jnp.float32)  1.09 us
  transfers between devices with their start and end apart: 5, of which 5 were waited for; matrix products, arithmetic and copies ran while one was open for 0% of the time, Pallas kernels for 0%

profile of v5, /device:TPU:0, one launch (start us, length us, event | category | flops | bytes accessed | tf_op | source)
XLA Modules:
  0.0 34.6 jit_solution(17149126427449530995)
XLA Ops:
  0.0 15.8 %correlate.1 = (bf16[2,256,256]{2,1,0:T(8,128)(2,1)}, f32[2,256,256]{2,1,0:T(8,128)}) custom-call(s32[1]{0:T(128)} %bitcast.core_ref, s32[3,16]{1,0:T(4,128)} %bitcast.28, s32[2,16]{1,0:T(2,128)} %bitcast.29, bf16[3,16,1024]{2,1,0:T(8,128)(2,1)} %bitcast.27, bf16[16,3,200,256]{3,2,1,0:T(8,128)(2,1)} %templates_ref.1), custom_call_target="tpu_custom_call" | custom-call | tf_op jit(solution)/shard_map/correlate/pallas_call | solution.py:185
  15.8 0.5 %collective-permute-start = (bf16[2,256,256]{2,1,0:T(8,128)(2,1)}, bf16[2,256,256]{2,1,0:T(8,128)(2,1)S(1)}, u32[]{:S(2)}, u32[]{:S(2)}) collective-permute-start(bf16[2,256,256]{2,1,0:T(8,128)(2,1)} %get-tuple-element.8), channel_id=1, source_target_pairs={{0,4},{4,0},{8,12},{12,8},{1,5},{5,1},{9,13},{13,9},{2,6},{6,2},{1... | collective-permute-start | bytes 786440 | tf_op jit(solution)/shard_map/ppermute | solution.py:219
  16.3 1.4 %collective-permute-done = bf16[2,256,256]{2,1,0:T(8,128)(2,1)S(1)} collective-permute-done((bf16[2,256,256]{2,1,0:T(8,128)(2,1)}, bf16[2,256,256]{2,1,0:T(8,128)(2,1)S(1)}, u32[]{:S(2)}, u32[]{:S(2)}) %collective-permute-start) | collective-permute-done | bytes 262176 | tf_op jit(solution)/shard_map/ppermute | solution.py:219
  17.7 1.1 %convert_add_fusion = f32[2,256,256]{2,1,0:T(8,128)S(1)} fusion(f32[2,256,256]{2,1,0:T(8,128)} %get-tuple-element.7, bf16[2,256,256]{2,1,0:T(8,128)(2,1)S(1)} %collective-permute-done), kind=kLoop, calls=%fused_computation | loop fusion | flops 262144 | bytes 1310720 | tf_op jit(solution)/shard_map/add | solution.py:220
  18.8 2.9 %collective-permute-start.1 = (bf16[256,256]{1,0:T(8,128)(2,1)S(1)}, bf16[256,256]{1,0:T(8,128)(2,1)S(1)}, u32[]{:S(2)}, u32[]{:S(2)}) collective-permute-start(bf16[256,256]{1,0:T(8,128)(2,1)S(1)} %fusion), channel_id=1, source_target_pairs={{0,8},{4,12},{8,0},{12,4},{1,9},{5,13},{9,1},{13,5},{2,10},{6,14},... | collective-permute-start | bytes 393224 | tf_op jit(solution)/shard_map/ppermute | solution.py:225
  21.7 3.8 %collective-permute-done.1 = bf16[256,256]{1,0:T(8,128)(2,1)S(1)} collective-permute-done((bf16[256,256]{1,0:T(8,128)(2,1)S(1)}, bf16[256,256]{1,0:T(8,128)(2,1)S(1)}, u32[]{:S(2)}, u32[]{:S(2)}) %collective-permute-start.1) | collective-permute-done | bytes 131104 | tf_op jit(solution)/shard_map/ppermute | solution.py:225
  25.6 1.9 %collective-permute-start.2 = (bf16[64,256]{1,0:T(8,128)(2,1)S(1)}, bf16[64,256]{1,0:T(8,128)(2,1)S(1)}, u32[]{:S(2)}, u32[]{:S(2)}) collective-permute-start(bf16[64,256]{1,0:T(8,128)(2,1)S(1)} %get-tuple-element.9), channel_id=1, source_target_pairs={{0,1},{1,2},{2,3},{3,0},{4,5},{5,6},{6,7},{7,4},{8,9},{9,10},{10,1... | collective-permute-start | bytes 98312 | tf_op jit(solution)/shard_map/ppermute | solution.py:231
  27.5 2.6 %collective-permute-start.3 = (bf16[64,256]{1,0:T(8,128)(2,1)S(1)}, bf16[64,256]{1,0:T(8,128)(2,1)S(1)}, u32[]{:S(2)}, u32[]{:S(2)}) collective-permute-start(bf16[64,256]{1,0:T(8,128)(2,1)S(1)} %get-tuple-element.11), channel_id=1, source_target_pairs={{0,2},{1,3},{2,0},{3,1},{4,6},{5,7},{6,4},{7,5},{8,10},{9,11},{10,... | collective-permute-start | bytes 98312 | tf_op jit(solution)/shard_map/ppermute | solution.py:231
  30.1 1.3 %collective-permute-start.4 = (bf16[64,256]{1,0:T(8,128)(2,1)S(1)}, bf16[64,256]{1,0:T(8,128)(2,1)S(1)}, u32[]{:S(2)}, u32[]{:S(2)}) collective-permute-start(bf16[64,256]{1,0:T(8,128)(2,1)S(1)} %get-tuple-element.10), channel_id=1, source_target_pairs={{0,3},{1,0},{2,1},{3,2},{4,7},{5,4},{6,5},{7,6},{8,11},{9,8},{10,9... | collective-permute-start | bytes 98312 | tf_op jit(solution)/shard_map/ppermute | solution.py:231
  31.4 0.4 %collective-permute-done.2 = bf16[64,256]{1,0:T(8,128)(2,1)S(1)} collective-permute-done((bf16[64,256]{1,0:T(8,128)(2,1)S(1)}, bf16[64,256]{1,0:T(8,128)(2,1)S(1)}, u32[]{:S(2)}, u32[]{:S(2)}) %collective-permute-start.2) | collective-permute-done | bytes 32800 | tf_op jit(solution)/shard_map/ppermute | solution.py:231
  31.9 0.6 %collective-permute-done.3 = bf16[64,256]{1,0:T(8,128)(2,1)S(1)} collective-permute-done((bf16[64,256]{1,0:T(8,128)(2,1)S(1)}, bf16[64,256]{1,0:T(8,128)(2,1)S(1)}, u32[]{:S(2)}, u32[]{:S(2)}) %collective-permute-start.3) | collective-permute-done | bytes 32800 | tf_op jit(solution)/shard_map/ppermute | solution.py:231
  32.4 1.6 %collective-permute-done.4 = bf16[64,256]{1,0:T(8,128)(2,1)S(1)} collective-permute-done((bf16[64,256]{1,0:T(8,128)(2,1)S(1)}, bf16[64,256]{1,0:T(8,128)(2,1)S(1)}, u32[]{:S(2)}, u32[]{:S(2)}) %collective-permute-start.4) | collective-permute-done | bytes 32800 | tf_op jit(solution)/shard_map/ppermute | solution.py:231
  34.0 0.6 %fusion.3 = f32[256,64]{0,1:T(8,128)} fusion(bf16[64,256]{1,0:T(8,128)(2,1)S(1)} %collective-permute-done.4, bf16[64,256]{1,0:T(8,128)(2,1)S(1)} %collective-permute-done.3, bf16[64,256]{1,0:T(8,128)(2,1)S(1)} %collective-permute-done.2, f32[4,64,256]{2,1,0:T(8,128)S(1)} %bitcast.26, s32[]{:T(128)S(6)} %select_n.52), kind=kLoop, calls=%fused_computation.7 | loop fusion | flops 98304 | bytes 229380 | tf_op jit(solution)/shard_map/transpose | solution.py:232
  (3 shorter events, 0.1 us)
Async XLA Ops:
  15.8 1.9 %collective-permute-start = (bf16[2,256,256]{2,1,0:T(8,128)(2,1)}, bf16[2,256,256]{2,1,0:T(8,128)(2,1)S(1)}, u32[]{:S(2)}, u32[]{:S(2)}) collective-permute-start(bf16[2,256,256]{2,1,0:T(8,128)(2,1)} %get-tuple-element.8), channel_id=1, source_target_pairs={{0,4},{4,0},{8,12},{12,8},{1,5},{5,1},{9,13},{13,9},{2,6},{6,2},{1... | collective-permute-start | bytes 786440 | tf_op jit(solution)/shard_map/ppermute | solution.py:219
  18.8 6.7 %collective-permute-start.1 = (bf16[256,256]{1,0:T(8,128)(2,1)S(1)}, bf16[256,256]{1,0:T(8,128)(2,1)S(1)}, u32[]{:S(2)}, u32[]{:S(2)}) collective-permute-start(bf16[256,256]{1,0:T(8,128)(2,1)S(1)} %fusion), channel_id=1, source_target_pairs={{0,8},{4,12},{8,0},{12,4},{1,9},{5,13},{9,1},{13,5},{2,10},{6,14},... | collective-permute-start | bytes 393224 | tf_op jit(solution)/shard_map/ppermute | solution.py:225
  25.6 6.3 %collective-permute-start.2 = (bf16[64,256]{1,0:T(8,128)(2,1)S(1)}, bf16[64,256]{1,0:T(8,128)(2,1)S(1)}, u32[]{:S(2)}, u32[]{:S(2)}) collective-permute-start(bf16[64,256]{1,0:T(8,128)(2,1)S(1)} %get-tuple-element.9), channel_id=1, source_target_pairs={{0,1},{1,2},{2,3},{3,0},{4,5},{5,6},{6,7},{7,4},{8,9},{9,10},{10,1... | collective-permute-start | bytes 98312 | tf_op jit(solution)/shard_map/ppermute | solution.py:231
  27.5 4.9 %collective-permute-start.3 = (bf16[64,256]{1,0:T(8,128)(2,1)S(1)}, bf16[64,256]{1,0:T(8,128)(2,1)S(1)}, u32[]{:S(2)}, u32[]{:S(2)}) collective-permute-start(bf16[64,256]{1,0:T(8,128)(2,1)S(1)} %get-tuple-element.11), channel_id=1, source_target_pairs={{0,2},{1,3},{2,0},{3,1},{4,6},{5,7},{6,4},{7,5},{8,10},{9,11},{10,... | collective-permute-start | bytes 98312 | tf_op jit(solution)/shard_map/ppermute | solution.py:231
  30.1 3.9 %collective-permute-start.4 = (bf16[64,256]{1,0:T(8,128)(2,1)S(1)}, bf16[64,256]{1,0:T(8,128)(2,1)S(1)}, u32[]{:S(2)}, u32[]{:S(2)}) collective-permute-start(bf16[64,256]{1,0:T(8,128)(2,1)S(1)} %get-tuple-element.10), channel_id=1, source_target_pairs={{0,3},{1,0},{2,1},{3,2},{4,7},{5,4},{6,5},{7,6},{8,11},{9,8},{10,9... | collective-permute-start | bytes 98312 | tf_op jit(solution)/shard_map/ppermute | solution.py:231

commit v6 on v4

v6 whole, which is shorter than its diff:
```python
import functools

import jax
import jax.numpy as jnp
from jax import lax
from jax.experimental import pallas as pl
from jax.experimental.pallas import tpu as pltpu
from jax.sharding import PartitionSpec as P

MAXMO = 1000
LANES = 128
GROUP = 16


def up(value, unit):
    return -(-value // unit) * unit


def window_sum(values, window):
    def behind(array, by):
        return array if by == 0 else pltpu.roll(array, by, 1)

    total, offset, size, run = None, 0, 1, values
    while size <= window:
        if window & size:
            piece = behind(run, offset)
            total = piece if total is None else total + piece
            offset += size
        size *= 2
        if size <= window:
            run = run + behind(run, size // 2)
    return total


def mirrored(array, region, size):
    return pl.multiple_of(array - (region + 1) * size, LANES)


def build_windows(shifted, factor, windows, channel, row, begins, size, groups, margin):
    for n, begin in enumerate(begins):
        half = jnp.broadcast_to(
            shifted[pl.ds(channel, 1), pl.ds(begin, size + margin)], (8, size + margin))
        strip = jnp.concatenate(
            [pltpu.roll(half, b, 1, stride=1, stride_axis=0) for b in (0, 8)], axis=0
        ).astype(jnp.bfloat16)
        scale = jnp.broadcast_to(factor[pl.ds(channel, 1), pl.ds(begin, size)], (GROUP, size))
        scale = scale.astype(jnp.bfloat16)
        for a in range(min(groups, LANES // GROUP)):
            deepest = list(range(a, groups, LANES // GROUP))[-1]
            first = margin - (deepest - a) * GROUP
            cut = max(first - LANES, 0)
            rolled = strip[:, cut:]
            rolled = rolled if a == 0 else pltpu.roll(rolled, a * GROUP, 1)
            for g in range(a, groups, LANES // GROUP):
                lane = margin - (g - a) * GROUP - cut
                windows[row + g * GROUP:row + (g + 1) * GROUP, n * size:(n + 1) * size] = (
                    rolled[:, lane:lane + size] * scale)


def multiply(total, windows, banks, width):
    for n in range(0, total.shape[1], width):
        result = total[:, n:n + width]
        for k, bank in enumerate(banks):
            depth = bank.shape[1]
            result += jnp.dot(
                bank[...], windows[k * depth:(k + 1) * depth, n:n + width],
                preferred_element_type=jnp.float32)
        total[:, n:n + width] = result


def in_order(total, at, h):
    flip = LANES - 1 - lax.broadcasted_iota(jnp.int32, (LANES, LANES), 1)
    return jnp.take_along_axis(total[h:h + LANES, at:at + LANES], flip, axis=1).T


def write_regions(total, out_ref, extra=None):
    count, size, bank_size = out_ref.shape
    for n in range(count):
        for r in range(0, size, LANES):
            for h in range(0, bank_size, LANES):
                block = in_order(total, n * size + size - LANES - r, h)
                if extra is not None:
                    block = block + extra(r, h)
                out_ref[n, r:r + LANES, h:h + LANES] = block.astype(out_ref.dtype)


def first_kernel(
    place_ref, moveouts_ref, uptime_ref, records_ref, templates_ref,
    send_ref, shifted, factor, banks_ref,
    masked, loaded, bank, windows_a, windows_b, bank_a, bank_b, total, arrived, stored,
    *, window, batch,
):
    components, stations, length = records_ref.shape
    block_count = uptime_ref.shape[0]
    batches = stations // batch
    rows = masked.shape[0]
    groups = up(window, GROUP) // GROUP
    margin = up(window, LANES)
    block_len = length // block_count
    span = shifted.shape[1]
    lead = masked.shape[1] - length

    def fetch(i):
        at = pl.ds(i * batch, batch)
        return pltpu.make_async_copy(templates_ref.at[at], loaded.at[at], arrived.at[i])

    for i in range(batches):
        fetch(i).start()

    masked[...] = jnp.zeros(masked.shape, jnp.float32)
    offsets = lax.broadcasted_iota(jnp.int32, (stations, LANES), 1)
    which = lax.broadcasted_iota(jnp.int32, (stations, LANES), 0)
    for b in range(block_count):
        limit = jnp.zeros((stations, LANES), jnp.int32)
        for s in range(stations):
            limit = jnp.where(which == s, uptime_ref[b, s], limit)
        for i in range(block_len // LANES):
            at = b * block_len + i * LANES
            live = offsets + i * LANES < limit
            for j in range(components):
                values = records_ref[j, :, at:at + LANES].astype(jnp.float32)
                factor[j * stations:(j + 1) * stations, at:at + LANES] = jnp.where(live, values, 0.0)
    mirror = LANES - 1 - lax.broadcasted_iota(jnp.int32, (8, LANES), 1)
    for g in range(0, rows, 8):
        for at in range(0, length, LANES):
            to = lead + length - LANES - at
            masked[g:g + 8, to:to + LANES] = jnp.take_along_axis(
                factor[g:g + 8, at:at + LANES], mirror, axis=1)
    shifted[...] = jnp.zeros(shifted.shape, jnp.float32)
    for j in range(components):
        for s in range(stations):
            c = j * stations + s
            moveout = moveouts_ref[j, s]
            whole = moveout // LANES * LANES
            base = pl.multiple_of(lead - margin - LANES - whole, LANES)
            row = masked[c:c + 1, pl.ds(base, span + LANES)]
            row = pltpu.roll(row, moveout - whole, 1)
            shifted[c:c + 1, :] = row[:, LANES:]
    for g in range(0, rows, 8):
        values = shifted[g:g + 8, :]
        energy = window_sum(values * values, window)[:, margin:]
        factor[g:g + 8, :] = lax.rsqrt(jnp.maximum(energy, 1.0))
    bank[...] = jnp.zeros(bank.shape, bank.dtype)
    total[...] = jnp.zeros(total.shape, total.dtype)
    depth = batch * components * groups * GROUP
    for windows in (windows_a, windows_b):
        if windows.shape[0] > depth:
            windows[depth:, :] = jnp.zeros((windows.shape[0] - depth, windows.shape[1]), windows.dtype)

    count, size = send_ref.shape[:2]
    core = place_ref[0] % 2
    begins = [mirrored(length, 2 * x + 1 - core, size) for x in range(count)]
    width = min(2 * LANES, size)

    def store(i, turned, which):
        return pltpu.make_async_copy(turned, banks_ref.at[i], stored.at[which])

    def build(i, windows, turned, which):
        fetch(i).wait()
        for u in range(batch):
            for j in range(components):
                values = loaded[i * batch + u, j].astype(jnp.float32)
                squares = jnp.sum(values * values, axis=0, keepdims=True)
                unit = (values * lax.rsqrt(squares + 1e-06)).astype(jnp.bfloat16)
                at = (u * components + j) * groups * GROUP
                bank[at:at + window, :] = unit
        turned[...] = bank[...].T
        for u in range(batch):
            for j in range(components):
                build_windows(
                    shifted, factor, windows, j * stations + i * batch + u,
                    (u * components + j) * groups * GROUP, begins, size, groups, margin)
        store(i, turned, which).start()

    build(0, windows_a, bank_a, 0)

    def two_batches(i, carry):
        @pl.when(i > 0)
        def _():
            store(2 * i - 1, bank_b, 1).wait()
        build(2 * i + 1, windows_b, bank_b, 1)
        multiply(total, windows_a, [bank_a], width)
        store(2 * i, bank_a, 0).wait()
        build(2 * i + 2, windows_a, bank_a, 0)
        multiply(total, windows_b, [bank_b], width)
        return carry

    if batches > 2:
        lax.fori_loop(0, (batches - 1) // 2, two_batches, 0)
    if batches % 2 == 0:
        if batches > 2:
            store(batches - 3, bank_b, 1).wait()
        build(batches - 1, windows_b, bank_b, 1)
        multiply(total, windows_a, [bank_a], width)
        multiply(total, windows_b, [bank_b], width)
        store(batches - 2, bank_a, 0).wait()
        store(batches - 1, bank_b, 1).wait()
    else:
        multiply(total, windows_a, [bank_a], width)
        store(batches - 1, bank_a, 0).wait()
        if batches > 1:
            store(batches - 2, bank_b, 1).wait()
    write_regions(total, send_ref)


def next_kernel(
    place_ref, shifted, factor, banks_ref, *refs,
    components, window, batch, own, phases,
):
    if own:
        came_ref, *refs = refs
    out_ref, loaded, windows_a, windows_b, total, arrived = refs
    length = factor.shape[1]
    batches = banks_ref.shape[0]
    slabs = batches // phases
    stations = batches * batch
    groups = up(window, GROUP) // GROUP
    margin = up(window, LANES)
    count, size = out_ref.shape[:2]
    slab = loaded.shape[2]

    def fetch(i):
        return pltpu.make_async_copy(banks_ref.at[i], loaded.at[i], arrived.at[i])

    for i in range(batches):
        fetch(i).start()
    total[...] = jnp.zeros(total.shape, total.dtype)
    depth = batch * components * groups * GROUP
    for windows in (windows_a, windows_b):
        for k in range(slabs):
            if slab > depth:
                windows[k * slab + depth:(k + 1) * slab, :] = jnp.zeros(
                    (slab - depth, windows.shape[1]), windows.dtype)
    core, x = place_ref[0] % 2, place_ref[0] // 2
    hops = length // (2 * size)
    if own:
        begins = [mirrored(length, 2 * x + core, size)]
    else:
        begins = [mirrored(length, 2 * ((x + n) % hops) + core, size) for n in range(1, hops)]
    width = min(2 * LANES, size)

    def build(p, windows):
        for k in range(slabs):
            for u in range(batch):
                for j in range(components):
                    build_windows(
                        shifted, factor, windows,
                        j * stations + (p * slabs + k) * batch + u,
                        k * slab + (u * components + j) * groups * GROUP,
                        begins, size, groups, margin)

    def product(p, windows):
        multiply(total, windows, [loaded.at[p * slabs + k] for k in range(slabs)], width)

    def ready(p):
        for k in range(slabs):
            fetch(p * slabs + k).wait()

    build(0, windows_a)

    def two_phases(i, carry):
        ready(2 * i)
        build(2 * i + 1, windows_b)
        product(2 * i, windows_a)
        ready(2 * i + 1)
        build(2 * i + 2, windows_a)
        product(2 * i + 1, windows_b)
        return carry

    if phases > 2:
        lax.fori_loop(0, (phases - 1) // 2, two_phases, 0)
    if phases % 2 == 0:
        ready(phases - 2)
        build(phases - 1, windows_b)
        product(phases - 2, windows_a)
        ready(phases - 1)
        product(phases - 1, windows_b)
    else:
        ready(phases - 1)
        product(phases - 1, windows_a)
    if own:
        write_regions(total, out_ref, lambda r, h: came_ref[
            x, r:r + LANES, h:h + LANES].astype(jnp.float32))
    else:
        write_regions(total, out_ref)


SCALARS = pl.BlockSpec(memory_space=pltpu.SMEM)
VECTORS = pl.BlockSpec(memory_space=pltpu.VMEM)
FAR = pl.BlockSpec(memory_space=pl.ANY)


def cost(stations, components, window, bank_size, samples, read):
    return pl.CostEstimate(
        flops=2 * stations * components * window * bank_size * samples,
        bytes_accessed=read, transcendentals=0)


def first_part(place, records, templates, moveouts, uptime, hops, batch):
    components, stations, length = records.shape
    window, bank_size = templates.shape[2:]
    margin = up(window, LANES)
    rows = up(stations * components, 8)
    region = length // (2 * hops)
    depth = up(batch * components * up(window, GROUP), LANES)
    return pl.pallas_call(
        functools.partial(first_kernel, window=window, batch=batch),
        in_specs=[SCALARS, SCALARS, SCALARS, VECTORS, FAR],
        out_specs=[VECTORS, VECTORS, VECTORS, FAR],
        scratch_shapes=[
            pltpu.VMEM((rows, length + margin + LANES + up(MAXMO, LANES)), jnp.float32),
            pltpu.VMEM(templates.shape, templates.dtype),
            pltpu.VMEM((depth, bank_size), jnp.bfloat16),
            pltpu.VMEM((depth, hops * region), jnp.bfloat16),
            pltpu.VMEM((depth, hops * region), jnp.bfloat16),
            pltpu.VMEM((bank_size, depth), jnp.bfloat16),
            pltpu.VMEM((bank_size, depth), jnp.bfloat16),
            pltpu.VMEM((bank_size, hops * region), jnp.float32),
            pltpu.SemaphoreType.DMA((stations // batch,)),
            pltpu.SemaphoreType.DMA((2,)),
        ],
        out_shape=[
            jax.ShapeDtypeStruct((hops, region, bank_size), jnp.bfloat16),
            jax.ShapeDtypeStruct((rows, length + margin), jnp.float32),
            jax.ShapeDtypeStruct((rows, length), jnp.float32),
            jax.ShapeDtypeStruct((stations // batch, bank_size, depth), jnp.bfloat16),
        ],
        compiler_params=pltpu.CompilerParams(vmem_limit_bytes=60 * 2**20),
        cost_estimate=cost(stations, components, window, bank_size, hops * region,
                           2 * templates.size * 2),
        name="other_core",
    )(place, moveouts, uptime, records, templates)


def next_part(place, shifted, factor, banks, came, count, region, components, window, batch):
    batches, bank_size, depth = banks.shape
    phases = batches // 2 if batches % 2 == 0 else batches
    slabs = batches // phases
    own = came is not None
    return pl.pallas_call(
        functools.partial(next_kernel, components=components, window=window, batch=batch,
                          own=own, phases=phases),
        in_specs=[SCALARS, VECTORS, VECTORS, FAR] + [VECTORS] * own,
        out_specs=VECTORS,
        scratch_shapes=[
            pltpu.VMEM(banks.shape, banks.dtype),
            pltpu.VMEM((slabs * depth, count * region), jnp.bfloat16),
            pltpu.VMEM((slabs * depth, count * region), jnp.bfloat16),
            pltpu.VMEM((bank_size, count * region), jnp.float32),
            pltpu.SemaphoreType.DMA((batches,)),
        ],
        out_shape=jax.ShapeDtypeStruct((count, region, bank_size), jnp.float32),
        compiler_params=pltpu.CompilerParams(vmem_limit_bytes=60 * 2**20),
        cost_estimate=cost(batches * batch, components, window, bank_size, count * region,
                           banks.size * 2),
        name="own_region" if own else "other_chips",
    )(place, shifted, factor, banks, *([came] if own else []))


def body(records, templates, moveouts, uptime):
    tm, chan = lax.axis_size("tm"), lax.axis_size("chan")
    hops = tm // 2
    t, z = lax.axis_index("tm"), lax.axis_index("chan")
    x = t // 2
    place = t.reshape(1)
    stations, components, length = records.shape
    window = templates.shape[2]
    region = length // tm
    batch = 2 if stations % 2 == 0 else 1
    send, shifted, factor, banks = first_part(
        place, records.transpose(1, 0, 2), templates, moveouts.T, uptime.T, hops, batch)
    came = lax.ppermute(send, "tm", [(i, i ^ 1) for i in range(tm)])
    arriving = []
    if hops > 1:
        others = next_part(
            place, shifted, factor, banks, None, hops - 1, region, components, window, batch)
        for step in range(1, hops):
            piece = lax.dynamic_index_in_dim(came, (x + step) % hops, 0, keepdims=False)
            piece = (others[step - 1] + piece.astype(jnp.float32)).astype(jnp.bfloat16)
            perm = [(i, ((i // 2 + step) % hops) * 2 + i % 2) for i in range(tm)]
            arriving.append(lax.ppermute(piece, "tm", perm))
    result = next_part(
        place, shifted, factor, banks, came, 1, region, components, window, batch)[0]
    for piece in arriving:
        result = result + piece.astype(jnp.float32)
    mine = result.reshape(chan, result.shape[0] // chan, result.shape[1])
    result = lax.dynamic_index_in_dim(mine, z, 0, keepdims=False)
    for step in range(1, chan):
        block = lax.dynamic_index_in_dim(mine, (z + step) % chan, 0, keepdims=False)
        perm = [(i, (i + step) % chan) for i in range(chan)]
        result = result + lax.ppermute(block.astype(jnp.bfloat16), "chan", perm).astype(jnp.float32)
    return result.T


def solution(mesh):
    placed = (
        P(("grp", "tm", "chan"), None, None),
        P(("tm", "chan"), None, None, None),
        P(("tm", "chan"), None),
        P(("grp", "tm", "chan"), None),
    )
    return jax.shard_map(
        body, mesh=mesh, in_specs=placed, out_specs=P(None, ("grp", "tm", "chan")), check_vma=False
    )
```

time: 34.8 us -> 46.8 us (1.34)
  Pallas kernels: 15.8 us -> 31.3 us
  waiting for transfers between devices: 7.75 us -> 4.71 us
  starting transfers between devices: 9.25 us -> 7.78 us
  other arithmetic: 1.76 us -> 2.7 us
    pallas_call x1 -> x3, Pallas kernels: 15.8 us -> 31.3 us  [the longest x1 16.6 us: first_part(): pl.pallas_call(functools.partial(first_kernel, window=window, batch=batch...]
    ppermute x2, waiting for transfers between devices: 5.17 us -> 0.01 us  [the longest x1 0.01 us: body(): came = lax.ppermute(send, 'tm', [(i, i ^ 1) for i in range(tm)])]
    ppermute x3, waiting for transfers between devices: 2.57 us -> 4.7 us  [body(): lax.ppermute(block.astype(jnp.bfloat16), 'chan', perm).astype(jnp.float32)]
    ppermute x3, starting transfers between devices: 5.82 us -> 4.64 us  [body(): lax.ppermute(block.astype(jnp.bfloat16), 'chan', perm).astype(jnp.float32)]
    convert_element_type x0 -> x1, other arithmetic: none -> 1.08 us  [body(): piece = (others[step - 1] + piece.astype(jnp.float32)).astype(jnp.bfloat16)]
    add x2 -> x1, other arithmetic: 1.12 us -> 0.98 us  [body(): result = result + piece.astype(jnp.float32)]
  transfers between devices with their start and end apart: 5 -> 5, of which waited for: 5 -> 3; matrix products, arithmetic and copies ran while one was open for 0% -> 0% of each run, Pallas kernels for 0% -> 32%
where the time goes in v6:
time: 46.8 us; the launch traced here: 46.5 us
  Pallas kernels  31.3 us (67%)
  starting transfers between devices  7.78 us (17%)
  waiting for transfers between devices  4.71 us (10%)
  other arithmetic  2.7 us (6%)
    pallas_call x1, Pallas kernels, first_part(): pl.pallas_call(functools.partial(first_kernel, window=window, batch=batch...  16.6 us
    pallas_call x2, Pallas kernels, next_part(): pl.pallas_call(functools.partial(next_kernel, components=components, wind...  14.7 us
    ppermute x3, waiting for transfers between devices, body(): lax.ppermute(block.astype(jnp.bfloat16), 'chan', perm).astype(jnp.float32)  4.7 us
    ppermute x3, starting transfers between devices, body(): lax.ppermute(block.astype(jnp.bfloat16), 'chan', perm).astype(jnp.float32)  4.64 us
    ppermute x1, starting transfers between devices, body(): arriving.append(lax.ppermute(piece, 'tm', perm))  2.62 us
    convert_element_type x1, other arithmetic, body(): piece = (others[step - 1] + piece.astype(jnp.float32)).astype(jnp.bfloat16)  1.08 us
    add x1, other arithmetic, body(): result = result + piece.astype(jnp.float32)  0.98 us
  transfers between devices with their start and end apart: 5, of which 3 were waited for; matrix products, arithmetic and copies ran while one was open for 0% of the time, Pallas kernels for 32%

profile of v6, /device:TPU:0, one launch (start us, length us, event | category | flops | bytes accessed | tf_op | source)
XLA Modules:
  0.0 46.5 jit_solution(6408490794145155838)
XLA Ops:
  0.0 16.6 %other_core.1 = (bf16[2,256,256]{2,1,0:T(8,128)(2,1)}, f32[48,1280]{1,0:T(8,128)}, f32[48,1024]{1,0:T(8,128)}, bf16[8,256,1280]{2,1,0:T(8,128)(2,1)}) custom-call(s32[1]{0:T(128)} %bitcast.place_ref, s32[3,16]{1,0:T(4,128)} %bitcast.28, s32[2,16]{1,0:T(2,128)} %bitcast.29, bf16[3,16,1024]{2,1,0:T(8,128)(2,1)} %bitcast.27, bf16[16,3,200,256]{3,2,1,0:T(8,128)(2,1)} %templates_ref.1), custom_call_target="tpu_custom_call" | custom-call | flops 2516582400 | bytes 9830400 | tf_op jit(solution)/shard_map/other_core/pallas_call | solution.py:306
  16.6 0.5 %collective-permute-start = (bf16[2,256,256]{2,1,0:T(8,128)(2,1)}, bf16[2,256,256]{2,1,0:T(8,128)(2,1)S(1)}, u32[]{:S(2)}, u32[]{:S(2)}) collective-permute-start(bf16[2,256,256]{2,1,0:T(8,128)(2,1)} %get-tuple-element.12), channel_id=1, source_target_pairs={{0,4},{4,0},{8,12},{12,8},{1,5},{5,1},{9,13},{13,9},{2,6},{6,2},{1... | collective-permute-start | bytes 786440 | tf_op jit(solution)/shard_map/ppermute | solution.py:372
  17.1 7.3 %other_chips.1 = f32[1,256,256]{2,1,0:T(8,128)} custom-call(s32[1]{0:T(128)} %bitcast.place_ref, f32[48,1280]{1,0:T(8,128)} %get-tuple-element.9.shifted, f32[48,1024]{1,0:T(8,128)} %get-tuple-element.10.factor, bf16[8,256,1280]{2,1,0:T(8,128)(2,1)} %get-tuple-element.11.banks_ref), custom_call_target="tpu_custom_call" | custom-call | flops 1258291200 | bytes 5242880 | tf_op jit(solution)/shard_map/other_chips/pallas_call | solution.py:340
  24.4 0.0 collective-permute-done.refs_0_
  24.4 0.0 copy-start
  24.4 1.1 %fusion = bf16[256,256]{1,0:T(8,128)(2,1)S(1)} fusion(f32[1,256,256]{2,1,0:T(8,128)} %other_chips.1, bf16[2,256,256]{2,1,0:T(8,128)(2,1)S(1)} %collective-permute-done.refs_0_, s32[]{:T(128)S(6)} %select_n.42), kind=kLoop, calls=%fused_computation.2 | loop fusion | flops 196608 | bytes 524292 | tf_op jit(solution)/shard_map/convert_element_type | solution.py:379
  25.5 2.6 %collective-permute-start.1 = (bf16[256,256]{1,0:T(8,128)(2,1)S(1)}, bf16[256,256]{1,0:T(8,128)(2,1)S(1)}, u32[]{:S(2)}, u32[]{:S(2)}) collective-permute-start(bf16[256,256]{1,0:T(8,128)(2,1)S(1)} %fusion), channel_id=1, source_target_pairs={{0,8},{4,12},{8,0},{12,4},{1,9},{5,13},{9,1},{13,5},{2,10},{6,14},... | collective-permute-start | bytes 393224 | tf_op jit(solution)/shard_map/ppermute | solution.py:381
  28.1 0.0 copy-done
  28.1 7.4 %own_region.1 = f32[1,256,256]{2,1,0:T(8,128)} custom-call(s32[1]{0:T(128)} %bitcast.place_ref, f32[48,1280]{1,0:T(8,128)} %get-tuple-element.9.shifted, f32[48,1024]{1,0:T(8,128)} %get-tuple-element.10.factor, bf16[8,256,1280]{2,1,0:T(8,128)(2,1)} %get-tuple-element.11.banks_ref, bf16[2,256,256]{2,1,0:T(8,128)(2,1)} %copy-done), custom_call_target="tpu_custom_call" | custom-call | flops 1258291200 | bytes 5242880 | tf_op jit(solution)/shard_map/own_region/pallas_call | solution.py:340
  35.5 0.0 collective-permute-done.1
  35.5 1.0 %bitcast_add_fusion = f32[256,256]{1,0:T(8,128)S(1)} fusion(f32[1,256,256]{2,1,0:T(8,128)} %own_region.1, bf16[256,256]{1,0:T(8,128)(2,1)S(1)} %collective-permute-done.1), kind=kLoop, calls=%fused_computation | loop fusion | flops 131072 | bytes 655360 | tf_op jit(solution)/shard_map/add | solution.py:385
  36.5 3.6 %collective-permute-start.4 = (bf16[64,256]{1,0:T(8,128)(2,1)S(1)}, bf16[64,256]{1,0:T(8,128)(2,1)S(1)}, u32[]{:S(2)}, u32[]{:S(2)}) collective-permute-start(bf16[64,256]{1,0:T(8,128)(2,1)S(1)} %get-tuple-element.14), channel_id=1, source_target_pairs={{0,3},{1,0},{2,1},{3,2},{4,7},{5,4},{6,5},{7,6},{8,11},{9,8},{10,9... | collective-permute-start | bytes 98312 | tf_op jit(solution)/shard_map/ppermute | solution.py:391
  40.2 0.0 collective-permute-start.3
  40.2 1.0 %collective-permute-start.2 = (bf16[64,256]{1,0:T(8,128)(2,1)S(1)}, bf16[64,256]{1,0:T(8,128)(2,1)S(1)}, u32[]{:S(2)}, u32[]{:S(2)}) collective-permute-start(bf16[64,256]{1,0:T(8,128)(2,1)S(1)} %get-tuple-element.13), channel_id=1, source_target_pairs={{0,1},{1,2},{2,3},{3,0},{4,5},{5,6},{6,7},{7,4},{8,9},{9,10},{10,1... | collective-permute-start | bytes 98312 | tf_op jit(solution)/shard_map/ppermute | solution.py:391
  41.2 0.7 %collective-permute-done.4 = bf16[64,256]{1,0:T(8,128)(2,1)S(1)} collective-permute-done((bf16[64,256]{1,0:T(8,128)(2,1)S(1)}, bf16[64,256]{1,0:T(8,128)(2,1)S(1)}, u32[]{:S(2)}, u32[]{:S(2)}) %collective-permute-start.4) | collective-permute-done | bytes 32800 | tf_op jit(solution)/shard_map/ppermute | solution.py:391
  41.9 3.3 %collective-permute-done.3 = bf16[64,256]{1,0:T(8,128)(2,1)S(1)} collective-permute-done((bf16[64,256]{1,0:T(8,128)(2,1)S(1)}, bf16[64,256]{1,0:T(8,128)(2,1)S(1)}, u32[]{:S(2)}, u32[]{:S(2)}) %collective-permute-start.3) | collective-permute-done | bytes 32800 | tf_op jit(solution)/shard_map/ppermute | solution.py:391
  45.2 0.7 %collective-permute-done.2 = bf16[64,256]{1,0:T(8,128)(2,1)S(1)} collective-permute-done((bf16[64,256]{1,0:T(8,128)(2,1)S(1)}, bf16[64,256]{1,0:T(8,128)(2,1)S(1)}, u32[]{:S(2)}, u32[]{:S(2)}) %collective-permute-start.2) | collective-permute-done | bytes 32800 | tf_op jit(solution)/shard_map/ppermute | solution.py:391
  45.9 0.6 %fusion.3 = f32[256,64]{0,1:T(8,128)} fusion(bf16[64,256]{1,0:T(8,128)(2,1)S(1)} %collective-permute-done.4, bf16[64,256]{1,0:T(8,128)(2,1)S(1)} %collective-permute-done.3, bf16[64,256]{1,0:T(8,128)(2,1)S(1)} %collective-permute-done.2, f32[4,64,256]{2,1,0:T(8,128)S(1)} %bitcast.26, s32[]{:T(128)S(6)} %select_n.43), kind=kLoop, calls=%fused_computation.6 | loop fusion | flops 98304 | bytes 229380 | tf_op jit(solution)/shard_map/transpose | solution.py:392
  (1 shorter events, 0.0 us)
Async XLA Ops:
  16.6 7.8 %collective-permute-start = (bf16[2,256,256]{2,1,0:T(8,128)(2,1)}, bf16[2,256,256]{2,1,0:T(8,128)(2,1)S(1)}, u32[]{:S(2)}, u32[]{:S(2)}) collective-permute-start(bf16[2,256,256]{2,1,0:T(8,128)(2,1)} %get-tuple-element.12), channel_id=1, source_target_pairs={{0,4},{4,0},{8,12},{12,8},{1,5},{5,1},{9,13},{13,9},{2,6},{6,2},{1... | collective-permute-start | bytes 786440 | tf_op jit(solution)/shard_map/ppermute | solution.py:372
  24.4 3.7 %copy-start = (bf16[2,256,256]{2,1,0:T(8,128)(2,1)}, bf16[2,256,256]{2,1,0:T(8,128)(2,1)S(1)}, u32[]{:S(2)}) copy-start(bf16[2,256,256]{2,1,0:T(8,128)(2,1)S(1)} %collective-permute-done.refs_0_) | copy-start | bytes 786436
  25.5 10.0 %collective-permute-start.1 = (bf16[256,256]{1,0:T(8,128)(2,1)S(1)}, bf16[256,256]{1,0:T(8,128)(2,1)S(1)}, u32[]{:S(2)}, u32[]{:S(2)}) collective-permute-start(bf16[256,256]{1,0:T(8,128)(2,1)S(1)} %fusion), channel_id=1, source_target_pairs={{0,8},{4,12},{8,0},{12,4},{1,9},{5,13},{9,1},{13,5},{2,10},{6,14},... | collective-permute-start | bytes 393224 | tf_op jit(solution)/shard_map/ppermute | solution.py:381
  36.5 5.3 %collective-permute-start.4 = (bf16[64,256]{1,0:T(8,128)(2,1)S(1)}, bf16[64,256]{1,0:T(8,128)(2,1)S(1)}, u32[]{:S(2)}, u32[]{:S(2)}) collective-permute-start(bf16[64,256]{1,0:T(8,128)(2,1)S(1)} %get-tuple-element.14), channel_id=1, source_target_pairs={{0,3},{1,0},{2,1},{3,2},{4,7},{5,4},{6,5},{7,6},{8,11},{9,8},{10,9... | collective-permute-start | bytes 98312 | tf_op jit(solution)/shard_map/ppermute | solution.py:391
  40.2 5.0 %collective-permute-start.3 = (bf16[64,256]{1,0:T(8,128)(2,1)S(1)}, bf16[64,256]{1,0:T(8,128)(2,1)S(1)}, u32[]{:S(2)}, u32[]{:S(2)}) collective-permute-start(bf16[64,256]{1,0:T(8,128)(2,1)S(1)} %get-tuple-element.15), channel_id=1, source_target_pairs={{0,2},{1,3},{2,0},{3,1},{4,6},{5,7},{6,4},{7,5},{8,10},{9,11},{10,... | collective-permute-start | bytes 98312 | tf_op jit(solution)/shard_map/ppermute | solution.py:391
  40.2 5.7 %collective-permute-start.2 = (bf16[64,256]{1,0:T(8,128)(2,1)S(1)}, bf16[64,256]{1,0:T(8,128)(2,1)S(1)}, u32[]{:S(2)}, u32[]{:S(2)}) collective-permute-start(bf16[64,256]{1,0:T(8,128)(2,1)S(1)} %get-tuple-element.13), channel_id=1, source_target_pairs={{0,1},{1,2},{2,3},{3,0},{4,5},{5,6},{6,7},{7,4},{8,9},{9,10},{10,1... | collective-permute-start | bytes 98312 | tf_op jit(solution)/shard_map/ppermute | solution.py:391

commit v7 on v5

v7 whole, which is shorter than its diff:
```python
import functools

import jax
import jax.numpy as jnp
from jax import lax
from jax.experimental import pallas as pl
from jax.experimental.pallas import tpu as pltpu
from jax.sharding import PartitionSpec as P

MAXMO = 1000
LANES = 128
GROUP = 16


def up(value, unit):
    return -(-value // unit) * unit


def window_sum(values, window):
    def behind(array, by):
        return array if by == 0 else pltpu.roll(array, by, 1)

    total, offset, size, run = None, 0, 1, values
    while size <= window:
        if window & size:
            piece = behind(run, offset)
            total = piece if total is None else total + piece
            offset += size
        size *= 2
        if size <= window:
            run = run + behind(run, size // 2)
    return total


def correlate_kernel(
    core_ref, moveouts_ref, uptime_ref, records_ref, templates_ref,
    send_ref, keep_ref,
    masked, shifted, factor, loaded, bank, windows_a, windows_b, bank_a, bank_b, total, arrived,
    *, window,
):
    components, stations, length = records_ref.shape
    block_count = uptime_ref.shape[0]
    rows = masked.shape[0]
    groups = up(window, GROUP) // GROUP
    margin = up(window, LANES)
    block_len = length // block_count
    span = shifted.shape[1]
    lead = masked.shape[1] - length

    def fetch(i):
        return pltpu.make_async_copy(templates_ref.at[i], loaded.at[i], arrived.at[i])

    def start(i, carry):
        fetch(i).start()
        return carry

    lax.fori_loop(0, stations, start, 0)

    masked[:, :lead] = jnp.zeros((rows, lead), jnp.float32)
    shifted[...] = jnp.zeros(shifted.shape, jnp.float32)
    total[...] = jnp.zeros(total.shape, total.dtype)
    for ref in (bank, bank_a, bank_b, windows_b):
        ref[...] = jnp.zeros(ref.shape, ref.dtype)
    depth = components * groups * GROUP
    if windows_a.shape[0] > depth:
        windows_a[depth:, :] = jnp.zeros((windows_a.shape[0] - depth, length), windows_a.dtype)
    offsets = lax.broadcasted_iota(jnp.int32, (stations, LANES), 1)
    which = lax.broadcasted_iota(jnp.int32, (stations, LANES), 0)
    mirror = LANES - 1 - lax.broadcasted_iota(jnp.int32, (up(stations, 8), LANES), 1)

    def mask_tile(i, carry):
        at = pl.multiple_of(i * LANES, LANES)
        to = pl.multiple_of(lead + length - LANES - at, LANES)
        block = at // block_len
        limit = jnp.zeros((stations, LANES), jnp.int32)
        for s in range(stations):
            limit = jnp.where(which == s, uptime_ref[block, s], limit)
        live = offsets + (at - block * block_len) < limit
        for j in range(components):
            values = records_ref[j, :, pl.ds(at, LANES)].astype(jnp.float32)
            values = jnp.where(live, values, 0.0)
            if stations % 8:
                rest = jnp.zeros((up(stations, 8) - stations, LANES), jnp.float32)
                values = jnp.concatenate([values, rest], axis=0)
            values = jnp.take_along_axis(values, mirror, axis=1)
            masked[j * stations:(j + 1) * stations, pl.ds(to, LANES)] = values[:stations]
        return carry

    lax.fori_loop(0, length // LANES, mask_tile, 0)
    burst = 4 if stations % 4 == 0 else 1

    def shift_some(i, carry):
        shifts = []
        for u in range(burst):
            for j in range(components):
                c = j * stations + i * burst + u
                moveout = moveouts_ref[j, i * burst + u]
                whole = moveout // LANES * LANES
                base = pl.multiple_of(lead - margin - LANES - whole, LANES)
                row = masked[pl.ds(c, 1), pl.ds(base, span + LANES)]
                shifts.append((c, pltpu.roll(row, moveout - whole, 1)))
        for c, row in shifts:
            shifted[pl.ds(c, 1), :] = row[:, LANES:]
        return carry

    lax.fori_loop(0, stations // burst, shift_some, 0)
    chunk = rows // 2 if rows % 16 == 0 else 8

    def energy_some(i, carry):
        at = pl.ds(pl.multiple_of(i * chunk, 8), chunk)
        values = shifted[at, :]
        energy = window_sum(values * values, window)[:, margin:]
        factor[at, :] = lax.rsqrt(jnp.maximum(energy, 1.0))
        return carry

    lax.fori_loop(0, rows // chunk, energy_some, 0)
    width = min(2 * LANES, length)

    def multiply(n, windows, turned):
        total[:, n:n + width] += jnp.dot(
            turned[...], windows[:, n:n + width], preferred_element_type=jnp.float32)

    def build(i, windows, turned, pending):
        strips, scales = [], []
        for j in range(components):
            c = j * stations + i
            half = jnp.broadcast_to(shifted[pl.ds(c, 1), :], (8, span))
            strips.append(jnp.concatenate(
                [pltpu.roll(half, b, 1, stride=1, stride_axis=0) for b in (0, 8)], axis=0
            ).astype(jnp.bfloat16))
            scale = jnp.broadcast_to(factor[pl.ds(c, 1), :], (GROUP, length))
            scales.append(scale.astype(jnp.bfloat16))
        for j in range(components):
            values = loaded[i, j].astype(jnp.float32)
            squares = jnp.sum(values * values, axis=0, keepdims=True)
            unit = (values * lax.rsqrt(squares + 1e-06)).astype(jnp.bfloat16)
            at = j * groups * GROUP
            bank[at:at + window, :] = unit
        turned[...] = bank[...].T
        left = list(range(0, length, width))
        share = up(len(left), components) // components
        for j in range(components):
            for a in range(min(groups, LANES // GROUP)):
                rolled = strips[j] if a == 0 else pltpu.roll(strips[j], a * GROUP, 1)
                for g in range(a, groups, LANES // GROUP):
                    begin = margin - (g - a) * GROUP
                    at = (j * groups + g) * GROUP
                    windows[at:at + GROUP, :] = rolled[:, begin:begin + length] * scales[j]
            for n in left[:share]:
                multiply(n, *pending)
            left = left[share:]

    def two_stations(i, carry):
        station = jnp.minimum(2 * i, stations - 1)

        @pl.when(2 * i < stations)
        def _():
            fetch(2 * i).wait()

        build(station, windows_a, bank_a, (windows_b, bank_b))

        @pl.when(2 * i < stations)
        def _():
            later = jnp.minimum(2 * i + 1, stations - 1)

            @pl.when(2 * i + 1 < stations)
            def _():
                fetch(2 * i + 1).wait()

            build(later, windows_b, bank_b, (windows_a, bank_a))

        return carry

    lax.fori_loop(0, stations // 2 + 1, two_stations, 0)

    core = core_ref[0]
    hops, region = keep_ref.shape[0], keep_ref.shape[1]
    flip = LANES - 1 - lax.broadcasted_iota(jnp.int32, (LANES, LANES), 1)

    def ordered(begin, h):
        at = pl.multiple_of(length - LANES - begin, LANES)
        block = total[h:h + LANES, pl.ds(at, LANES)]
        return jnp.take_along_axis(block, flip, axis=1).T

    def write(i, carry):
        x = i // (region // LANES)
        r = pl.multiple_of(i % (region // LANES) * LANES, LANES)
        own = (2 * x + core) * region + r
        other = (2 * x + 1 - core) * region + r
        for h in range(0, total.shape[0], LANES):
            keep_ref[x, pl.ds(r, LANES), h:h + LANES] = ordered(own, h)
            send_ref[x, pl.ds(r, LANES), h:h + LANES] = ordered(other, h).astype(send_ref.dtype)
        return carry

    lax.fori_loop(0, hops * (region // LANES), write, 0)


def correlate(core, records, templates, moveouts, uptime, hops):
    components, stations, length = records.shape
    window, bank_size = templates.shape[2:]
    margin = up(window, LANES)
    rows = up(stations * components, 8)
    region = length // (2 * hops)
    depth = up(components * up(window, GROUP), LANES)
    scalars = pl.BlockSpec(memory_space=pltpu.SMEM)
    vectors = pl.BlockSpec(memory_space=pltpu.VMEM)
    return pl.pallas_call(
        functools.partial(correlate_kernel, window=window),
        in_specs=[scalars, scalars, scalars, vectors, pl.BlockSpec(memory_space=pl.ANY)],
        out_specs=[vectors, vectors],
        scratch_shapes=[
            pltpu.VMEM((rows, length + margin + LANES + up(MAXMO, LANES)), jnp.float32),
            pltpu.VMEM((rows, length + margin), jnp.float32),
            pltpu.VMEM((rows, length), jnp.float32),
            pltpu.VMEM(templates.shape, templates.dtype),
            pltpu.VMEM((depth, bank_size), jnp.bfloat16),
            pltpu.VMEM((depth, length), jnp.bfloat16),
            pltpu.VMEM((depth, length), jnp.bfloat16),
            pltpu.VMEM((bank_size, depth), jnp.bfloat16),
            pltpu.VMEM((bank_size, depth), jnp.bfloat16),
            pltpu.VMEM((bank_size, length), jnp.float32),
            pltpu.SemaphoreType.DMA((stations,)),
        ],
        out_shape=[
            jax.ShapeDtypeStruct((hops, region, bank_size), jnp.bfloat16),
            jax.ShapeDtypeStruct((hops, region, bank_size), jnp.float32),
        ],
        compiler_params=pltpu.CompilerParams(vmem_limit_bytes=52 * 2**20),
        name="correlate",
    )(core, moveouts, uptime, records, templates)


def body(records, templates, moveouts, uptime):
    tm, chan = lax.axis_size("tm"), lax.axis_size("chan")
    hops = tm // 2
    t, z = lax.axis_index("tm"), lax.axis_index("chan")
    x, core = t // 2, t % 2
    send, keep = correlate(
        core.reshape(1), records.transpose(1, 0, 2), templates, moveouts.T, uptime.T, hops
    )
    got = lax.ppermute(send, "tm", [(i, i ^ 1) for i in range(tm)])
    mine = keep + got.astype(jnp.float32)
    result = lax.dynamic_index_in_dim(mine, x, 0, keepdims=False)
    for step in range(1, hops):
        block = lax.dynamic_index_in_dim(mine, (x + step) % hops, 0, keepdims=False)
        perm = [(i, ((i // 2 + step) % hops) * 2 + i % 2) for i in range(tm)]
        result = result + lax.ppermute(block.astype(jnp.bfloat16), "tm", perm).astype(jnp.float32)
    mine = result.reshape(chan, result.shape[0] // chan, result.shape[1])
    result = lax.dynamic_index_in_dim(mine, z, 0, keepdims=False)
    for step in range(1, chan):
        block = lax.dynamic_index_in_dim(mine, (z + step) % chan, 0, keepdims=False)
        perm = [(i, (i + step) % chan) for i in range(chan)]
        result = result + lax.ppermute(block.astype(jnp.bfloat16), "chan", perm).astype(jnp.float32)
    return result.T


def solution(mesh):
    placed = (
        P(("grp", "tm", "chan"), None, None),
        P(("tm", "chan"), None, None, None),
        P(("tm", "chan"), None),
        P(("grp", "tm", "chan"), None),
    )
    return jax.shard_map(
        body, mesh=mesh, in_specs=placed, out_specs=P(None, ("grp", "tm", "chan")), check_vma=False
    )
```

time: 34.8 us -> 35.6 us (1.023)
  local copies, waits for them, and re-layouts: 0.04 us -> 2.3 us
  other arithmetic: 1.76 us -> 0.72 us
    unnamed x0 -> x6, local copies, waits for them, and re-layouts: none -> 2.25 us
    add x1, other arithmetic: 1.09 us -> 0.05 us  [body(): mine = keep + got.astype(jnp.float32)]
where the time goes in v7:
time: 35.6 us; the launch traced here: 35.4 us
  Pallas kernels  15.6 us (44%)
  starting transfers between devices  9.2 us (26%)
  waiting for transfers between devices  7.53 us (21%)
  local copies, waits for them, and re-layouts  2.3 us (6%)
  other arithmetic  0.72 us (2%)
    pallas_call x1, Pallas kernels, correlate(): pl.pallas_call(functools.partial(correlate_kernel, window=window), in_spe...  15.6 us
    ppermute x3, starting transfers between devices, body(): lax.ppermute(block.astype(jnp.bfloat16), 'chan', perm).astype(jnp.float32)  5.8 us
    ppermute x1, waiting for transfers between devices, body(): lax.ppermute(block.astype(jnp.bfloat16), 'tm', perm).astype(jnp.float32)  3.8 us
    ppermute x1, starting transfers between devices, body(): lax.ppermute(block.astype(jnp.bfloat16), 'tm', perm).astype(jnp.float32)  2.87 us
    ppermute x3, waiting for transfers between devices, body(): lax.ppermute(block.astype(jnp.bfloat16), 'chan', perm).astype(jnp.float32)  2.57 us
    unnamed x6, local copies, waits for them, and re-layouts  2.25 us
    ppermute x1, waiting for transfers between devices, body(): got = lax.ppermute(send, 'tm', [(i, i ^ 1) for i in range(tm)])  1.16 us
  transfers between devices with their start and end apart: 5, of which 5 were waited for; matrix products, arithmetic and copies ran while one was open for 0% of the time, Pallas kernels for 0%

profile of v7, /device:TPU:0, one launch (start us, length us, event | category | flops | bytes accessed | tf_op | source)
XLA Modules:
  0.0 35.4 jit_solution(4580820819733449168)
XLA Ops:
  0.0 0.0 copy-start
  0.0 0.9 %copy-done = bf16[16,3,1024]{2,0,1:T(8,128)(2,1)S(1)} copy-done((bf16[16,3,1024]{2,0,1:T(8,128)(2,1)S(1)}, bf16[16,3,1024]{2,0,1:T(8,128)(2,1)}, u32[]{:S(2)}) %copy-start) | copy-done | bytes 98328
  0.9 0.0 copy-start.1
  0.9 0.7 %copy-done.1 = s32[16,3]{0,1:T(4,128)S(1)} copy-done((s32[16,3]{0,1:T(4,128)S(1)}, s32[16,3]{0,1:T(4,128)}, u32[]{:S(2)}) %copy-start.1) | copy-done | bytes 216
  1.6 0.0 copy-start.2
  1.6 0.7 %copy-done.2 = s32[16,2]{0,1:T(2,128)S(1)} copy-done((s32[16,2]{0,1:T(2,128)S(1)}, s32[16,2]{0,1:T(2,128)}, u32[]{:S(2)}) %copy-start.2) | copy-done | bytes 152
  2.3 15.6 %correlate.1 = (bf16[2,256,256]{2,1,0:T(8,128)(2,1)S(1)}, f32[2,256,256]{2,1,0:T(8,128)S(1)}) custom-call(s32[1]{0:T(128)} %bitcast.core_ref, s32[3,16]{1,0:T(4,128)S(1)} %bitcast.26, s32[2,16]{1,0:T(2,128)S(1)} %bitcast.27, bf16[3,16,1024]{2,1,0:T(8,128)(2,1)S(1)} %bitcast.25, bf16[16,3,200,256]{3,2,1,0:T(8,128)(2,1)} %templates_ref.1), custom_call_target="tpu_custom_call" | custom-call | tf_op jit(solution)/shard_map/correlate/pallas_call | solution.py:207
  17.9 0.5 %collective-permute-start = (bf16[2,256,256]{2,1,0:T(8,128)(2,1)S(1)}, bf16[2,256,256]{2,1,0:T(8,128)(2,1)S(1)}, u32[]{:S(2)}, u32[]{:S(2)}) collective-permute-start(bf16[2,256,256]{2,1,0:T(8,128)(2,1)S(1)} %get-tuple-element.8), channel_id=1, source_target_pairs={{0,4},{4,0},{8,12},{12,8},{1,5},{5,1},{9,13},{13,9},{2,6},{6,2},{1... | collective-permute-start | bytes 786440 | tf_op jit(solution)/shard_map/ppermute | solution.py:241
  18.4 1.2 %collective-permute-done = bf16[2,256,256]{2,1,0:T(8,128)(2,1)S(1)} collective-permute-done((bf16[2,256,256]{2,1,0:T(8,128)(2,1)S(1)}, bf16[2,256,256]{2,1,0:T(8,128)(2,1)S(1)}, u32[]{:S(2)}, u32[]{:S(2)}) %collective-permute-start) | collective-permute-done | bytes 262176 | tf_op jit(solution)/shard_map/ppermute | solution.py:241
  19.6 0.1 convert_add_fusion
  19.6 2.9 %collective-permute-start.1 = (bf16[256,256]{1,0:T(8,128)(2,1)S(1)}, bf16[256,256]{1,0:T(8,128)(2,1)S(1)}, u32[]{:S(2)}, u32[]{:S(2)}) collective-permute-start(bf16[256,256]{1,0:T(8,128)(2,1)S(1)} %fusion), channel_id=1, source_target_pairs={{0,8},{4,12},{8,0},{12,4},{1,9},{5,13},{9,1},{13,5},{2,10},{6,14},... | collective-permute-start | bytes 393224 | tf_op jit(solution)/shard_map/ppermute | solution.py:247
  22.5 3.8 %collective-permute-done.1 = bf16[256,256]{1,0:T(8,128)(2,1)S(1)} collective-permute-done((bf16[256,256]{1,0:T(8,128)(2,1)S(1)}, bf16[256,256]{1,0:T(8,128)(2,1)S(1)}, u32[]{:S(2)}, u32[]{:S(2)}) %collective-permute-start.1) | collective-permute-done | bytes 131104 | tf_op jit(solution)/shard_map/ppermute | solution.py:247
  26.4 1.9 %collective-permute-start.2 = (bf16[64,256]{1,0:T(8,128)(2,1)S(1)}, bf16[64,256]{1,0:T(8,128)(2,1)S(1)}, u32[]{:S(2)}, u32[]{:S(2)}) collective-permute-start(bf16[64,256]{1,0:T(8,128)(2,1)S(1)} %get-tuple-element.9), channel_id=1, source_target_pairs={{0,1},{1,2},{2,3},{3,0},{4,5},{5,6},{6,7},{7,4},{8,9},{9,10},{10,1... | collective-permute-start | bytes 98312 | tf_op jit(solution)/shard_map/ppermute | solution.py:253
  28.2 2.6 %collective-permute-start.3 = (bf16[64,256]{1,0:T(8,128)(2,1)S(1)}, bf16[64,256]{1,0:T(8,128)(2,1)S(1)}, u32[]{:S(2)}, u32[]{:S(2)}) collective-permute-start(bf16[64,256]{1,0:T(8,128)(2,1)S(1)} %get-tuple-element.11), channel_id=1, source_target_pairs={{0,2},{1,3},{2,0},{3,1},{4,6},{5,7},{6,4},{7,5},{8,10},{9,11},{10,... | collective-permute-start | bytes 98312 | tf_op jit(solution)/shard_map/ppermute | solution.py:253
  30.8 1.3 %collective-permute-start.4 = (bf16[64,256]{1,0:T(8,128)(2,1)S(1)}, bf16[64,256]{1,0:T(8,128)(2,1)S(1)}, u32[]{:S(2)}, u32[]{:S(2)}) collective-permute-start(bf16[64,256]{1,0:T(8,128)(2,1)S(1)} %get-tuple-element.10), channel_id=1, source_target_pairs={{0,3},{1,0},{2,1},{3,2},{4,7},{5,4},{6,5},{7,6},{8,11},{9,8},{10,9... | collective-permute-start | bytes 98312 | tf_op jit(solution)/shard_map/ppermute | solution.py:253
  32.2 0.4 %collective-permute-done.2 = bf16[64,256]{1,0:T(8,128)(2,1)S(1)} collective-permute-done((bf16[64,256]{1,0:T(8,128)(2,1)S(1)}, bf16[64,256]{1,0:T(8,128)(2,1)S(1)}, u32[]{:S(2)}, u32[]{:S(2)}) %collective-permute-start.2) | collective-permute-done | bytes 32800 | tf_op jit(solution)/shard_map/ppermute | solution.py:253
  32.6 0.6 %collective-permute-done.3 = bf16[64,256]{1,0:T(8,128)(2,1)S(1)} collective-permute-done((bf16[64,256]{1,0:T(8,128)(2,1)S(1)}, bf16[64,256]{1,0:T(8,128)(2,1)S(1)}, u32[]{:S(2)}, u32[]{:S(2)}) %collective-permute-start.3) | collective-permute-done | bytes 32800 | tf_op jit(solution)/shard_map/ppermute | solution.py:253
  33.2 1.6 %collective-permute-done.4 = bf16[64,256]{1,0:T(8,128)(2,1)S(1)} collective-permute-done((bf16[64,256]{1,0:T(8,128)(2,1)S(1)}, bf16[64,256]{1,0:T(8,128)(2,1)S(1)}, u32[]{:S(2)}, u32[]{:S(2)}) %collective-permute-start.4) | collective-permute-done | bytes 32800 | tf_op jit(solution)/shard_map/ppermute | solution.py:253
  34.8 0.6 %fusion.3 = f32[256,64]{0,1:T(8,128)} fusion(bf16[64,256]{1,0:T(8,128)(2,1)S(1)} %collective-permute-done.4, bf16[64,256]{1,0:T(8,128)(2,1)S(1)} %collective-permute-done.3, bf16[64,256]{1,0:T(8,128)(2,1)S(1)} %collective-permute-done.2, f32[4,64,256]{2,1,0:T(8,128)S(1)} %bitcast.29, s32[]{:T(128)S(6)} %select_n.52), kind=kLoop, calls=%fused_computation.7 | loop fusion | flops 98304 | bytes 229380 | tf_op jit(solution)/shard_map/transpose | solution.py:254
  (3 shorter events, 0.1 us)
Async XLA Ops:
  0.0 0.9 %copy-start = (bf16[16,3,1024]{2,0,1:T(8,128)(2,1)S(1)}, bf16[16,3,1024]{2,0,1:T(8,128)(2,1)}, u32[]{:S(2)}) copy-start(bf16[16,3,1024]{2,0,1:T(8,128)(2,1)} %param.4) | copy-start | bytes 294916
  0.9 0.7 %copy-start.1 = (s32[16,3]{0,1:T(4,128)S(1)}, s32[16,3]{0,1:T(4,128)}, u32[]{:S(2)}) copy-start(s32[16,3]{0,1:T(4,128)} %param.6) | copy-start | bytes 580
  1.6 0.7 %copy-start.2 = (s32[16,2]{0,1:T(2,128)S(1)}, s32[16,2]{0,1:T(2,128)}, u32[]{:S(2)}) copy-start(s32[16,2]{0,1:T(2,128)} %param.7) | copy-start | bytes 388
  17.9 1.7 %collective-permute-start = (bf16[2,256,256]{2,1,0:T(8,128)(2,1)S(1)}, bf16[2,256,256]{2,1,0:T(8,128)(2,1)S(1)}, u32[]{:S(2)}, u32[]{:S(2)}) collective-permute-start(bf16[2,256,256]{2,1,0:T(8,128)(2,1)S(1)} %get-tuple-element.8), channel_id=1, source_target_pairs={{0,4},{4,0},{8,12},{12,8},{1,5},{5,1},{9,13},{13,9},{2,6},{6,2},{1... | collective-permute-start | bytes 786440 | tf_op jit(solution)/shard_map/ppermute | solution.py:241
  19.6 6.7 %collective-permute-start.1 = (bf16[256,256]{1,0:T(8,128)(2,1)S(1)}, bf16[256,256]{1,0:T(8,128)(2,1)S(1)}, u32[]{:S(2)}, u32[]{:S(2)}) collective-permute-start(bf16[256,256]{1,0:T(8,128)(2,1)S(1)} %fusion), channel_id=1, source_target_pairs={{0,8},{4,12},{8,0},{12,4},{1,9},{5,13},{9,1},{13,5},{2,10},{6,14},... | collective-permute-start | bytes 393224 | tf_op jit(solution)/shard_map/ppermute | solution.py:247
  26.4 6.3 %collective-permute-start.2 = (bf16[64,256]{1,0:T(8,128)(2,1)S(1)}, bf16[64,256]{1,0:T(8,128)(2,1)S(1)}, u32[]{:S(2)}, u32[]{:S(2)}) collective-permute-start(bf16[64,256]{1,0:T(8,128)(2,1)S(1)} %get-tuple-element.9), channel_id=1, source_target_pairs={{0,1},{1,2},{2,3},{3,0},{4,5},{5,6},{6,7},{7,4},{8,9},{9,10},{10,1... | collective-permute-start | bytes 98312 | tf_op jit(solution)/shard_map/ppermute | solution.py:253
  28.2 4.9 %collective-permute-start.3 = (bf16[64,256]{1,0:T(8,128)(2,1)S(1)}, bf16[64,256]{1,0:T(8,128)(2,1)S(1)}, u32[]{:S(2)}, u32[]{:S(2)}) collective-permute-start(bf16[64,256]{1,0:T(8,128)(2,1)S(1)} %get-tuple-element.11), channel_id=1, source_target_pairs={{0,2},{1,3},{2,0},{3,1},{4,6},{5,7},{6,4},{7,5},{8,10},{9,11},{10,... | collective-permute-start | bytes 98312 | tf_op jit(solution)/shard_map/ppermute | solution.py:253
  30.8 3.9 %collective-permute-start.4 = (bf16[64,256]{1,0:T(8,128)(2,1)S(1)}, bf16[64,256]{1,0:T(8,128)(2,1)S(1)}, u32[]{:S(2)}, u32[]{:S(2)}) collective-permute-start(bf16[64,256]{1,0:T(8,128)(2,1)S(1)} %get-tuple-element.10), channel_id=1, source_target_pairs={{0,3},{1,0},{2,1},{3,2},{4,7},{5,4},{6,5},{7,6},{8,11},{9,8},{10,9... | collective-permute-start | bytes 98312 | tf_op jit(solution)/shard_map/ppermute | solution.py:253

commit v8 on v6

--- a/solution.py
+++ b/solution.py
@@ -36,14 +36,24 @@
     return pl.multiple_of(array - (region + 1) * size, LANES)
 
 
-def build_windows(shifted, factor, windows, channel, row, begins, size, groups, margin):
-    for n, begin in enumerate(begins):
-        half = jnp.broadcast_to(
-            shifted[pl.ds(channel, 1), pl.ds(begin, size + margin)], (8, size + margin))
+def read_rows(shifted, factor, channels, begins, size, margin):
+    rows = []
+    for channel in channels:
+        for begin in begins:
+            rows.append((
+                jnp.broadcast_to(
+                    shifted[pl.ds(channel, 1), pl.ds(begin, size + margin)], (8, size + margin)),
+                jnp.broadcast_to(factor[pl.ds(channel, 1), pl.ds(begin, size)], (GROUP, size)),
+            ))
+    return rows
+
+
+def build_windows(rows, windows, bases, regions, size, groups, margin):
+    for m, (half, scale) in enumerate(rows):
+        base, n = bases[m // regions], m % regions
         strip = jnp.concatenate(
             [pltpu.roll(half, b, 1, stride=1, stride_axis=0) for b in (0, 8)], axis=0
         ).astype(jnp.bfloat16)
-        scale = jnp.broadcast_to(factor[pl.ds(channel, 1), pl.ds(begin, size)], (GROUP, size))
         scale = scale.astype(jnp.bfloat16)
         for a in range(min(groups, LANES // GROUP)):
             deepest = list(range(a, groups, LANES // GROUP))[-1]
@@ -53,7 +63,7 @@
             rolled = rolled if a == 0 else pltpu.roll(rolled, a * GROUP, 1)
             for g in range(a, groups, LANES // GROUP):
                 lane = margin - (g - a) * GROUP - cut
-                windows[row + g * GROUP:row + (g + 1) * GROUP, n * size:(n + 1) * size] = (
+                windows[base + g * GROUP:base + (g + 1) * GROUP, n * size:(n + 1) * size] = (
                     rolled[:, lane:lane + size] * scale)
 
 
@@ -87,7 +97,7 @@
 def first_kernel(
     place_ref, moveouts_ref, uptime_ref, records_ref, templates_ref,
     send_ref, shifted, factor, banks_ref,
-    masked, loaded, bank, windows_a, windows_b, bank_a, bank_b, total, arrived, stored,
+    masked, loaded_a, loaded_b, bank, windows_a, windows_b, bank_a, bank_b, total, arrived, stored,
     *, window, batch,
 ):
     components, stations, length = records_ref.shape
@@ -100,12 +110,12 @@
     span = shifted.shape[1]
     lead = masked.shape[1] - length
 
-    def fetch(i):
-        at = pl.ds(i * batch, batch)
-        return pltpu.make_async_copy(templates_ref.at[at], loaded.at[at], arrived.at[i])
-
-    for i in range(batches):
-        fetch(i).start()
+    def fetch(i, which):
+        return pltpu.make_async_copy(
+            templates_ref.at[pl.ds(i * batch, batch)], (loaded_a, loaded_b)[which], arrived.at[which])
+
+    for i in range(min(batches, 2)):
+        fetch(i, i).start()
 
     masked[...] = jnp.zeros(masked.shape, jnp.float32)
     offsets = lax.broadcasted_iota(jnp.int32, (stations, LANES), 1)
@@ -155,24 +165,36 @@
     def store(i, turned, which):
         return pltpu.make_async_copy(turned, banks_ref.at[i], stored.at[which])
 
+    bases = [m * groups * GROUP for m in range(batch * components)]
+
     def build(i, windows, turned, which):
-        fetch(i).wait()
+        fetch(i, which).wait()
+        loaded = (loaded_a, loaded_b)[which]
+        rows = read_rows(
+            shifted, factor,
+            [j * stations + i * batch + u for u in range(batch) for j in range(components)],
+            begins, size, margin)
         for u in range(batch):
             for j in range(components):
-                values = loaded[i * batch + u, j].astype(jnp.float32)
+                values = loaded[u, j].astype(jnp.float32)
                 squares = jnp.sum(values * values, axis=0, keepdims=True)
                 unit = (values * lax.rsqrt(squares + 1e-06)).astype(jnp.bfloat16)
-                at = (u * components + j) * groups * GROUP
+                at = bases[u * components + j]
                 bank[at:at + window, :] = unit
         turned[...] = bank[...].T
-        for u in range(batch):
-            for j in range(components):
-                build_windows(
-                    shifted, factor, windows, j * stations + i * batch + u,
-                    (u * components + j) * groups * GROUP, begins, size, groups, margin)
+        build_windows(rows, windows, bases, count, size, groups, margin)
+
+    def pass_on(i, turned, which, more):
         store(i, turned, which).start()
+        if more is True:
+            fetch(i + 2, which).start()
+        elif more is not False:
+            @pl.when(more)
+            def _():
+                fetch(i + 2, which).start()
 
     build(0, windows_a, bank_a, 0)
+    pass_on(0, bank_a, 0, batches > 2)
 
     def two_batches(i, carry):
         @pl.when(i > 0)
@@ -180,9 +202,11 @@
             store(2 * i - 1, bank_b, 1).wait()
         build(2 * i + 1, windows_b, bank_b, 1)
         multiply(total, windows_a, [bank_a], width)
+        pass_on(2 * i + 1, bank_b, 1, 2 * i + 3 < batches)
         store(2 * i, bank_a, 0).wait()
         build(2 * i + 2, windows_a, bank_a, 0)
         multiply(total, windows_b, [bank_b], width)
+        pass_on(2 * i + 2, bank_a, 0, 2 * i + 4 < batches)
         return carry
 
     if batches > 2:
@@ -192,6 +216,7 @@
             store(batches - 3, bank_b, 1).wait()
         build(batches - 1, windows_b, bank_b, 1)
         multiply(total, windows_a, [bank_a], width)
+        pass_on(batches - 1, bank_b, 1, False)
         multiply(total, windows_b, [bank_b], width)
         store(batches - 2, bank_a, 0).wait()
         store(batches - 1, bank_b, 1).wait()
@@ -239,45 +264,22 @@
         begins = [mirrored(length, 2 * ((x + n) % hops) + core, size) for n in range(1, hops)]
     width = min(2 * LANES, size)
 
-    def build(p, windows):
-        for k in range(slabs):
-            for u in range(batch):
-                for j in range(components):
-                    build_windows(
-                        shifted, factor, windows,
-                        j * stations + (p * slabs + k) * batch + u,
-                        k * slab + (u * components + j) * groups * GROUP,
-                        begins, size, groups, margin)
-
-    def product(p, windows):
-        multiply(total, windows, [loaded.at[p * slabs + k] for k in range(slabs)], width)
-
-    def ready(p):
+    places = [(k, u, j) for k in range(slabs) for u in range(batch) for j in range(components)]
+    bases = [k * slab + (u * components + j) * groups * GROUP for k, u, j in places]
+
+    def read(p):
+        return read_rows(
+            shifted, factor, [j * stations + (p * slabs + k) * batch + u for k, u, j in places],
+            begins, size, margin)
+
+    build_windows(read(0), windows_a, bases, len(begins), size, groups, margin)
+    for p in range(phases):
+        now, later = (windows_a, windows_b) if p % 2 == 0 else (windows_b, windows_a)
         for k in range(slabs):
             fetch(p * slabs + k).wait()
-
-    build(0, windows_a)
-
-    def two_phases(i, carry):
-        ready(2 * i)
-        build(2 * i + 1, windows_b)
-        product(2 * i, windows_a)
-        ready(2 * i + 1)
-        build(2 * i + 2, windows_a)
-        product(2 * i + 1, windows_b)
-        return carry
-
-    if phases > 2:
-        lax.fori_loop(0, (phases - 1) // 2, two_phases, 0)
-    if phases % 2 == 0:
-        ready(phases - 2)
-        build(phases - 1, windows_b)
-        product(phases - 2, windows_a)
-        ready(phases - 1)
-        product(phases - 1, windows_b)
-    else:
-        ready(phases - 1)
-        product(phases - 1, windows_a)
+        if p + 1 < phases:
+            build_windows(read(p + 1), later, bases, len(begins), size, groups, margin)
+        multiply(total, now, [loaded.at[p * slabs + k] for k in range(slabs)], width)
     if own:
         write_regions(total, out_ref, lambda r, h: came_ref[
             x, r:r + LANES, h:h + LANES].astype(jnp.float32))
@@ -309,14 +311,15 @@
         out_specs=[VECTORS, VECTORS, VECTORS, FAR],
         scratch_shapes=[
             pltpu.VMEM((rows, length + margin + LANES + up(MAXMO, LANES)), jnp.float32),
-            pltpu.VMEM(templates.shape, templates.dtype),
+            pltpu.VMEM((batch,) + templates.shape[1:], templates.dtype),
+            pltpu.VMEM((batch,) + templates.shape[1:], templates.dtype),
             pltpu.VMEM((depth, bank_size), jnp.bfloat16),
             pltpu.VMEM((depth, hops * region), jnp.bfloat16),
             pltpu.VMEM((depth, hops * region), jnp.bfloat16),
             pltpu.VMEM((bank_size, depth), jnp.bfloat16),
             pltpu.VMEM((bank_size, depth), jnp.bfloat16),
             pltpu.VMEM((bank_size, hops * region), jnp.float32),
-            pltpu.SemaphoreType.DMA((stations // batch,)),
+            pltpu.SemaphoreType.DMA((2,)),
             pltpu.SemaphoreType.DMA((2,)),
         ],
         out_shape=[

time: 46.8 us -> 46.7 us (level)
  no operation moved by 1% of the time
where the time goes in v8:
time: 46.7 us; the launch traced here: 46.4 us
  Pallas kernels  31.2 us (67%)
  starting transfers between devices  7.77 us (17%)
  waiting for transfers between devices  4.71 us (10%)
  other arithmetic  2.7 us (6%)
    pallas_call x1, Pallas kernels, first_part(): pl.pallas_call(functools.partial(first_kernel, window=window, batch=batch...  16.5 us
    pallas_call x2, Pallas kernels, next_part(): pl.pallas_call(functools.partial(next_kernel, components=components, wind...  14.7 us
    ppermute x3, waiting for transfers between devices, body(): lax.ppermute(block.astype(jnp.bfloat16), 'chan', perm).astype(jnp.float32)  4.7 us
    ppermute x3, starting transfers between devices, body(): lax.ppermute(block.astype(jnp.bfloat16), 'chan', perm).astype(jnp.float32)  4.67 us
    ppermute x1, starting transfers between devices, body(): arriving.append(lax.ppermute(piece, 'tm', perm))  2.59 us
    convert_element_type x1, other arithmetic, body(): piece = (others[step - 1] + piece.astype(jnp.float32)).astype(jnp.bfloat16)  1.08 us
    add x1, other arithmetic, body(): result = result + piece.astype(jnp.float32)  0.98 us
  transfers between devices with their start and end apart: 5, of which 3 were waited for; matrix products, arithmetic and copies ran while one was open for 0% of the time, Pallas kernels for 32%

profile of v8, /device:TPU:0, one launch (start us, length us, event | category | flops | bytes accessed | tf_op | source)
XLA Modules:
  0.0 46.4 jit_solution(4493144519053612739)
XLA Ops:
  0.0 16.5 %other_core.1 = (bf16[2,256,256]{2,1,0:T(8,128)(2,1)}, f32[48,1280]{1,0:T(8,128)}, f32[48,1024]{1,0:T(8,128)}, bf16[8,256,1280]{2,1,0:T(8,128)(2,1)}) custom-call(s32[1]{0:T(128)} %bitcast.place_ref, s32[3,16]{1,0:T(4,128)} %bitcast.28, s32[2,16]{1,0:T(2,128)} %bitcast.29, bf16[3,16,1024]{2,1,0:T(8,128)(2,1)} %bitcast.27, bf16[16,3,200,256]{3,2,1,0:T(8,128)(2,1)} %templates_ref.1), custom_call_target="tpu_custom_call" | custom-call | flops 2516582400 | bytes 9830400 | tf_op jit(solution)/shard_map/other_core/pallas_call | solution.py:308
  16.5 0.5 %collective-permute-start = (bf16[2,256,256]{2,1,0:T(8,128)(2,1)}, bf16[2,256,256]{2,1,0:T(8,128)(2,1)S(1)}, u32[]{:S(2)}, u32[]{:S(2)}) collective-permute-start(bf16[2,256,256]{2,1,0:T(8,128)(2,1)} %get-tuple-element.12), channel_id=1, source_target_pairs={{0,4},{4,0},{8,12},{12,8},{1,5},{5,1},{9,13},{13,9},{2,6},{6,2},{1... | collective-permute-start | bytes 786440 | tf_op jit(solution)/shard_map/ppermute | solution.py:375
  17.0 7.3 %other_chips.1 = f32[1,256,256]{2,1,0:T(8,128)} custom-call(s32[1]{0:T(128)} %bitcast.place_ref, f32[48,1280]{1,0:T(8,128)} %get-tuple-element.9.shifted, f32[48,1024]{1,0:T(8,128)} %get-tuple-element.10.factor, bf16[8,256,1280]{2,1,0:T(8,128)(2,1)} %get-tuple-element.11.banks_ref), custom_call_target="tpu_custom_call" | custom-call | flops 1258291200 | bytes 5242880 | tf_op jit(solution)/shard_map/other_chips/pallas_call | solution.py:343
  24.3 0.0 collective-permute-done.refs_0_
  24.3 0.0 copy-start
  24.3 1.1 %fusion = bf16[256,256]{1,0:T(8,128)(2,1)S(1)} fusion(f32[1,256,256]{2,1,0:T(8,128)} %other_chips.1, bf16[2,256,256]{2,1,0:T(8,128)(2,1)S(1)} %collective-permute-done.refs_0_, s32[]{:T(128)S(6)} %select_n.42), kind=kLoop, calls=%fused_computation.2 | loop fusion | flops 196608 | bytes 524292 | tf_op jit(solution)/shard_map/convert_element_type | solution.py:382
  25.4 2.6 %collective-permute-start.1 = (bf16[256,256]{1,0:T(8,128)(2,1)S(1)}, bf16[256,256]{1,0:T(8,128)(2,1)S(1)}, u32[]{:S(2)}, u32[]{:S(2)}) collective-permute-start(bf16[256,256]{1,0:T(8,128)(2,1)S(1)} %fusion), channel_id=1, source_target_pairs={{0,8},{4,12},{8,0},{12,4},{1,9},{5,13},{9,1},{13,5},{2,10},{6,14},... | collective-permute-start | bytes 393224 | tf_op jit(solution)/shard_map/ppermute | solution.py:384
  28.0 0.0 copy-done
  28.0 7.4 %own_region.1 = f32[1,256,256]{2,1,0:T(8,128)} custom-call(s32[1]{0:T(128)} %bitcast.place_ref, f32[48,1280]{1,0:T(8,128)} %get-tuple-element.9.shifted, f32[48,1024]{1,0:T(8,128)} %get-tuple-element.10.factor, bf16[8,256,1280]{2,1,0:T(8,128)(2,1)} %get-tuple-element.11.banks_ref, bf16[2,256,256]{2,1,0:T(8,128)(2,1)} %copy-done), custom_call_target="tpu_custom_call" | custom-call | flops 1258291200 | bytes 5242880 | tf_op jit(solution)/shard_map/own_region/pallas_call | solution.py:343
  35.4 0.0 collective-permute-done.1
  35.4 1.0 %bitcast_add_fusion = f32[256,256]{1,0:T(8,128)S(1)} fusion(f32[1,256,256]{2,1,0:T(8,128)} %own_region.1, bf16[256,256]{1,0:T(8,128)(2,1)S(1)} %collective-permute-done.1), kind=kLoop, calls=%fused_computation | loop fusion | flops 131072 | bytes 655360 | tf_op jit(solution)/shard_map/add | solution.py:388
  36.4 3.7 %collective-permute-start.4 = (bf16[64,256]{1,0:T(8,128)(2,1)S(1)}, bf16[64,256]{1,0:T(8,128)(2,1)S(1)}, u32[]{:S(2)}, u32[]{:S(2)}) collective-permute-start(bf16[64,256]{1,0:T(8,128)(2,1)S(1)} %get-tuple-element.14), channel_id=1, source_target_pairs={{0,3},{1,0},{2,1},{3,2},{4,7},{5,4},{6,5},{7,6},{8,11},{9,8},{10,9... | collective-permute-start | bytes 98312 | tf_op jit(solution)/shard_map/ppermute | solution.py:394
  40.1 0.0 collective-permute-start.3
  40.1 1.0 %collective-permute-start.2 = (bf16[64,256]{1,0:T(8,128)(2,1)S(1)}, bf16[64,256]{1,0:T(8,128)(2,1)S(1)}, u32[]{:S(2)}, u32[]{:S(2)}) collective-permute-start(bf16[64,256]{1,0:T(8,128)(2,1)S(1)} %get-tuple-element.13), channel_id=1, source_target_pairs={{0,1},{1,2},{2,3},{3,0},{4,5},{5,6},{6,7},{7,4},{8,9},{9,10},{10,1... | collective-permute-start | bytes 98312 | tf_op jit(solution)/shard_map/ppermute | solution.py:394
  41.1 0.7 %collective-permute-done.4 = bf16[64,256]{1,0:T(8,128)(2,1)S(1)} collective-permute-done((bf16[64,256]{1,0:T(8,128)(2,1)S(1)}, bf16[64,256]{1,0:T(8,128)(2,1)S(1)}, u32[]{:S(2)}, u32[]{:S(2)}) %collective-permute-start.4) | collective-permute-done | bytes 32800 | tf_op jit(solution)/shard_map/ppermute | solution.py:394
  41.8 3.3 %collective-permute-done.3 = bf16[64,256]{1,0:T(8,128)(2,1)S(1)} collective-permute-done((bf16[64,256]{1,0:T(8,128)(2,1)S(1)}, bf16[64,256]{1,0:T(8,128)(2,1)S(1)}, u32[]{:S(2)}, u32[]{:S(2)}) %collective-permute-start.3) | collective-permute-done | bytes 32800 | tf_op jit(solution)/shard_map/ppermute | solution.py:394
  45.1 0.7 %collective-permute-done.2 = bf16[64,256]{1,0:T(8,128)(2,1)S(1)} collective-permute-done((bf16[64,256]{1,0:T(8,128)(2,1)S(1)}, bf16[64,256]{1,0:T(8,128)(2,1)S(1)}, u32[]{:S(2)}, u32[]{:S(2)}) %collective-permute-start.2) | collective-permute-done | bytes 32800 | tf_op jit(solution)/shard_map/ppermute | solution.py:394
  45.8 0.6 %fusion.3 = f32[256,64]{0,1:T(8,128)} fusion(bf16[64,256]{1,0:T(8,128)(2,1)S(1)} %collective-permute-done.4, bf16[64,256]{1,0:T(8,128)(2,1)S(1)} %collective-permute-done.3, bf16[64,256]{1,0:T(8,128)(2,1)S(1)} %collective-permute-done.2, f32[4,64,256]{2,1,0:T(8,128)S(1)} %bitcast.26, s32[]{:T(128)S(6)} %select_n.43), kind=kLoop, calls=%fused_computation.6 | loop fusion | flops 98304 | bytes 229380 | tf_op jit(solution)/shard_map/transpose | solution.py:395
  (1 shorter events, 0.0 us)
Async XLA Ops:
  16.5 7.8 %collective-permute-start = (bf16[2,256,256]{2,1,0:T(8,128)(2,1)}, bf16[2,256,256]{2,1,0:T(8,128)(2,1)S(1)}, u32[]{:S(2)}, u32[]{:S(2)}) collective-permute-start(bf16[2,256,256]{2,1,0:T(8,128)(2,1)} %get-tuple-element.12), channel_id=1, source_target_pairs={{0,4},{4,0},{8,12},{12,8},{1,5},{5,1},{9,13},{13,9},{2,6},{6,2},{1... | collective-permute-start | bytes 786440 | tf_op jit(solution)/shard_map/ppermute | solution.py:375
  24.3 3.7 %copy-start = (bf16[2,256,256]{2,1,0:T(8,128)(2,1)}, bf16[2,256,256]{2,1,0:T(8,128)(2,1)S(1)}, u32[]{:S(2)}) copy-start(bf16[2,256,256]{2,1,0:T(8,128)(2,1)S(1)} %collective-permute-done.refs_0_) | copy-start | bytes 786436
  25.4 10.0 %collective-permute-start.1 = (bf16[256,256]{1,0:T(8,128)(2,1)S(1)}, bf16[256,256]{1,0:T(8,128)(2,1)S(1)}, u32[]{:S(2)}, u32[]{:S(2)}) collective-permute-start(bf16[256,256]{1,0:T(8,128)(2,1)S(1)} %fusion), channel_id=1, source_target_pairs={{0,8},{4,12},{8,0},{12,4},{1,9},{5,13},{9,1},{13,5},{2,10},{6,14},... | collective-permute-start | bytes 393224 | tf_op jit(solution)/shard_map/ppermute | solution.py:384
  36.4 5.3 %collective-permute-start.4 = (bf16[64,256]{1,0:T(8,128)(2,1)S(1)}, bf16[64,256]{1,0:T(8,128)(2,1)S(1)}, u32[]{:S(2)}, u32[]{:S(2)}) collective-permute-start(bf16[64,256]{1,0:T(8,128)(2,1)S(1)} %get-tuple-element.14), channel_id=1, source_target_pairs={{0,3},{1,0},{2,1},{3,2},{4,7},{5,4},{6,5},{7,6},{8,11},{9,8},{10,9... | collective-permute-start | bytes 98312 | tf_op jit(solution)/shard_map/ppermute | solution.py:394
  40.1 5.0 %collective-permute-start.3 = (bf16[64,256]{1,0:T(8,128)(2,1)S(1)}, bf16[64,256]{1,0:T(8,128)(2,1)S(1)}, u32[]{:S(2)}, u32[]{:S(2)}) collective-permute-start(bf16[64,256]{1,0:T(8,128)(2,1)S(1)} %get-tuple-element.15), channel_id=1, source_target_pairs={{0,2},{1,3},{2,0},{3,1},{4,6},{5,7},{6,4},{7,5},{8,10},{9,11},{10,... | collective-permute-start | bytes 98312 | tf_op jit(solution)/shard_map/ppermute | solution.py:394
  40.1 5.7 %collective-permute-start.2 = (bf16[64,256]{1,0:T(8,128)(2,1)S(1)}, bf16[64,256]{1,0:T(8,128)(2,1)S(1)}, u32[]{:S(2)}, u32[]{:S(2)}) collective-permute-start(bf16[64,256]{1,0:T(8,128)(2,1)S(1)} %get-tuple-element.13), channel_id=1, source_target_pairs={{0,1},{1,2},{2,3},{3,0},{4,5},{5,6},{6,7},{7,4},{8,9},{9,10},{10,1... | collective-permute-start | bytes 98312 | tf_op jit(solution)/shard_map/ppermute | solution.py:394

commit v9 on v7

--- a/solution.py
+++ b/solution.py
@@ -33,11 +33,9 @@
 
 
 def correlate_kernel(
-    core_ref, moveouts_ref, uptime_ref, records_ref, templates_ref,
-    send_ref, keep_ref,
-    masked, shifted, factor, loaded, bank, windows_a, windows_b, bank_a, bank_b, total, arrived,
-    *, window,
+    place_ref, moveouts_ref, uptime_ref, records_ref, templates_ref, *refs, window,
 ):
+    *out_refs, masked, shifted, factor, loaded, bank, windows_a, windows_b, bank_a, bank_b, total, arrived = refs
     components, stations, length = records_ref.shape
     block_count = uptime_ref.shape[0]
     rows = masked.shape[0]
@@ -86,8 +84,8 @@
             masked[j * stations:(j + 1) * stations, pl.ds(to, LANES)] = values[:stations]
         return carry
 
-    lax.fori_loop(0, length // LANES, mask_tile, 0)
-    burst = 4 if stations % 4 == 0 else 1
+    lax.fori_loop(0, length // LANES, mask_tile, 0, unroll=length // LANES <= 8)
+    burst = stations
 
     def shift_some(i, carry):
         shifts = []
@@ -104,7 +102,7 @@
         return carry
 
     lax.fori_loop(0, stations // burst, shift_some, 0)
-    chunk = rows // 2 if rows % 16 == 0 else 8
+    chunk = rows
 
     def energy_some(i, carry):
         at = pl.ds(pl.multiple_of(i * chunk, 8), chunk)
@@ -173,41 +171,35 @@
 
     lax.fori_loop(0, stations // 2 + 1, two_stations, 0)
 
-    core = core_ref[0]
-    hops, region = keep_ref.shape[0], keep_ref.shape[1]
+    size = out_refs[0].shape[0]
     flip = LANES - 1 - lax.broadcasted_iota(jnp.int32, (LANES, LANES), 1)
-
-    def ordered(begin, h):
-        at = pl.multiple_of(length - LANES - begin, LANES)
-        block = total[h:h + LANES, pl.ds(at, LANES)]
-        return jnp.take_along_axis(block, flip, axis=1).T
-
-    def write(i, carry):
-        x = i // (region // LANES)
-        r = pl.multiple_of(i % (region // LANES) * LANES, LANES)
-        own = (2 * x + core) * region + r
-        other = (2 * x + 1 - core) * region + r
-        for h in range(0, total.shape[0], LANES):
-            keep_ref[x, pl.ds(r, LANES), h:h + LANES] = ordered(own, h)
-            send_ref[x, pl.ds(r, LANES), h:h + LANES] = ordered(other, h).astype(send_ref.dtype)
-        return carry
-
-    lax.fori_loop(0, hops * (region // LANES), write, 0)
-
-
-def correlate(core, records, templates, moveouts, uptime, hops):
+    for step, out_ref in enumerate(out_refs, 1):
+        region = partner(place_ref[0], step % len(out_refs), len(out_refs))
+        for r in range(0, size, LANES):
+            at = pl.multiple_of(length - LANES - region * size - r, LANES)
+            for h in range(0, total.shape[0], LANES):
+                block = total[h:h + LANES, pl.ds(at, LANES)]
+                block = jnp.take_along_axis(block, flip, axis=1).T
+                out_ref[r:r + LANES, h:h + LANES] = block.astype(out_ref.dtype)
+
+
+def partner(place, step, count):
+    return place ^ step if count & (count - 1) == 0 else (place + step) % count
+
+
+def correlate(place, records, templates, moveouts, uptime, count):
     components, stations, length = records.shape
     window, bank_size = templates.shape[2:]
     margin = up(window, LANES)
     rows = up(stations * components, 8)
-    region = length // (2 * hops)
+    region = length // count
     depth = up(components * up(window, GROUP), LANES)
     scalars = pl.BlockSpec(memory_space=pltpu.SMEM)
     vectors = pl.BlockSpec(memory_space=pltpu.VMEM)
     return pl.pallas_call(
         functools.partial(correlate_kernel, window=window),
         in_specs=[scalars, scalars, scalars, vectors, pl.BlockSpec(memory_space=pl.ANY)],
-        out_specs=[vectors, vectors],
+        out_specs=[vectors] * count,
         scratch_shapes=[
             pltpu.VMEM((rows, length + margin + LANES + up(MAXMO, LANES)), jnp.float32),
             pltpu.VMEM((rows, length + margin), jnp.float32),
@@ -221,30 +213,22 @@
             pltpu.VMEM((bank_size, length), jnp.float32),
             pltpu.SemaphoreType.DMA((stations,)),
         ],
-        out_shape=[
-            jax.ShapeDtypeStruct((hops, region, bank_size), jnp.bfloat16),
-            jax.ShapeDtypeStruct((hops, region, bank_size), jnp.float32),
-        ],
-        compiler_params=pltpu.CompilerParams(vmem_limit_bytes=52 * 2**20),
+        out_shape=[jax.ShapeDtypeStruct((region, bank_size), jnp.bfloat16)] * (count - 1)
+        + [jax.ShapeDtypeStruct((region, bank_size), jnp.float32)],
+        compiler_params=pltpu.CompilerParams(vmem_limit_bytes=58 * 2**20),
         name="correlate",
-    )(core, moveouts, uptime, records, templates)
+    )(place, moveouts, uptime, records, templates)
 
 
 def body(records, templates, moveouts, uptime):
     tm, chan = lax.axis_size("tm"), lax.axis_size("chan")
-    hops = tm // 2
     t, z = lax.axis_index("tm"), lax.axis_index("chan")
-    x, core = t // 2, t % 2
-    send, keep = correlate(
-        core.reshape(1), records.transpose(1, 0, 2), templates, moveouts.T, uptime.T, hops
+    *sent, result = correlate(
+        t.reshape(1), records.transpose(1, 0, 2), templates, moveouts.T, uptime.T, tm
     )
-    got = lax.ppermute(send, "tm", [(i, i ^ 1) for i in range(tm)])
-    mine = keep + got.astype(jnp.float32)
-    result = lax.dynamic_index_in_dim(mine, x, 0, keepdims=False)
-    for step in range(1, hops):
-        block = lax.dynamic_index_in_dim(mine, (x + step) % hops, 0, keepdims=False)
-        perm = [(i, ((i // 2 + step) % hops) * 2 + i % 2) for i in range(tm)]
-        result = result + lax.ppermute(block.astype(jnp.bfloat16), "tm", perm).astype(jnp.float32)
+    for step in range(tm - 1, 0, -1):
+        perm = [(i, partner(i, step, tm)) for i in range(tm)]
+        result = result + lax.ppermute(sent[step - 1], "tm", perm).astype(jnp.float32)
     mine = result.reshape(chan, result.shape[0] // chan, result.shape[1])
     result = lax.dynamic_index_in_dim(mine, z, 0, keepdims=False)
     for step in range(1, chan):

time: 35.6 us -> 35.8 us (level)
  waiting for transfers between devices: 7.53 us -> 11.5 us
  local copies, waits for them, and re-layouts: 2.3 us -> 0.02 us
  starting transfers between devices: 9.2 us -> 7.88 us
  Pallas kernels: 15.6 us -> 14.6 us
  other arithmetic: 0.72 us -> 1.65 us
    unnamed x6 -> x0, local copies, waits for them, and re-layouts: 2.25 us -> none
    ppermute x3, waiting for transfers between devices: 2.57 us -> 4.7 us  [body(): lax.ppermute(block.astype(jnp.bfloat16), 'chan', perm).astype(jnp.float32)]
    ppermute x2 -> x3, waiting for transfers between devices: 4.96 us -> 6.78 us  [body(): lax.ppermute(sent[step - 1], 'tm', perm).astype(jnp.float32)]
    ppermute x3, starting transfers between devices: 5.8 us -> 4.77 us  [body(): lax.ppermute(block.astype(jnp.bfloat16), 'chan', perm).astype(jnp.float32)]
    pallas_call x1, Pallas kernels: 15.6 us -> 14.6 us  [correlate(): pl.pallas_call(functools.partial(correlate_kernel, window=window), in_spe...]
    add x2 -> x1, other arithmetic: 0.08 us -> 1 us  [body(): result + lax.ppermute(sent[step - 1], 'tm', perm).astype(jnp.float32)]
    ppermute x2 -> x3, starting transfers between devices: 3.39 us -> 3.11 us  [body(): lax.ppermute(sent[step - 1], 'tm', perm).astype(jnp.float32)]
  transfers between devices with their start and end apart: 5 -> 6, of which waited for: 5 -> 5; matrix products, arithmetic and copies ran while one was open for 0% -> 0% of each run, Pallas kernels for 0% -> 0%
where the time goes in v9:
time: 35.8 us; the launch traced here: 35.6 us
  Pallas kernels  14.6 us (41%)
  waiting for transfers between devices  11.5 us (32%)
  starting transfers between devices  7.88 us (22%)
  other arithmetic  1.65 us (5%)
    pallas_call x1, Pallas kernels, correlate(): pl.pallas_call(functools.partial(correlate_kernel, window=window), in_spe...  14.6 us
    ppermute x3, waiting for transfers between devices, body(): lax.ppermute(sent[step - 1], 'tm', perm).astype(jnp.float32)  6.78 us
    ppermute x3, starting transfers between devices, body(): lax.ppermute(block.astype(jnp.bfloat16), 'chan', perm).astype(jnp.float32)  4.77 us
    ppermute x3, waiting for transfers between devices, body(): lax.ppermute(block.astype(jnp.bfloat16), 'chan', perm).astype(jnp.float32)  4.7 us
    ppermute x3, starting transfers between devices, body(): lax.ppermute(sent[step - 1], 'tm', perm).astype(jnp.float32)  3.11 us
    add x1, other arithmetic, body(): result + lax.ppermute(sent[step - 1], 'tm', perm).astype(jnp.float32)  1 us
  transfers between devices with their start and end apart: 6, of which 5 were waited for; matrix products, arithmetic and copies ran while one was open for 0% of the time, Pallas kernels for 0%

profile of v9, /device:TPU:0, one launch (start us, length us, event | category | flops | bytes accessed | tf_op | source)
XLA Modules:
  0.0 35.6 jit_solution(3218484550284911578)
XLA Ops:
  0.0 14.6 %correlate.1 = (bf16[256,256]{1,0:T(8,128)(2,1)}, bf16[256,256]{1,0:T(8,128)(2,1)}, bf16[256,256]{1,0:T(8,128)(2,1)}, f32[256,256]{1,0:T(8,128)}) custom-call(s32[1]{0:T(128)} %bitcast.place_ref, s32[3,16]{1,0:T(4,128)} %bitcast.24, s32[2,16]{1,0:T(2,128)} %bitcast.25, bf16[3,16,1024]{2,1,0:T(8,128)(2,1)} %bitcast.23, bf16[16,3,200,256]{3,2,1,0:T(8,128)(2,1)} %templates_ref.1), custom_call_target="tpu_custom_call" | custom-call | tf_op jit(solution)/shard_map/correlate/pallas_call | solution.py:199
  14.6 0.5 %collective-permute-start.2 = (bf16[256,256]{1,0:T(8,128)(2,1)}, bf16[256,256]{1,0:T(8,128)(2,1)S(1)}, u32[]{:S(2)}, u32[]{:S(2)}) collective-permute-start(bf16[256,256]{1,0:T(8,128)(2,1)} %get-tuple-element.12), channel_id=1, source_target_pairs={{0,4},{4,0},{8,12},{12,8},{1,5},{5,1},{9,13},{13,9},{2,6},{6,2},{1... | collective-permute-start | bytes 393224 | tf_op jit(solution)/shard_map/ppermute | solution.py:231
  15.1 2.6 %collective-permute-start.1 = (bf16[256,256]{1,0:T(8,128)(2,1)}, bf16[256,256]{1,0:T(8,128)(2,1)S(1)}, u32[]{:S(2)}, u32[]{:S(2)}) collective-permute-start(bf16[256,256]{1,0:T(8,128)(2,1)} %get-tuple-element.11), channel_id=1, source_target_pairs={{0,8},{4,12},{8,0},{12,4},{1,9},{5,13},{9,1},{13,5},{2,10},{6,14},... | collective-permute-start | bytes 393224 | tf_op jit(solution)/shard_map/ppermute | solution.py:231
  17.6 0.1 collective-permute-start
  17.7 0.0 collective-permute-done.2
  17.7 4.5 %collective-permute-done.1 = bf16[256,256]{1,0:T(8,128)(2,1)S(1)} collective-permute-done((bf16[256,256]{1,0:T(8,128)(2,1)}, bf16[256,256]{1,0:T(8,128)(2,1)S(1)}, u32[]{:S(2)}, u32[]{:S(2)}) %collective-permute-start.1) | collective-permute-done | bytes 131104 | tf_op jit(solution)/shard_map/ppermute | solution.py:231
  22.2 2.3 %collective-permute-done = bf16[256,256]{1,0:T(8,128)(2,1)S(1)} collective-permute-done((bf16[256,256]{1,0:T(8,128)(2,1)}, bf16[256,256]{1,0:T(8,128)(2,1)S(1)}, u32[]{:S(2)}, u32[]{:S(2)}) %collective-permute-start) | collective-permute-done | bytes 131104 | tf_op jit(solution)/shard_map/ppermute | solution.py:231
  24.5 1.0 %convert_add_fusion = f32[256,256]{1,0:T(8,128)S(1)} fusion(bf16[256,256]{1,0:T(8,128)(2,1)S(1)} %collective-permute-done.2, bf16[256,256]{1,0:T(8,128)(2,1)S(1)} %collective-permute-done.1, f32[256,256]{1,0:T(8,128)} %get-tuple-element.9, bf16[256,256]{1,0:T(8,128)(2,1)S(1)} %collective-permute-done), kind=kLoop, calls=%fused_computation | loop fusion | flops 393216 | bytes 917504 | tf_op jit(solution)/shard_map/add | solution.py:231
  25.5 3.8 %collective-permute-start.5 = (bf16[64,256]{1,0:T(8,128)(2,1)S(1)}, bf16[64,256]{1,0:T(8,128)(2,1)S(1)}, u32[]{:S(2)}, u32[]{:S(2)}) collective-permute-start(bf16[64,256]{1,0:T(8,128)(2,1)S(1)} %get-tuple-element.14), channel_id=1, source_target_pairs={{0,3},{1,0},{2,1},{3,2},{4,7},{5,4},{6,5},{7,6},{8,11},{9,8},{10,9... | collective-permute-start | bytes 98312 | tf_op jit(solution)/shard_map/ppermute | solution.py:237
  29.3 0.0 collective-permute-start.4
  29.3 1.0 %collective-permute-start.3 = (bf16[64,256]{1,0:T(8,128)(2,1)S(1)}, bf16[64,256]{1,0:T(8,128)(2,1)S(1)}, u32[]{:S(2)}, u32[]{:S(2)}) collective-permute-start(bf16[64,256]{1,0:T(8,128)(2,1)S(1)} %get-tuple-element.13), channel_id=1, source_target_pairs={{0,1},{1,2},{2,3},{3,0},{4,5},{5,6},{6,7},{7,4},{8,9},{9,10},{10,1... | collective-permute-start | bytes 98312 | tf_op jit(solution)/shard_map/ppermute | solution.py:237
  30.3 0.7 %collective-permute-done.5 = bf16[64,256]{1,0:T(8,128)(2,1)S(1)} collective-permute-done((bf16[64,256]{1,0:T(8,128)(2,1)S(1)}, bf16[64,256]{1,0:T(8,128)(2,1)S(1)}, u32[]{:S(2)}, u32[]{:S(2)}) %collective-permute-start.5) | collective-permute-done | bytes 32800 | tf_op jit(solution)/shard_map/ppermute | solution.py:237
  31.0 3.4 %collective-permute-done.4 = bf16[64,256]{1,0:T(8,128)(2,1)S(1)} collective-permute-done((bf16[64,256]{1,0:T(8,128)(2,1)S(1)}, bf16[64,256]{1,0:T(8,128)(2,1)S(1)}, u32[]{:S(2)}, u32[]{:S(2)}) %collective-permute-start.4) | collective-permute-done | bytes 32800 | tf_op jit(solution)/shard_map/ppermute | solution.py:237
  34.4 0.6 %collective-permute-done.3 = bf16[64,256]{1,0:T(8,128)(2,1)S(1)} collective-permute-done((bf16[64,256]{1,0:T(8,128)(2,1)S(1)}, bf16[64,256]{1,0:T(8,128)(2,1)S(1)}, u32[]{:S(2)}, u32[]{:S(2)}) %collective-permute-start.3) | collective-permute-done | bytes 32800 | tf_op jit(solution)/shard_map/ppermute | solution.py:237
  35.0 0.6 %fusion.2 = f32[256,64]{0,1:T(8,128)} fusion(bf16[64,256]{1,0:T(8,128)(2,1)S(1)} %collective-permute-done.5, bf16[64,256]{1,0:T(8,128)(2,1)S(1)} %collective-permute-done.4, bf16[64,256]{1,0:T(8,128)(2,1)S(1)} %collective-permute-done.3, f32[4,64,256]{2,1,0:T(8,128)S(1)} %bitcast.22, s32[]{:T(128)S(6)} %select_n.28), kind=kLoop, calls=%fused_computation.4 | loop fusion | flops 98304 | bytes 229380 | tf_op jit(solution)/shard_map/transpose | solution.py:238
  (1 shorter events, 0.0 us)
Async XLA Ops:
  14.6 3.1 %collective-permute-start.2 = (bf16[256,256]{1,0:T(8,128)(2,1)}, bf16[256,256]{1,0:T(8,128)(2,1)S(1)}, u32[]{:S(2)}, u32[]{:S(2)}) collective-permute-start(bf16[256,256]{1,0:T(8,128)(2,1)} %get-tuple-element.12), channel_id=1, source_target_pairs={{0,4},{4,0},{8,12},{12,8},{1,5},{5,1},{9,13},{13,9},{2,6},{6,2},{1... | collective-permute-start | bytes 393224 | tf_op jit(solution)/shard_map/ppermute | solution.py:231
  15.1 7.1 %collective-permute-start.1 = (bf16[256,256]{1,0:T(8,128)(2,1)}, bf16[256,256]{1,0:T(8,128)(2,1)S(1)}, u32[]{:S(2)}, u32[]{:S(2)}) collective-permute-start(bf16[256,256]{1,0:T(8,128)(2,1)} %get-tuple-element.11), channel_id=1, source_target_pairs={{0,8},{4,12},{8,0},{12,4},{1,9},{5,13},{9,1},{13,5},{2,10},{6,14},... | collective-permute-start | bytes 393224 | tf_op jit(solution)/shard_map/ppermute | solution.py:231
  17.6 6.8 %collective-permute-start = (bf16[256,256]{1,0:T(8,128)(2,1)}, bf16[256,256]{1,0:T(8,128)(2,1)S(1)}, u32[]{:S(2)}, u32[]{:S(2)}) collective-permute-start(bf16[256,256]{1,0:T(8,128)(2,1)} %get-tuple-element.10), channel_id=1, source_target_pairs={{0,12},{4,8},{8,4},{12,0},{1,13},{5,9},{9,5},{13,1},{2,14},{6,10},... | collective-permute-start | bytes 393224 | tf_op jit(solution)/shard_map/ppermute | solution.py:231
  25.5 5.5 %collective-permute-start.5 = (bf16[64,256]{1,0:T(8,128)(2,1)S(1)}, bf16[64,256]{1,0:T(8,128)(2,1)S(1)}, u32[]{:S(2)}, u32[]{:S(2)}) collective-permute-start(bf16[64,256]{1,0:T(8,128)(2,1)S(1)} %get-tuple-element.14), channel_id=1, source_target_pairs={{0,3},{1,0},{2,1},{3,2},{4,7},{5,4},{6,5},{7,6},{8,11},{9,8},{10,9... | collective-permute-start | bytes 98312 | tf_op jit(solution)/shard_map/ppermute | solution.py:237
  29.3 5.1 %collective-permute-start.4 = (bf16[64,256]{1,0:T(8,128)(2,1)S(1)}, bf16[64,256]{1,0:T(8,128)(2,1)S(1)}, u32[]{:S(2)}, u32[]{:S(2)}) collective-permute-start(bf16[64,256]{1,0:T(8,128)(2,1)S(1)} %get-tuple-element.15), channel_id=1, source_target_pairs={{0,2},{1,3},{2,0},{3,1},{4,6},{5,7},{6,4},{7,5},{8,10},{9,11},{10,... | collective-permute-start | bytes 98312 | tf_op jit(solution)/shard_map/ppermute | solution.py:237
  29.3 5.7 %collective-permute-start.3 = (bf16[64,256]{1,0:T(8,128)(2,1)S(1)}, bf16[64,256]{1,0:T(8,128)(2,1)S(1)}, u32[]{:S(2)}, u32[]{:S(2)}) collective-permute-start(bf16[64,256]{1,0:T(8,128)(2,1)S(1)} %get-tuple-element.13), channel_id=1, source_target_pairs={{0,1},{1,2},{2,3},{3,0},{4,5},{5,6},{6,7},{7,4},{8,9},{9,10},{10,1... | collective-permute-start | bytes 98312 | tf_op jit(solution)/shard_map/ppermute | solution.py:237

commit v10 on v9

--- a/solution.py
+++ b/solution.py
@@ -35,7 +35,7 @@
 def correlate_kernel(
     place_ref, moveouts_ref, uptime_ref, records_ref, templates_ref, *refs, window,
 ):
-    *out_refs, masked, shifted, factor, loaded, bank, windows_a, windows_b, bank_a, bank_b, total, arrived = refs
+    *out_refs, masked, shifted, factor, loaded, unit_matrix, bank, windows_a, windows_b, bank_a, bank_b, total, arrived = refs
     components, stations, length = records_ref.shape
     block_count = uptime_ref.shape[0]
     rows = masked.shape[0]
@@ -59,6 +59,9 @@
     total[...] = jnp.zeros(total.shape, total.dtype)
     for ref in (bank, bank_a, bank_b, windows_b):
         ref[...] = jnp.zeros(ref.shape, ref.dtype)
+    across = lax.broadcasted_iota(jnp.int32, unit_matrix.shape, 1)
+    down = lax.broadcasted_iota(jnp.int32, unit_matrix.shape, 0)
+    unit_matrix[...] = jnp.where(across == down, 1.0, 0.0).astype(unit_matrix.dtype)
     depth = components * groups * GROUP
     if windows_a.shape[0] > depth:
         windows_a[depth:, :] = jnp.zeros((windows_a.shape[0] - depth, length), windows_a.dtype)
@@ -134,7 +137,9 @@
             unit = (values * lax.rsqrt(squares + 1e-06)).astype(jnp.bfloat16)
             at = j * groups * GROUP
             bank[at:at + window, :] = unit
-        turned[...] = bank[...].T
+        turned[...] = lax.dot_general(
+            unit_matrix[...], bank[...], (((1,), (1,)), ((), ())),
+            preferred_element_type=jnp.float32).astype(turned.dtype)
         left = list(range(0, length, width))
         share = up(len(left), components) // components
         for j in range(components):
@@ -171,40 +176,46 @@
 
     lax.fori_loop(0, stations // 2 + 1, two_stations, 0)
 
-    size = out_refs[0].shape[0]
+    send_far, send_near, keep_far, keep_near = out_refs
+    size = send_near.shape[1]
+    hops = length // (2 * size)
+    core, x = place_ref[0] % 2, place_ref[0] // 2
     flip = LANES - 1 - lax.broadcasted_iota(jnp.int32, (LANES, LANES), 1)
-    for step, out_ref in enumerate(out_refs, 1):
-        region = partner(place_ref[0], step % len(out_refs), len(out_refs))
+
+    def write(region, out_ref, n):
         for r in range(0, size, LANES):
             at = pl.multiple_of(length - LANES - region * size - r, LANES)
             for h in range(0, total.shape[0], LANES):
                 block = total[h:h + LANES, pl.ds(at, LANES)]
                 block = jnp.take_along_axis(block, flip, axis=1).T
-                out_ref[r:r + LANES, h:h + LANES] = block.astype(out_ref.dtype)
-
-
-def partner(place, step, count):
-    return place ^ step if count & (count - 1) == 0 else (place + step) % count
-
-
-def correlate(place, records, templates, moveouts, uptime, count):
+                out_ref[n, r:r + LANES, h:h + LANES] = block.astype(out_ref.dtype)
+
+    for n in range(hops):
+        chip = 2 * ((x + n) % hops)
+        send_ref, keep_ref = (send_far, keep_far) if n else (send_near, keep_near)
+        write(chip + 1 - core, send_ref, max(n - 1, 0))
+        write(chip + core, keep_ref, max(n - 1, 0))
+
+
+def correlate(place, records, templates, moveouts, uptime, hops):
     components, stations, length = records.shape
     window, bank_size = templates.shape[2:]
     margin = up(window, LANES)
     rows = up(stations * components, 8)
-    region = length // count
+    region = length // (2 * hops)
     depth = up(components * up(window, GROUP), LANES)
     scalars = pl.BlockSpec(memory_space=pltpu.SMEM)
     vectors = pl.BlockSpec(memory_space=pltpu.VMEM)
     return pl.pallas_call(
         functools.partial(correlate_kernel, window=window),
         in_specs=[scalars, scalars, scalars, vectors, pl.BlockSpec(memory_space=pl.ANY)],
-        out_specs=[vectors] * count,
+        out_specs=[vectors] * 4,
         scratch_shapes=[
             pltpu.VMEM((rows, length + margin + LANES + up(MAXMO, LANES)), jnp.float32),
             pltpu.VMEM((rows, length + margin), jnp.float32),
             pltpu.VMEM((rows, length), jnp.float32),
             pltpu.VMEM(templates.shape, templates.dtype),
+            pltpu.VMEM((bank_size, bank_size), jnp.bfloat16),
             pltpu.VMEM((depth, bank_size), jnp.bfloat16),
             pltpu.VMEM((depth, length), jnp.bfloat16),
             pltpu.VMEM((depth, length), jnp.bfloat16),
@@ -213,8 +224,10 @@
             pltpu.VMEM((bank_size, length), jnp.float32),
             pltpu.SemaphoreType.DMA((stations,)),
         ],
-        out_shape=[jax.ShapeDtypeStruct((region, bank_size), jnp.bfloat16)] * (count - 1)
-        + [jax.ShapeDtypeStruct((region, bank_size), jnp.float32)],
+        out_shape=[
+            jax.ShapeDtypeStruct((count, region, bank_size), kind)
+            for kind in (jnp.bfloat16, jnp.float32) for count in (hops - 1, 1)
+        ],
         compiler_params=pltpu.CompilerParams(vmem_limit_bytes=58 * 2**20),
         name="correlate",
     )(place, moveouts, uptime, records, templates)
@@ -222,13 +235,19 @@
 
 def body(records, templates, moveouts, uptime):
     tm, chan = lax.axis_size("tm"), lax.axis_size("chan")
+    hops = tm // 2
     t, z = lax.axis_index("tm"), lax.axis_index("chan")
-    *sent, result = correlate(
-        t.reshape(1), records.transpose(1, 0, 2), templates, moveouts.T, uptime.T, tm
+    send_far, send_near, keep_far, keep_near = correlate(
+        t.reshape(1), records.transpose(1, 0, 2), templates, moveouts.T, uptime.T, hops
     )
-    for step in range(tm - 1, 0, -1):
-        perm = [(i, partner(i, step, tm)) for i in range(tm)]
-        result = result + lax.ppermute(sent[step - 1], "tm", perm).astype(jnp.float32)
+    cores = [(i, i ^ 1) for i in range(tm)]
+    far = lax.ppermute(send_far, "tm", cores)
+    near = lax.ppermute(send_near, "tm", cores)
+    far = (keep_far + far.astype(jnp.float32)).astype(jnp.bfloat16)
+    result = keep_near[0] + near[0].astype(jnp.float32)
+    for step in range(1, hops):
+        perm = [(i, ((i // 2 + step) % hops) * 2 + i % 2) for i in range(tm)]
+        result = result + lax.ppermute(far[step - 1], "tm", perm).astype(jnp.float32)
     mine = result.reshape(chan, result.shape[0] // chan, result.shape[1])
     result = lax.dynamic_index_in_dim(mine, z, 0, keepdims=False)
     for step in range(1, chan):

time: 35.8 us -> 38.3 us (1.070)
  Pallas kernels: 14.6 us -> 17.4 us
  waiting for transfers between devices: 11.5 us -> 9.63 us
  other arithmetic: 1.65 us -> 2.61 us
  starting transfers between devices: 7.88 us -> 8.43 us
    pallas_call x1, Pallas kernels: 14.6 us -> 17.4 us  [correlate(): pl.pallas_call(functools.partial(correlate_kernel, window=window), in_spe...]
    ppermute x3, waiting for transfers between devices: 6.78 us -> 4.93 us  [the longest x1 3.81 us: body(): lax.ppermute(far[step - 1], 'tm', perm).astype(jnp.float32)]
    squeeze x0 -> x1, other arithmetic: none -> 0.98 us  [body(): far[step - 1]]
    ppermute x3, starting transfers between devices: 3.11 us -> 3.51 us  [the longest x1 2.91 us: body(): lax.ppermute(far[step - 1], 'tm', perm).astype(jnp.float32)]
  transfers between devices with their start and end apart: 6 -> 6, of which waited for: 5 -> 5; matrix products, arithmetic and copies ran while one was open for 0% -> 3% of each run, Pallas kernels for 0% -> 0%
where the time goes in v10:
time: 38.3 us; the launch traced here: 38.1 us
  Pallas kernels  17.4 us (45%)
  waiting for transfers between devices  9.63 us (25%)
  starting transfers between devices  8.43 us (22%)
  other arithmetic  2.61 us (7%)
    pallas_call x1, Pallas kernels, correlate(): pl.pallas_call(functools.partial(correlate_kernel, window=window), in_spe...  17.4 us
    ppermute x3, starting transfers between devices, body(): lax.ppermute(block.astype(jnp.bfloat16), 'chan', perm).astype(jnp.float32)  4.92 us
    ppermute x3, waiting for transfers between devices, body(): lax.ppermute(block.astype(jnp.bfloat16), 'chan', perm).astype(jnp.float32)  4.7 us
    ppermute x1, waiting for transfers between devices, body(): lax.ppermute(far[step - 1], 'tm', perm).astype(jnp.float32)  3.81 us
    ppermute x1, starting transfers between devices, body(): lax.ppermute(far[step - 1], 'tm', perm).astype(jnp.float32)  2.91 us
    ppermute x1, waiting for transfers between devices, body(): far = lax.ppermute(send_far, 'tm', cores)  1.12 us
    add x1, other arithmetic, body(): result + lax.ppermute(far[step - 1], 'tm', perm).astype(jnp.float32)  0.99 us
    squeeze x1, other arithmetic, body(): far[step - 1]  0.98 us
  transfers between devices with their start and end apart: 6, of which 5 were waited for; matrix products, arithmetic and copies ran while one was open for 3% of the time, Pallas kernels for 0%

profile of v10, /device:TPU:0, one launch (start us, length us, event | category | flops | bytes accessed | tf_op | source)
XLA Modules:
  0.0 38.1 jit_solution(3423458967146882156)
XLA Ops:
  0.0 17.4 %correlate.1 = (bf16[1,256,256]{2,1,0:T(8,128)(2,1)}, bf16[1,256,256]{2,1,0:T(8,128)(2,1)}, f32[1,256,256]{2,1,0:T(8,128)}, f32[1,256,256]{2,1,0:T(8,128)}) custom-call(s32[1]{0:T(128)} %bitcast.place_ref, s32[3,16]{1,0:T(4,128)} %bitcast.28, s32[2,16]{1,0:T(2,128)} %bitcast.29, bf16[3,16,1024]{2,1,0:T(8,128)(2,1)} %bitcast.27, ...), custom_call_target="tpu_custom_call" | custom-call | tf_op jit(solution)/shard_map/correlate/pallas_call | solution.py:209
  17.4 0.5 %collective-permute-start.1 = (bf16[1,256,256]{2,1,0:T(8,128)(2,1)}, bf16[1,256,256]{2,1,0:T(8,128)(2,1)S(1)}, u32[]{:S(2)}, u32[]{:S(2)}) collective-permute-start(bf16[1,256,256]{2,1,0:T(8,128)(2,1)} %get-tuple-element.12), channel_id=1, source_target_pairs={{0,4},{4,0},{8,12},{12,8},{1,5},{5,1},{9,13},{13,9},{2,6},{6,2},{1... | collective-permute-start | bytes 393224 | tf_op jit(solution)/shard_map/ppermute | solution.py:244
  17.9 0.1 collective-permute-start
  18.0 1.1 %collective-permute-done.1 = bf16[1,256,256]{2,1,0:T(8,128)(2,1)S(1)} collective-permute-done((bf16[1,256,256]{2,1,0:T(8,128)(2,1)}, bf16[1,256,256]{2,1,0:T(8,128)(2,1)S(1)}, u32[]{:S(2)}, u32[]{:S(2)}) %collective-permute-start.1) | collective-permute-done | bytes 131104 | tf_op jit(solution)/shard_map/ppermute | solution.py:244
  19.1 1.0 %fusion = bf16[256,256]{1,0:T(8,128)(2,1)S(1)} fusion(f32[1,256,256]{2,1,0:T(8,128)} %get-tuple-element.11, bf16[1,256,256]{2,1,0:T(8,128)(2,1)S(1)} %collective-permute-done.1), kind=kLoop, calls=%fused_computation.2 | loop fusion | flops 196608 | bytes 524288 | tf_op jit(solution)/shard_map/squeeze | solution.py:250
  20.1 2.9 %collective-permute-start.2 = (bf16[256,256]{1,0:T(8,128)(2,1)S(1)}, bf16[256,256]{1,0:T(8,128)(2,1)S(1)}, u32[]{:S(2)}, u32[]{:S(2)}) collective-permute-start(bf16[256,256]{1,0:T(8,128)(2,1)S(1)} %fusion), channel_id=1, source_target_pairs={{0,8},{4,12},{8,0},{12,4},{1,9},{5,13},{9,1},{13,5},{2,10},{6,14},... | collective-permute-start | bytes 393224 | tf_op jit(solution)/shard_map/ppermute | solution.py:250
  23.0 0.0 collective-permute-done
  23.0 3.8 %collective-permute-done.2 = bf16[256,256]{1,0:T(8,128)(2,1)S(1)} collective-permute-done((bf16[256,256]{1,0:T(8,128)(2,1)S(1)}, bf16[256,256]{1,0:T(8,128)(2,1)S(1)}, u32[]{:S(2)}, u32[]{:S(2)}) %collective-permute-start.2) | collective-permute-done | bytes 131104 | tf_op jit(solution)/shard_map/ppermute | solution.py:250
  26.8 1.0 %bitcast_add_fusion = f32[256,256]{1,0:T(8,128)S(1)} fusion(bf16[256,256]{1,0:T(8,128)(2,1)S(1)} %collective-permute-done.2, f32[1,256,256]{2,1,0:T(8,128)} %get-tuple-element.9, bf16[1,256,256]{2,1,0:T(8,128)(2,1)S(1)} %collective-permute-done), kind=kLoop, calls=%fused_computation | loop fusion | flops 262144 | bytes 786432 | tf_op jit(solution)/shard_map/add | solution.py:250
  27.8 3.9 %collective-permute-start.5 = (bf16[64,256]{1,0:T(8,128)(2,1)S(1)}, bf16[64,256]{1,0:T(8,128)(2,1)S(1)}, u32[]{:S(2)}, u32[]{:S(2)}) collective-permute-start(bf16[64,256]{1,0:T(8,128)(2,1)S(1)} %get-tuple-element.14), channel_id=1, source_target_pairs={{0,3},{1,0},{2,1},{3,2},{4,7},{5,4},{6,5},{7,6},{8,11},{9,8},{10,9... | collective-permute-start | bytes 98312 | tf_op jit(solution)/shard_map/ppermute | solution.py:256
  31.7 0.0 collective-permute-start.4
  31.7 1.0 %collective-permute-start.3 = (bf16[64,256]{1,0:T(8,128)(2,1)S(1)}, bf16[64,256]{1,0:T(8,128)(2,1)S(1)}, u32[]{:S(2)}, u32[]{:S(2)}) collective-permute-start(bf16[64,256]{1,0:T(8,128)(2,1)S(1)} %get-tuple-element.13), channel_id=1, source_target_pairs={{0,1},{1,2},{2,3},{3,0},{4,5},{5,6},{6,7},{7,4},{8,9},{9,10},{10,1... | collective-permute-start | bytes 98312 | tf_op jit(solution)/shard_map/ppermute | solution.py:256
  32.7 0.6 %collective-permute-done.5 = bf16[64,256]{1,0:T(8,128)(2,1)S(1)} collective-permute-done((bf16[64,256]{1,0:T(8,128)(2,1)S(1)}, bf16[64,256]{1,0:T(8,128)(2,1)S(1)}, u32[]{:S(2)}, u32[]{:S(2)}) %collective-permute-start.5) | collective-permute-done | bytes 32800 | tf_op jit(solution)/shard_map/ppermute | solution.py:256
  33.3 3.2 %collective-permute-done.4 = bf16[64,256]{1,0:T(8,128)(2,1)S(1)} collective-permute-done((bf16[64,256]{1,0:T(8,128)(2,1)S(1)}, bf16[64,256]{1,0:T(8,128)(2,1)S(1)}, u32[]{:S(2)}, u32[]{:S(2)}) %collective-permute-start.4) | collective-permute-done | bytes 32800 | tf_op jit(solution)/shard_map/ppermute | solution.py:256
  36.5 0.9 %collective-permute-done.3 = bf16[64,256]{1,0:T(8,128)(2,1)S(1)} collective-permute-done((bf16[64,256]{1,0:T(8,128)(2,1)S(1)}, bf16[64,256]{1,0:T(8,128)(2,1)S(1)}, u32[]{:S(2)}, u32[]{:S(2)}) %collective-permute-start.3) | collective-permute-done | bytes 32800 | tf_op jit(solution)/shard_map/ppermute | solution.py:256
  37.4 0.6 %fusion.3 = f32[256,64]{0,1:T(8,128)} fusion(bf16[64,256]{1,0:T(8,128)(2,1)S(1)} %collective-permute-done.5, bf16[64,256]{1,0:T(8,128)(2,1)S(1)} %collective-permute-done.4, bf16[64,256]{1,0:T(8,128)(2,1)S(1)} %collective-permute-done.3, f32[4,64,256]{2,1,0:T(8,128)S(1)} %bitcast.26, s32[]{:T(128)S(6)} %select_n.28), kind=kLoop, calls=%fused_computation.6 | loop fusion | flops 98304 | bytes 229380 | tf_op jit(solution)/shard_map/transpose | solution.py:257
  (1 shorter events, 0.0 us)
Async XLA Ops:
  17.4 1.7 %collective-permute-start.1 = (bf16[1,256,256]{2,1,0:T(8,128)(2,1)}, bf16[1,256,256]{2,1,0:T(8,128)(2,1)S(1)}, u32[]{:S(2)}, u32[]{:S(2)}) collective-permute-start(bf16[1,256,256]{2,1,0:T(8,128)(2,1)} %get-tuple-element.12), channel_id=1, source_target_pairs={{0,4},{4,0},{8,12},{12,8},{1,5},{5,1},{9,13},{13,9},{2,6},{6,2},{1... | collective-permute-start | bytes 393224 | tf_op jit(solution)/shard_map/ppermute | solution.py:244
  17.9 5.1 %collective-permute-start = (bf16[1,256,256]{2,1,0:T(8,128)(2,1)}, bf16[1,256,256]{2,1,0:T(8,128)(2,1)S(1)}, u32[]{:S(2)}, u32[]{:S(2)}) collective-permute-start(bf16[1,256,256]{2,1,0:T(8,128)(2,1)} %get-tuple-element.10), channel_id=1, source_target_pairs={{0,4},{4,0},{8,12},{12,8},{1,5},{5,1},{9,13},{13,9},{2,6},{6,2},{1... | collective-permute-start | bytes 393224 | tf_op jit(solution)/shard_map/ppermute | solution.py:245
  20.1 6.7 %collective-permute-start.2 = (bf16[256,256]{1,0:T(8,128)(2,1)S(1)}, bf16[256,256]{1,0:T(8,128)(2,1)S(1)}, u32[]{:S(2)}, u32[]{:S(2)}) collective-permute-start(bf16[256,256]{1,0:T(8,128)(2,1)S(1)} %fusion), channel_id=1, source_target_pairs={{0,8},{4,12},{8,0},{12,4},{1,9},{5,13},{9,1},{13,5},{2,10},{6,14},... | collective-permute-start | bytes 393224 | tf_op jit(solution)/shard_map/ppermute | solution.py:250
  27.8 5.5 %collective-permute-start.5 = (bf16[64,256]{1,0:T(8,128)(2,1)S(1)}, bf16[64,256]{1,0:T(8,128)(2,1)S(1)}, u32[]{:S(2)}, u32[]{:S(2)}) collective-permute-start(bf16[64,256]{1,0:T(8,128)(2,1)S(1)} %get-tuple-element.14), channel_id=1, source_target_pairs={{0,3},{1,0},{2,1},{3,2},{4,7},{5,4},{6,5},{7,6},{8,11},{9,8},{10,9... | collective-permute-start | bytes 98312 | tf_op jit(solution)/shard_map/ppermute | solution.py:256
  31.7 4.8 %collective-permute-start.4 = (bf16[64,256]{1,0:T(8,128)(2,1)S(1)}, bf16[64,256]{1,0:T(8,128)(2,1)S(1)}, u32[]{:S(2)}, u32[]{:S(2)}) collective-permute-start(bf16[64,256]{1,0:T(8,128)(2,1)S(1)} %get-tuple-element.15), channel_id=1, source_target_pairs={{0,2},{1,3},{2,0},{3,1},{4,6},{5,7},{6,4},{7,5},{8,10},{9,11},{10,... | collective-permute-start | bytes 98312 | tf_op jit(solution)/shard_map/ppermute | solution.py:256
  31.7 5.7 %collective-permute-start.3 = (bf16[64,256]{1,0:T(8,128)(2,1)S(1)}, bf16[64,256]{1,0:T(8,128)(2,1)S(1)}, u32[]{:S(2)}, u32[]{:S(2)}) collective-permute-start(bf16[64,256]{1,0:T(8,128)(2,1)S(1)} %get-tuple-element.13), channel_id=1, source_target_pairs={{0,1},{1,2},{2,3},{3,0},{4,5},{5,6},{6,7},{7,4},{8,9},{9,10},{10,1... | collective-permute-start | bytes 98312 | tf_op jit(solution)/shard_map/ppermute | solution.py:256

commit v11 on v7

--- a/solution.py
+++ b/solution.py
@@ -33,10 +33,9 @@
 
 
 def correlate_kernel(
-    core_ref, moveouts_ref, uptime_ref, records_ref, templates_ref,
-    send_ref, keep_ref,
+    place_ref, moveouts_ref, uptime_ref, records_ref, templates_ref, send_ref, keep_ref,
     masked, shifted, factor, loaded, bank, windows_a, windows_b, bank_a, bank_b, total, arrived,
-    *, window,
+    *, window, batch,
 ):
     components, stations, length = records_ref.shape
     block_count = uptime_ref.shape[0]
@@ -48,20 +47,22 @@
     lead = masked.shape[1] - length
 
     def fetch(i):
-        return pltpu.make_async_copy(templates_ref.at[i], loaded.at[i], arrived.at[i])
+        at = pl.ds(i * batch, batch)
+        return pltpu.make_async_copy(templates_ref.at[at], loaded.at[at], arrived.at[i])
 
     def start(i, carry):
         fetch(i).start()
         return carry
 
-    lax.fori_loop(0, stations, start, 0)
+    batches = stations // batch
+    lax.fori_loop(0, batches, start, 0)
 
     masked[:, :lead] = jnp.zeros((rows, lead), jnp.float32)
     shifted[...] = jnp.zeros(shifted.shape, jnp.float32)
     total[...] = jnp.zeros(total.shape, total.dtype)
     for ref in (bank, bank_a, bank_b, windows_b):
         ref[...] = jnp.zeros(ref.shape, ref.dtype)
-    depth = components * groups * GROUP
+    depth = batch * components * groups * GROUP
     if windows_a.shape[0] > depth:
         windows_a[depth:, :] = jnp.zeros((windows_a.shape[0] - depth, length), windows_a.dtype)
     offsets = lax.broadcasted_iota(jnp.int32, (stations, LANES), 1)
@@ -86,8 +87,8 @@
             masked[j * stations:(j + 1) * stations, pl.ds(to, LANES)] = values[:stations]
         return carry
 
-    lax.fori_loop(0, length // LANES, mask_tile, 0)
-    burst = 4 if stations % 4 == 0 else 1
+    lax.fori_loop(0, length // LANES, mask_tile, 0, unroll=length // LANES <= 8)
+    burst = stations
 
     def shift_some(i, carry):
         shifts = []
@@ -104,7 +105,7 @@
         return carry
 
     lax.fori_loop(0, stations // burst, shift_some, 0)
-    chunk = rows // 2 if rows % 16 == 0 else 8
+    chunk = rows
 
     def energy_some(i, carry):
         at = pl.ds(pl.multiple_of(i * chunk, 8), chunk)
@@ -121,59 +122,54 @@
             turned[...], windows[:, n:n + width], preferred_element_type=jnp.float32)
 
     def build(i, windows, turned, pending):
+        places = [(u, j) for u in range(batch) for j in range(components)]
         strips, scales = [], []
-        for j in range(components):
-            c = j * stations + i
+        for u, j in places:
+            c = j * stations + i * batch + u
             half = jnp.broadcast_to(shifted[pl.ds(c, 1), :], (8, span))
             strips.append(jnp.concatenate(
                 [pltpu.roll(half, b, 1, stride=1, stride_axis=0) for b in (0, 8)], axis=0
             ).astype(jnp.bfloat16))
             scale = jnp.broadcast_to(factor[pl.ds(c, 1), :], (GROUP, length))
             scales.append(scale.astype(jnp.bfloat16))
-        for j in range(components):
-            values = loaded[i, j].astype(jnp.float32)
+        for m, (u, j) in enumerate(places):
+            values = loaded[i * batch + u, j].astype(jnp.float32)
             squares = jnp.sum(values * values, axis=0, keepdims=True)
             unit = (values * lax.rsqrt(squares + 1e-06)).astype(jnp.bfloat16)
-            at = j * groups * GROUP
-            bank[at:at + window, :] = unit
+            bank[m * groups * GROUP:m * groups * GROUP + window, :] = unit
         turned[...] = bank[...].T
         left = list(range(0, length, width))
-        share = up(len(left), components) // components
-        for j in range(components):
+        share = up(len(left), len(places)) // len(places)
+        for m in range(len(places)):
             for a in range(min(groups, LANES // GROUP)):
-                rolled = strips[j] if a == 0 else pltpu.roll(strips[j], a * GROUP, 1)
+                rolled = strips[m] if a == 0 else pltpu.roll(strips[m], a * GROUP, 1)
                 for g in range(a, groups, LANES // GROUP):
                     begin = margin - (g - a) * GROUP
-                    at = (j * groups + g) * GROUP
-                    windows[at:at + GROUP, :] = rolled[:, begin:begin + length] * scales[j]
+                    at = (m * groups + g) * GROUP
+                    windows[at:at + GROUP, :] = rolled[:, begin:begin + length] * scales[m]
             for n in left[:share]:
                 multiply(n, *pending)
             left = left[share:]
 
-    def two_stations(i, carry):
-        station = jnp.minimum(2 * i, stations - 1)
-
-        @pl.when(2 * i < stations)
+    def two_batches(i, carry):
+        @pl.when(2 * i < batches)
         def _():
             fetch(2 * i).wait()
 
-        build(station, windows_a, bank_a, (windows_b, bank_b))
-
-        @pl.when(2 * i < stations)
+        build(jnp.minimum(2 * i, batches - 1), windows_a, bank_a, (windows_b, bank_b))
+
+        @pl.when(2 * i < batches)
         def _():
-            later = jnp.minimum(2 * i + 1, stations - 1)
-
-            @pl.when(2 * i + 1 < stations)
+            @pl.when(2 * i + 1 < batches)
             def _():
                 fetch(2 * i + 1).wait()
 
-            build(later, windows_b, bank_b, (windows_a, bank_a))
-
-        return carry
-
-    lax.fori_loop(0, stations // 2 + 1, two_stations, 0)
-
-    core = core_ref[0]
+            build(jnp.minimum(2 * i + 1, batches - 1), windows_b, bank_b, (windows_a, bank_a))
+
+        return carry
+
+    lax.fori_loop(0, batches // 2 + 1, two_batches, 0)
+    core = place_ref[0] % 2
     hops, region = keep_ref.shape[0], keep_ref.shape[1]
     flip = LANES - 1 - lax.broadcasted_iota(jnp.int32, (LANES, LANES), 1)
 
@@ -182,32 +178,29 @@
         block = total[h:h + LANES, pl.ds(at, LANES)]
         return jnp.take_along_axis(block, flip, axis=1).T
 
-    def write(i, carry):
-        x = i // (region // LANES)
-        r = pl.multiple_of(i % (region // LANES) * LANES, LANES)
-        own = (2 * x + core) * region + r
-        other = (2 * x + 1 - core) * region + r
-        for h in range(0, total.shape[0], LANES):
-            keep_ref[x, pl.ds(r, LANES), h:h + LANES] = ordered(own, h)
-            send_ref[x, pl.ds(r, LANES), h:h + LANES] = ordered(other, h).astype(send_ref.dtype)
-        return carry
-
-    lax.fori_loop(0, hops * (region // LANES), write, 0)
-
-
-def correlate(core, records, templates, moveouts, uptime, hops):
+    for x in range(hops):
+        for r in range(0, region, LANES):
+            for h in range(0, total.shape[0], LANES):
+                own = (2 * x + core) * region + r
+                other = (2 * x + 1 - core) * region + r
+                keep_ref[x, r:r + LANES, h:h + LANES] = ordered(own, h)
+                send_ref[x, r:r + LANES, h:h + LANES] = ordered(other, h).astype(send_ref.dtype)
+
+
+def correlate(place, records, templates, moveouts, uptime, hops):
     components, stations, length = records.shape
     window, bank_size = templates.shape[2:]
     margin = up(window, LANES)
     rows = up(stations * components, 8)
     region = length // (2 * hops)
-    depth = up(components * up(window, GROUP), LANES)
+    batch = 2 if stations % 2 == 0 else 1
+    depth = up(batch * components * up(window, GROUP), LANES)
     scalars = pl.BlockSpec(memory_space=pltpu.SMEM)
     vectors = pl.BlockSpec(memory_space=pltpu.VMEM)
     return pl.pallas_call(
-        functools.partial(correlate_kernel, window=window),
+        functools.partial(correlate_kernel, window=window, batch=batch),
         in_specs=[scalars, scalars, scalars, vectors, pl.BlockSpec(memory_space=pl.ANY)],
-        out_specs=[vectors, vectors],
+        out_specs=[vectors] * 2,
         scratch_shapes=[
             pltpu.VMEM((rows, length + margin + LANES + up(MAXMO, LANES)), jnp.float32),
             pltpu.VMEM((rows, length + margin), jnp.float32),
@@ -219,24 +212,24 @@
             pltpu.VMEM((bank_size, depth), jnp.bfloat16),
             pltpu.VMEM((bank_size, depth), jnp.bfloat16),
             pltpu.VMEM((bank_size, length), jnp.float32),
-            pltpu.SemaphoreType.DMA((stations,)),
+            pltpu.SemaphoreType.DMA((stations // batch,)),
         ],
         out_shape=[
-            jax.ShapeDtypeStruct((hops, region, bank_size), jnp.bfloat16),
-            jax.ShapeDtypeStruct((hops, region, bank_size), jnp.float32),
+            jax.ShapeDtypeStruct((hops, region, bank_size), kind)
+            for kind in (jnp.bfloat16, jnp.float32)
         ],
-        compiler_params=pltpu.CompilerParams(vmem_limit_bytes=52 * 2**20),
+        compiler_params=pltpu.CompilerParams(vmem_limit_bytes=58 * 2**20),
         name="correlate",
-    )(core, moveouts, uptime, records, templates)
+    )(place, moveouts, uptime, records, templates)
 
 
 def body(records, templates, moveouts, uptime):
     tm, chan = lax.axis_size("tm"), lax.axis_size("chan")
     hops = tm // 2
     t, z = lax.axis_index("tm"), lax.axis_index("chan")
-    x, core = t // 2, t % 2
+    x = t // 2
     send, keep = correlate(
-        core.reshape(1), records.transpose(1, 0, 2), templates, moveouts.T, uptime.T, hops
+        t.reshape(1), records.transpose(1, 0, 2), templates, moveouts.T, uptime.T, hops
     )
     got = lax.ppermute(send, "tm", [(i, i ^ 1) for i in range(tm)])
     mine = keep + got.astype(jnp.float32)

time: 35.6 us -> 32.9 us (0.924)
  Pallas kernels: 15.6 us -> 12.6 us
  waiting for transfers between devices: 7.53 us -> 9.87 us
  local copies, waits for them, and re-layouts: 2.3 us -> 0.04 us
  other arithmetic: 0.72 us -> 1.76 us
  starting transfers between devices: 9.2 us -> 8.35 us
    pallas_call x1, Pallas kernels: 15.6 us -> 12.6 us  [correlate(): pl.pallas_call(functools.partial(correlate_kernel, window=window, batch=b...]
    unnamed x6 -> x0, local copies, waits for them, and re-layouts: 2.25 us -> none
    ppermute x3, waiting for transfers between devices: 2.57 us -> 4.7 us  [body(): lax.ppermute(block.astype(jnp.bfloat16), 'chan', perm).astype(jnp.float32)]
    add x1, other arithmetic: 0.05 us -> 1.09 us  [body(): mine = keep + got.astype(jnp.float32)]
    ppermute x3, starting transfers between devices: 5.8 us -> 4.91 us  [body(): lax.ppermute(block.astype(jnp.bfloat16), 'chan', perm).astype(jnp.float32)]
where the time goes in v11:
time: 32.9 us; the launch traced here: 32.7 us
  Pallas kernels  12.6 us (38%)
  waiting for transfers between devices  9.87 us (30%)
  starting transfers between devices  8.35 us (25%)
  other arithmetic  1.76 us (5%)
    pallas_call x1, Pallas kernels, correlate(): pl.pallas_call(functools.partial(correlate_kernel, window=window, batch=b...  12.6 us
    ppermute x3, starting transfers between devices, body(): lax.ppermute(block.astype(jnp.bfloat16), 'chan', perm).astype(jnp.float32)  4.91 us
    ppermute x3, waiting for transfers between devices, body(): lax.ppermute(block.astype(jnp.bfloat16), 'chan', perm).astype(jnp.float32)  4.7 us
    ppermute x1, waiting for transfers between devices, body(): lax.ppermute(block.astype(jnp.bfloat16), 'tm', perm).astype(jnp.float32)  3.8 us
    ppermute x1, starting transfers between devices, body(): lax.ppermute(block.astype(jnp.bfloat16), 'tm', perm).astype(jnp.float32)  2.93 us
    ppermute x1, waiting for transfers between devices, body(): got = lax.ppermute(send, 'tm', [(i, i ^ 1) for i in range(tm)])  1.37 us
    add x1, other arithmetic, body(): mine = keep + got.astype(jnp.float32)  1.09 us
  transfers between devices with their start and end apart: 5, of which 5 were waited for; matrix products, arithmetic and copies ran while one was open for 0% of the time, Pallas kernels for 0%

profile of v11, /device:TPU:0, one launch (start us, length us, event | category | flops | bytes accessed | tf_op | source)
XLA Modules:
  0.0 32.7 jit_solution(3136116799512198252)
XLA Ops:
  0.0 12.6 %correlate.1 = (bf16[2,256,256]{2,1,0:T(8,128)(2,1)}, f32[2,256,256]{2,1,0:T(8,128)}) custom-call(s32[1]{0:T(128)} %bitcast.place_ref, s32[3,16]{1,0:T(4,128)} %bitcast.28, s32[2,16]{1,0:T(2,128)} %bitcast.29, bf16[3,16,1024]{2,1,0:T(8,128)(2,1)} %bitcast.27, bf16[16,3,200,256]{3,2,1,0:T(8,128)(2,1)} %templates_ref.1), custom_call_target="tpu_custom_call" | custom-call | tf_op jit(solution)/shard_map/correlate/pallas_call | solution.py:200
  12.6 0.5 %collective-permute-start = (bf16[2,256,256]{2,1,0:T(8,128)(2,1)}, bf16[2,256,256]{2,1,0:T(8,128)(2,1)S(1)}, u32[]{:S(2)}, u32[]{:S(2)}) collective-permute-start(bf16[2,256,256]{2,1,0:T(8,128)(2,1)} %get-tuple-element.8), channel_id=1, source_target_pairs={{0,4},{4,0},{8,12},{12,8},{1,5},{5,1},{9,13},{13,9},{2,6},{6,2},{1... | collective-permute-start | bytes 786440 | tf_op jit(solution)/shard_map/ppermute | solution.py:234
  13.1 1.4 %collective-permute-done = bf16[2,256,256]{2,1,0:T(8,128)(2,1)S(1)} collective-permute-done((bf16[2,256,256]{2,1,0:T(8,128)(2,1)}, bf16[2,256,256]{2,1,0:T(8,128)(2,1)S(1)}, u32[]{:S(2)}, u32[]{:S(2)}) %collective-permute-start) | collective-permute-done | bytes 262176 | tf_op jit(solution)/shard_map/ppermute | solution.py:234
  14.5 1.1 %convert_add_fusion = f32[2,256,256]{2,1,0:T(8,128)S(1)} fusion(f32[2,256,256]{2,1,0:T(8,128)} %get-tuple-element.7, bf16[2,256,256]{2,1,0:T(8,128)(2,1)S(1)} %collective-permute-done), kind=kLoop, calls=%fused_computation | loop fusion | flops 262144 | bytes 1310720 | tf_op jit(solution)/shard_map/add | solution.py:235
  15.6 2.9 %collective-permute-start.1 = (bf16[256,256]{1,0:T(8,128)(2,1)S(1)}, bf16[256,256]{1,0:T(8,128)(2,1)S(1)}, u32[]{:S(2)}, u32[]{:S(2)}) collective-permute-start(bf16[256,256]{1,0:T(8,128)(2,1)S(1)} %fusion), channel_id=1, source_target_pairs={{0,8},{4,12},{8,0},{12,4},{1,9},{5,13},{9,1},{13,5},{2,10},{6,14},... | collective-permute-start | bytes 393224 | tf_op jit(solution)/shard_map/ppermute | solution.py:240
  18.6 3.8 %collective-permute-done.1 = bf16[256,256]{1,0:T(8,128)(2,1)S(1)} collective-permute-done((bf16[256,256]{1,0:T(8,128)(2,1)S(1)}, bf16[256,256]{1,0:T(8,128)(2,1)S(1)}, u32[]{:S(2)}, u32[]{:S(2)}) %collective-permute-start.1) | collective-permute-done | bytes 131104 | tf_op jit(solution)/shard_map/ppermute | solution.py:240
  22.4 3.9 %collective-permute-start.4 = (bf16[64,256]{1,0:T(8,128)(2,1)S(1)}, bf16[64,256]{1,0:T(8,128)(2,1)S(1)}, u32[]{:S(2)}, u32[]{:S(2)}) collective-permute-start(bf16[64,256]{1,0:T(8,128)(2,1)S(1)} %get-tuple-element.10), channel_id=1, source_target_pairs={{0,3},{1,0},{2,1},{3,2},{4,7},{5,4},{6,5},{7,6},{8,11},{9,8},{10,9... | collective-permute-start | bytes 98312 | tf_op jit(solution)/shard_map/ppermute | solution.py:246
  26.3 0.0 collective-permute-start.3
  26.3 1.0 %collective-permute-start.2 = (bf16[64,256]{1,0:T(8,128)(2,1)S(1)}, bf16[64,256]{1,0:T(8,128)(2,1)S(1)}, u32[]{:S(2)}, u32[]{:S(2)}) collective-permute-start(bf16[64,256]{1,0:T(8,128)(2,1)S(1)} %get-tuple-element.9), channel_id=1, source_target_pairs={{0,1},{1,2},{2,3},{3,0},{4,5},{5,6},{6,7},{7,4},{8,9},{9,10},{10,1... | collective-permute-start | bytes 98312 | tf_op jit(solution)/shard_map/ppermute | solution.py:246
  27.3 0.6 %collective-permute-done.4 = bf16[64,256]{1,0:T(8,128)(2,1)S(1)} collective-permute-done((bf16[64,256]{1,0:T(8,128)(2,1)S(1)}, bf16[64,256]{1,0:T(8,128)(2,1)S(1)}, u32[]{:S(2)}, u32[]{:S(2)}) %collective-permute-start.4) | collective-permute-done | bytes 32800 | tf_op jit(solution)/shard_map/ppermute | solution.py:246
  27.9 3.2 %collective-permute-done.3 = bf16[64,256]{1,0:T(8,128)(2,1)S(1)} collective-permute-done((bf16[64,256]{1,0:T(8,128)(2,1)S(1)}, bf16[64,256]{1,0:T(8,128)(2,1)S(1)}, u32[]{:S(2)}, u32[]{:S(2)}) %collective-permute-start.3) | collective-permute-done | bytes 32800 | tf_op jit(solution)/shard_map/ppermute | solution.py:246
  31.1 0.9 %collective-permute-done.2 = bf16[64,256]{1,0:T(8,128)(2,1)S(1)} collective-permute-done((bf16[64,256]{1,0:T(8,128)(2,1)S(1)}, bf16[64,256]{1,0:T(8,128)(2,1)S(1)}, u32[]{:S(2)}, u32[]{:S(2)}) %collective-permute-start.2) | collective-permute-done | bytes 32800 | tf_op jit(solution)/shard_map/ppermute | solution.py:246
  32.0 0.6 %fusion.3 = f32[256,64]{0,1:T(8,128)} fusion(bf16[64,256]{1,0:T(8,128)(2,1)S(1)} %collective-permute-done.4, bf16[64,256]{1,0:T(8,128)(2,1)S(1)} %collective-permute-done.3, bf16[64,256]{1,0:T(8,128)(2,1)S(1)} %collective-permute-done.2, f32[4,64,256]{2,1,0:T(8,128)S(1)} %bitcast.26, s32[]{:T(128)S(6)} %select_n.47), kind=kLoop, calls=%fused_computation.7 | loop fusion | flops 98304 | bytes 229380 | tf_op jit(solution)/shard_map/transpose | solution.py:247
  (3 shorter events, 0.1 us)
Async XLA Ops:
  12.6 1.9 %collective-permute-start = (bf16[2,256,256]{2,1,0:T(8,128)(2,1)}, bf16[2,256,256]{2,1,0:T(8,128)(2,1)S(1)}, u32[]{:S(2)}, u32[]{:S(2)}) collective-permute-start(bf16[2,256,256]{2,1,0:T(8,128)(2,1)} %get-tuple-element.8), channel_id=1, source_target_pairs={{0,4},{4,0},{8,12},{12,8},{1,5},{5,1},{9,13},{13,9},{2,6},{6,2},{1... | collective-permute-start | bytes 786440 | tf_op jit(solution)/shard_map/ppermute | solution.py:234
  15.6 6.7 %collective-permute-start.1 = (bf16[256,256]{1,0:T(8,128)(2,1)S(1)}, bf16[256,256]{1,0:T(8,128)(2,1)S(1)}, u32[]{:S(2)}, u32[]{:S(2)}) collective-permute-start(bf16[256,256]{1,0:T(8,128)(2,1)S(1)} %fusion), channel_id=1, source_target_pairs={{0,8},{4,12},{8,0},{12,4},{1,9},{5,13},{9,1},{13,5},{2,10},{6,14},... | collective-permute-start | bytes 393224 | tf_op jit(solution)/shard_map/ppermute | solution.py:240
  22.4 5.5 %collective-permute-start.4 = (bf16[64,256]{1,0:T(8,128)(2,1)S(1)}, bf16[64,256]{1,0:T(8,128)(2,1)S(1)}, u32[]{:S(2)}, u32[]{:S(2)}) collective-permute-start(bf16[64,256]{1,0:T(8,128)(2,1)S(1)} %get-tuple-element.10), channel_id=1, source_target_pairs={{0,3},{1,0},{2,1},{3,2},{4,7},{5,4},{6,5},{7,6},{8,11},{9,8},{10,9... | collective-permute-start | bytes 98312 | tf_op jit(solution)/shard_map/ppermute | solution.py:246
  26.3 4.8 %collective-permute-start.3 = (bf16[64,256]{1,0:T(8,128)(2,1)S(1)}, bf16[64,256]{1,0:T(8,128)(2,1)S(1)}, u32[]{:S(2)}, u32[]{:S(2)}) collective-permute-start(bf16[64,256]{1,0:T(8,128)(2,1)S(1)} %get-tuple-element.11), channel_id=1, source_target_pairs={{0,2},{1,3},{2,0},{3,1},{4,6},{5,7},{6,4},{7,5},{8,10},{9,11},{10,... | collective-permute-start | bytes 98312 | tf_op jit(solution)/shard_map/ppermute | solution.py:246
  26.3 5.7 %collective-permute-start.2 = (bf16[64,256]{1,0:T(8,128)(2,1)S(1)}, bf16[64,256]{1,0:T(8,128)(2,1)S(1)}, u32[]{:S(2)}, u32[]{:S(2)}) collective-permute-start(bf16[64,256]{1,0:T(8,128)(2,1)S(1)} %get-tuple-element.9), channel_id=1, source_target_pairs={{0,1},{1,2},{2,3},{3,0},{4,5},{5,6},{6,7},{7,4},{8,9},{9,10},{10,1... | collective-permute-start | bytes 98312 | tf_op jit(solution)/shard_map/ppermute | solution.py:246

commit v12 on v11

--- a/solution.py
+++ b/solution.py
@@ -233,18 +233,45 @@
     )
     got = lax.ppermute(send, "tm", [(i, i ^ 1) for i in range(tm)])
     mine = keep + got.astype(jnp.float32)
-    result = lax.dynamic_index_in_dim(mine, x, 0, keepdims=False)
-    for step in range(1, hops):
-        block = lax.dynamic_index_in_dim(mine, (x + step) % hops, 0, keepdims=False)
-        perm = [(i, ((i // 2 + step) % hops) * 2 + i % 2) for i in range(tm)]
-        result = result + lax.ppermute(block.astype(jnp.bfloat16), "tm", perm).astype(jnp.float32)
-    mine = result.reshape(chan, result.shape[0] // chan, result.shape[1])
-    result = lax.dynamic_index_in_dim(mine, z, 0, keepdims=False)
-    for step in range(1, chan):
-        block = lax.dynamic_index_in_dim(mine, (z + step) % chan, 0, keepdims=False)
-        perm = [(i, (i + step) % chan) for i in range(chan)]
-        result = result + lax.ppermute(block.astype(jnp.bfloat16), "chan", perm).astype(jnp.float32)
-    return result.T
+    x_bits = [("tm", 2 << b, (x >> b) & 1) for b in range((hops - 1).bit_length())]
+    z_bits = [("chan", 1 << b, (z >> b) & 1) for b in range((chan - 1).bit_length())]
+    names = x_bits[::-1] + z_bits[::-1]
+    orders = (x_bits + z_bits, z_bits[:1] + x_bits + z_bits[1:])
+    samples, bank_size = mine.shape[1] // chan, mine.shape[2]
+    mine = mine.reshape((2,) * len(names) + (samples, bank_size))
+    width = bank_size // len(orders)
+    halves = [mine[..., h * width:(h + 1) * width] for h in range(len(orders))]
+    left = [list(names) for _ in orders]
+
+    def give(part, axis, bit):
+        send = lax.dynamic_index_in_dim(part, 1 - bit, axis, keepdims=False)
+        return send.astype(jnp.bfloat16)
+
+    def swap(array, axis_name, distance):
+        count = lax.axis_size(axis_name)
+        return lax.ppermute(array, axis_name, [(i, i ^ distance) for i in range(count)])
+
+    joined = None
+    for steps in zip(*orders):
+        if all(step is steps[0] for step in steps) and len(left[0]) == 1:
+            joined = jnp.concatenate(halves, axis=-1)
+            name, distance, bit = steps[0]
+            came = swap(give(joined, 0, bit), name, distance)
+            joined = lax.dynamic_index_in_dim(joined, bit, 0, keepdims=False)
+            joined = joined + came.astype(jnp.float32)
+            break
+        axes = [left[h].index(step) for h, step in enumerate(steps)]
+        came = [
+            swap(give(halves[h], axes[h], step[2]), step[0], step[1])
+            for h, step in enumerate(steps)
+        ]
+        for h, step in enumerate(steps):
+            kept = lax.dynamic_index_in_dim(halves[h], step[2], axes[h], keepdims=False)
+            halves[h] = kept + came[h].astype(jnp.float32)
+            left[h].pop(axes[h])
+    if joined is None:
+        joined = jnp.concatenate(halves, axis=-1)
+    return joined.T
 
 
 def solution(mesh):

time: 32.9 us -> 32.8 us (level)
  waiting for transfers between devices: 9.87 us -> 6.72 us
  starting transfers between devices: 8.35 us -> 11.3 us
    ppermute x4 -> x5, waiting for transfers between devices: 8.5 us -> 5.35 us  [swap(): lax.ppermute(array, axis_name, [(i, i ^ distance) for i in range(count)])]
    ppermute x4 -> x5, starting transfers between devices: 7.84 us -> 10.9 us  [swap(): lax.ppermute(array, axis_name, [(i, i ^ distance) for i in range(count)])]
  transfers between devices with their start and end apart: 5 -> 6, of which waited for: 5 -> 5; matrix products, arithmetic and copies ran while one was open for 0% -> 0% of each run, Pallas kernels for 0% -> 0%
where the time goes in v12:
time: 32.8 us; the launch traced here: 32.6 us
  Pallas kernels  12.6 us (38%)
  starting transfers between devices  11.3 us (34%)
  waiting for transfers between devices  6.72 us (20%)
  other arithmetic  1.79 us (5%)
    pallas_call x1, Pallas kernels, correlate(): pl.pallas_call(functools.partial(correlate_kernel, window=window, batch=b...  12.6 us
    ppermute x5, starting transfers between devices, swap(): lax.ppermute(array, axis_name, [(i, i ^ distance) for i in range(count)])  10.9 us
    ppermute x5, waiting for transfers between devices, swap(): lax.ppermute(array, axis_name, [(i, i ^ distance) for i in range(count)])  5.35 us
    ppermute x1, waiting for transfers between devices, body(): got = lax.ppermute(send, 'tm', [(i, i ^ 1) for i in range(tm)])  1.37 us
    add x1, other arithmetic, body(): mine = keep + got.astype(jnp.float32)  1.09 us
  transfers between devices with their start and end apart: 6, of which 5 were waited for; matrix products, arithmetic and copies ran while one was open for 0% of the time, Pallas kernels for 0%

profile of v12, /device:TPU:0, one launch (start us, length us, event | category | flops | bytes accessed | tf_op | source)
XLA Modules:
  0.0 32.6 jit_solution(5669054126114752690)
XLA Ops:
  0.0 12.6 %correlate.1 = (bf16[2,256,256]{2,1,0:T(8,128)(2,1)}, f32[2,256,256]{2,1,0:T(8,128)}) custom-call(s32[1]{0:T(128)} %bitcast.place_ref, s32[3,16]{1,0:T(4,128)} %bitcast.41, s32[2,16]{1,0:T(2,128)} %bitcast.42, bf16[3,16,1024]{2,1,0:T(8,128)(2,1)} %bitcast.40, bf16[16,3,200,256]{3,2,1,0:T(8,128)(2,1)} %templates_ref.1), custom_call_target="tpu_custom_call" | custom-call | tf_op jit(solution)/shard_map/correlate/pallas_call | solution.py:200
  12.6 0.5 %collective-permute-start = (bf16[2,256,256]{2,1,0:T(8,128)(2,1)}, bf16[2,256,256]{2,1,0:T(8,128)(2,1)S(1)}, u32[]{:S(2)}, u32[]{:S(2)}) collective-permute-start(bf16[2,256,256]{2,1,0:T(8,128)(2,1)} %get-tuple-element.8), channel_id=1, source_target_pairs={{0,4},{4,0},{8,12},{12,8},{1,5},{5,1},{9,13},{13,9},{2,6},{6,2},{1... | collective-permute-start | bytes 786440 | tf_op jit(solution)/shard_map/ppermute | solution.py:234
  13.1 1.4 %collective-permute-done = bf16[2,256,256]{2,1,0:T(8,128)(2,1)S(1)} collective-permute-done((bf16[2,256,256]{2,1,0:T(8,128)(2,1)}, bf16[2,256,256]{2,1,0:T(8,128)(2,1)S(1)}, u32[]{:S(2)}, u32[]{:S(2)}) %collective-permute-start) | collective-permute-done | bytes 262176 | tf_op jit(solution)/shard_map/ppermute | solution.py:234
  14.4 1.1 %convert_add_fusion = f32[2,256,256]{2,1,0:T(8,128)S(1)} fusion(f32[2,256,256]{2,1,0:T(8,128)} %get-tuple-element.7, bf16[2,256,256]{2,1,0:T(8,128)(2,1)S(1)} %collective-permute-done), kind=kLoop, calls=%fused_computation | loop fusion | flops 262144 | bytes 1310720 | tf_op jit(solution)/shard_map/add | solution.py:235
  15.6 2.9 %collective-permute-start.1 = (bf16[2,2,64,128]{3,2,0,1:T(8,128)(2,1)S(1)}, bf16[2,2,64,128]{3,2,0,1:T(8,128)(2,1)S(1)}, u32[]{:S(2)}, u32[]{:S(2)}) collective-permute-start(bf16[2,2,64,128]{3,2,0,1:T(8,128)(2,1)S(1)} %fusion.1), channel_id=1, source_target_pairs={{0,8},{4,12},{8,0},{12,4},{1,9},{5,13},{9,1},{13,5},{2,10},{6,14},... | collective-permute-start | bytes 196616 | tf_op jit(solution)/shard_map/ppermute | solution.py:252
  18.6 1.7 %collective-permute-start.3 = (bf16[2,2,64,128]{3,2,1,0:T(8,128)(2,1)S(1)}, bf16[2,2,64,128]{3,2,1,0:T(8,128)(2,1)S(1)}, u32[]{:S(2)}, u32[]{:S(2)}) collective-permute-start(bf16[2,2,64,128]{3,2,1,0:T(8,128)(2,1)S(1)} %fusion.2), channel_id=1, source_target_pairs={{0,1},{1,0},{2,3},{3,2},{4,5},{5,4},{6,7},{7,6},{8,9},{9,8},{10,11... | collective-permute-start | bytes 196616 | tf_op jit(solution)/shard_map/ppermute | solution.py:252
  20.2 0.7 %collective-permute-done.1 = bf16[2,2,64,128]{3,2,0,1:T(8,128)(2,1)S(1)} collective-permute-done((bf16[2,2,64,128]{3,2,0,1:T(8,128)(2,1)S(1)}, bf16[2,2,64,128]{3,2,0,1:T(8,128)(2,1)S(1)}, u32[]{:S(2)}, u32[]{:S(2)}) %collective-permute-start.1) | collective-permute-done | bytes 65568 | tf_op jit(solution)/shard_map/ppermute | solution.py:252
  21.0 2.1 %collective-permute-start.2 = (bf16[2,64,128]{2,1,0:T(8,128)(2,1)S(1)}, bf16[2,64,128]{2,1,0:T(8,128)(2,1)S(1)}, u32[]{:S(2)}, u32[]{:S(2)}) collective-permute-start(bf16[2,64,128]{2,1,0:T(8,128)(2,1)S(1)} %fusion.9), channel_id=1, source_target_pairs={{0,1},{1,0},{2,3},{3,2},{4,5},{5,4},{6,7},{7,6},{8,9},{9,8},{10,11... | collective-permute-start | bytes 98312 | tf_op jit(solution)/shard_map/ppermute | solution.py:252
  23.1 0.0 collective-permute-done.3
  23.1 1.6 %collective-permute-start.4 = (bf16[2,64,128]{2,1,0:T(8,128)(2,1)S(1)}, bf16[2,64,128]{2,1,0:T(8,128)(2,1)S(1)}, u32[]{:S(2)}, u32[]{:S(2)}) collective-permute-start(bf16[2,64,128]{2,1,0:T(8,128)(2,1)S(1)} %fusion.10), channel_id=1, source_target_pairs={{0,8},{4,12},{8,0},{12,4},{1,9},{5,13},{9,1},{13,5},{2,10},{6,14},... | collective-permute-start | bytes 98312 | tf_op jit(solution)/shard_map/ppermute | solution.py:252
  24.7 0.3 collective-permute-done.2
  25.0 2.1 %collective-permute-done.4 = bf16[2,64,128]{2,1,0:T(8,128)(2,1)S(1)} collective-permute-done((bf16[2,64,128]{2,1,0:T(8,128)(2,1)S(1)}, bf16[2,64,128]{2,1,0:T(8,128)(2,1)S(1)}, u32[]{:S(2)}, u32[]{:S(2)}) %collective-permute-start.4) | collective-permute-done | bytes 32800 | tf_op jit(solution)/shard_map/ppermute | solution.py:252
  27.1 2.6 %collective-permute-start.5 = (bf16[64,256]{1,0:T(8,128)(2,1)S(1)}, bf16[64,256]{1,0:T(8,128)(2,1)S(1)}, u32[]{:S(2)}, u32[]{:S(2)}) collective-permute-start(bf16[64,256]{1,0:T(8,128)(2,1)S(1)} %fusion.11), channel_id=1, source_target_pairs={{0,2},{1,3},{2,0},{3,1},{4,6},{5,7},{6,4},{7,5},{8,10},{9,11},{10,... | collective-permute-start | bytes 98312 | tf_op jit(solution)/shard_map/ppermute | solution.py:252
  29.8 2.2 %collective-permute-done.5 = bf16[64,256]{1,0:T(8,128)(2,1)S(1)} collective-permute-done((bf16[64,256]{1,0:T(8,128)(2,1)S(1)}, bf16[64,256]{1,0:T(8,128)(2,1)S(1)}, u32[]{:S(2)}, u32[]{:S(2)}) %collective-permute-start.5) | collective-permute-done | bytes 32800 | tf_op jit(solution)/shard_map/ppermute | solution.py:252
  32.0 0.6 %fusion.8 = f32[256,64]{0,1:T(8,128)} fusion(s32[]{:T(128)S(6)} %select_n.37, f32[2,64,128]{2,1,0:T(8,128)S(1)} %bitcast_add_fusion.2, f32[2,64,128]{2,1,0:T(8,128)S(1)} %bitcast_add_fusion.1, bf16[64,256]{1,0:T(8,128)(2,1)S(1)} %collective-permute-done.5), kind=kLoop, calls=%fused_computation.17 | loop fusion | flops 49152 | bytes 229380 | tf_op jit(solution)/shard_map/transpose | solution.py:274
  (10 shorter events, 0.2 us)
Async XLA Ops:
  12.6 1.9 %collective-permute-start = (bf16[2,256,256]{2,1,0:T(8,128)(2,1)}, bf16[2,256,256]{2,1,0:T(8,128)(2,1)S(1)}, u32[]{:S(2)}, u32[]{:S(2)}) collective-permute-start(bf16[2,256,256]{2,1,0:T(8,128)(2,1)} %get-tuple-element.8), channel_id=1, source_target_pairs={{0,4},{4,0},{8,12},{12,8},{1,5},{5,1},{9,13},{13,9},{2,6},{6,2},{1... | collective-permute-start | bytes 786440 | tf_op jit(solution)/shard_map/ppermute | solution.py:234
  15.6 5.3 %collective-permute-start.1 = (bf16[2,2,64,128]{3,2,0,1:T(8,128)(2,1)S(1)}, bf16[2,2,64,128]{3,2,0,1:T(8,128)(2,1)S(1)}, u32[]{:S(2)}, u32[]{:S(2)}) collective-permute-start(bf16[2,2,64,128]{3,2,0,1:T(8,128)(2,1)S(1)} %fusion.1), channel_id=1, source_target_pairs={{0,8},{4,12},{8,0},{12,4},{1,9},{5,13},{9,1},{13,5},{2,10},{6,14},... | collective-permute-start | bytes 196616 | tf_op jit(solution)/shard_map/ppermute | solution.py:252
  18.6 4.5 %collective-permute-start.3 = (bf16[2,2,64,128]{3,2,1,0:T(8,128)(2,1)S(1)}, bf16[2,2,64,128]{3,2,1,0:T(8,128)(2,1)S(1)}, u32[]{:S(2)}, u32[]{:S(2)}) collective-permute-start(bf16[2,2,64,128]{3,2,1,0:T(8,128)(2,1)S(1)} %fusion.2), channel_id=1, source_target_pairs={{0,1},{1,0},{2,3},{3,2},{4,5},{5,4},{6,7},{7,6},{8,9},{9,8},{10,11... | collective-permute-start | bytes 196616 | tf_op jit(solution)/shard_map/ppermute | solution.py:252
  21.0 4.0 %collective-permute-start.2 = (bf16[2,64,128]{2,1,0:T(8,128)(2,1)S(1)}, bf16[2,64,128]{2,1,0:T(8,128)(2,1)S(1)}, u32[]{:S(2)}, u32[]{:S(2)}) collective-permute-start(bf16[2,64,128]{2,1,0:T(8,128)(2,1)S(1)} %fusion.9), channel_id=1, source_target_pairs={{0,1},{1,0},{2,3},{3,2},{4,5},{5,4},{6,7},{7,6},{8,9},{9,8},{10,11... | collective-permute-start | bytes 98312 | tf_op jit(solution)/shard_map/ppermute | solution.py:252
  23.1 4.0 %collective-permute-start.4 = (bf16[2,64,128]{2,1,0:T(8,128)(2,1)S(1)}, bf16[2,64,128]{2,1,0:T(8,128)(2,1)S(1)}, u32[]{:S(2)}, u32[]{:S(2)}) collective-permute-start(bf16[2,64,128]{2,1,0:T(8,128)(2,1)S(1)} %fusion.10), channel_id=1, source_target_pairs={{0,8},{4,12},{8,0},{12,4},{1,9},{5,13},{9,1},{13,5},{2,10},{6,14},... | collective-permute-start | bytes 98312 | tf_op jit(solution)/shard_map/ppermute | solution.py:252
  27.1 4.9 %collective-permute-start.5 = (bf16[64,256]{1,0:T(8,128)(2,1)S(1)}, bf16[64,256]{1,0:T(8,128)(2,1)S(1)}, u32[]{:S(2)}, u32[]{:S(2)}) collective-permute-start(bf16[64,256]{1,0:T(8,128)(2,1)S(1)} %fusion.11), channel_id=1, source_target_pairs={{0,2},{1,3},{2,0},{3,1},{4,6},{5,7},{6,4},{7,5},{8,10},{9,11},{10,... | collective-permute-start | bytes 98312 | tf_op jit(solution)/shard_map/ppermute | solution.py:252

commit v13 on v11

--- a/solution.py
+++ b/solution.py
@@ -33,12 +33,12 @@
 
 
 def correlate_kernel(
-    place_ref, moveouts_ref, uptime_ref, records_ref, templates_ref, send_ref, keep_ref,
+    place_ref, numbers_ref, records_ref, templates_ref, send_ref, keep_ref,
     masked, shifted, factor, loaded, bank, windows_a, windows_b, bank_a, bank_b, total, arrived,
     *, window, batch,
 ):
     components, stations, length = records_ref.shape
-    block_count = uptime_ref.shape[0]
+    block_count = numbers_ref.shape[0] - components
     rows = masked.shape[0]
     groups = up(window, GROUP) // GROUP
     margin = up(window, LANES)
@@ -75,7 +75,7 @@
         block = at // block_len
         limit = jnp.zeros((stations, LANES), jnp.int32)
         for s in range(stations):
-            limit = jnp.where(which == s, uptime_ref[block, s], limit)
+            limit = jnp.where(which == s, numbers_ref[components + block, s], limit)
         live = offsets + (at - block * block_len) < limit
         for j in range(components):
             values = records_ref[j, :, pl.ds(at, LANES)].astype(jnp.float32)
@@ -95,7 +95,7 @@
         for u in range(burst):
             for j in range(components):
                 c = j * stations + i * burst + u
-                moveout = moveouts_ref[j, i * burst + u]
+                moveout = numbers_ref[j, i * burst + u]
                 whole = moveout // LANES * LANES
                 base = pl.multiple_of(lead - margin - LANES - whole, LANES)
                 row = masked[pl.ds(c, 1), pl.ds(base, span + LANES)]
@@ -187,7 +187,7 @@
                 send_ref[x, r:r + LANES, h:h + LANES] = ordered(other, h).astype(send_ref.dtype)
 
 
-def correlate(place, records, templates, moveouts, uptime, hops):
+def correlate(place, numbers, records, templates, hops):
     components, stations, length = records.shape
     window, bank_size = templates.shape[2:]
     margin = up(window, LANES)
@@ -199,7 +199,7 @@
     vectors = pl.BlockSpec(memory_space=pltpu.VMEM)
     return pl.pallas_call(
         functools.partial(correlate_kernel, window=window, batch=batch),
-        in_specs=[scalars, scalars, scalars, vectors, pl.BlockSpec(memory_space=pl.ANY)],
+        in_specs=[scalars, scalars, vectors, pl.BlockSpec(memory_space=pl.ANY)],
         out_specs=[vectors] * 2,
         scratch_shapes=[
             pltpu.VMEM((rows, length + margin + LANES + up(MAXMO, LANES)), jnp.float32),
@@ -218,9 +218,9 @@
             jax.ShapeDtypeStruct((hops, region, bank_size), kind)
             for kind in (jnp.bfloat16, jnp.float32)
         ],
-        compiler_params=pltpu.CompilerParams(vmem_limit_bytes=58 * 2**20),
+        compiler_params=pltpu.CompilerParams(vmem_limit_bytes=52 * 2**20),
         name="correlate",
-    )(place, moveouts, uptime, records, templates)
+    )(place, numbers, records, templates)
 
 
 def body(records, templates, moveouts, uptime):
@@ -229,7 +229,7 @@
     t, z = lax.axis_index("tm"), lax.axis_index("chan")
     x = t // 2
     send, keep = correlate(
-        t.reshape(1), records.transpose(1, 0, 2), templates, moveouts.T, uptime.T, hops
+        t.reshape(1), jnp.concatenate([moveouts.T, uptime.T]), records.transpose(1, 0, 2), templates, hops
     )
     got = lax.ppermute(send, "tm", [(i, i ^ 1) for i in range(tm)])
     mine = keep + got.astype(jnp.float32)

time: 32.9 us -> 32 us (0.973)
  Pallas kernels: 12.6 us -> 11.4 us
  local copies, waits for them, and re-layouts: 0.04 us -> 0.94 us
  other arithmetic: 1.76 us -> 1.43 us
    pallas_call x1, Pallas kernels: 12.6 us -> 11.4 us  [correlate(): pl.pallas_call(functools.partial(correlate_kernel, window=window, batch=b...]
    add x1, other arithmetic: 1.09 us -> 0.05 us  [body(): mine = keep + got.astype(jnp.float32)]
    unnamed x0 -> x2, local copies, waits for them, and re-layouts: none -> 0.89 us
    concatenate x0 -> x1, other arithmetic: none -> 0.71 us  [body(): jnp.concatenate([moveouts.T, uptime.T])]
where the time goes in v13:
time: 32 us; the launch traced here: 31.8 us
  Pallas kernels  11.4 us (36%)
  waiting for transfers between devices  9.66 us (30%)
  starting transfers between devices  8.34 us (26%)
  other arithmetic  1.43 us (4%)
  local copies, waits for them, and re-layouts  0.94 us (3%)
    pallas_call x1, Pallas kernels, correlate(): pl.pallas_call(functools.partial(correlate_kernel, window=window, batch=b...  11.4 us
    ppermute x3, starting transfers between devices, body(): lax.ppermute(block.astype(jnp.bfloat16), 'chan', perm).astype(jnp.float32)  4.93 us
    ppermute x3, waiting for transfers between devices, body(): lax.ppermute(block.astype(jnp.bfloat16), 'chan', perm).astype(jnp.float32)  4.7 us
    ppermute x1, waiting for transfers between devices, body(): lax.ppermute(block.astype(jnp.bfloat16), 'tm', perm).astype(jnp.float32)  3.8 us
    ppermute x1, starting transfers between devices, body(): lax.ppermute(block.astype(jnp.bfloat16), 'tm', perm).astype(jnp.float32)  2.92 us
    ppermute x1, waiting for transfers between devices, body(): got = lax.ppermute(send, 'tm', [(i, i ^ 1) for i in range(tm)])  1.16 us
    unnamed x2, local copies, waits for them, and re-layouts  0.89 us
    concatenate x1, other arithmetic, body(): jnp.concatenate([moveouts.T, uptime.T])  0.71 us
  transfers between devices with their start and end apart: 5, of which 5 were waited for; matrix products, arithmetic and copies ran while one was open for 0% of the time, Pallas kernels for 0%

profile of v13, /device:TPU:0, one launch (start us, length us, event | category | flops | bytes accessed | tf_op | source)
XLA Modules:
  0.0 31.8 jit_solution(7360801254776169906)
XLA Ops:
  0.0 0.7 %pad_add_fusion.numbers_ref = s32[5,16]{1,0:T(8,128)S(1)} fusion(s32[2,16]{1,0:T(2,128)} %bitcast.29, s32[3,16]{1,0:T(4,128)} %bitcast.28), kind=kLoop, calls=%fused_computation.14 | loop fusion | flops 80 | bytes 640 | tf_op jit(solution)/shard_map/concatenate | solution.py:232
  0.7 0.0 copy-start
  0.7 0.9 %copy-done = bf16[16,3,1024]{2,0,1:T(8,128)(2,1)S(1)} copy-done((bf16[16,3,1024]{2,0,1:T(8,128)(2,1)S(1)}, bf16[16,3,1024]{2,0,1:T(8,128)(2,1)}, u32[]{:S(2)}) %copy-start) | copy-done | bytes 98328
  1.6 11.4 %correlate.1 = (bf16[2,256,256]{2,1,0:T(8,128)(2,1)S(1)}, f32[2,256,256]{2,1,0:T(8,128)S(1)}) custom-call(s32[1]{0:T(128)} %bitcast.place_ref, s32[5,16]{1,0:T(8,128)S(1)} %pad_add_fusion.numbers_ref, bf16[3,16,1024]{2,1,0:T(8,128)(2,1)S(1)} %bitcast.25, bf16[16,3,200,256]{3,2,1,0:T(8,128)(2,1)} %templates_ref.1), custom_call_target="tpu_custom_call" | custom-call | tf_op jit(solution)/shard_map/correlate/pallas_call | solution.py:200
  13.0 0.5 %collective-permute-start = (bf16[2,256,256]{2,1,0:T(8,128)(2,1)S(1)}, bf16[2,256,256]{2,1,0:T(8,128)(2,1)S(1)}, u32[]{:S(2)}, u32[]{:S(2)}) collective-permute-start(bf16[2,256,256]{2,1,0:T(8,128)(2,1)S(1)} %get-tuple-element.8), channel_id=1, source_target_pairs={{0,4},{4,0},{8,12},{12,8},{1,5},{5,1},{9,13},{13,9},{2,6},{6,2},{1... | collective-permute-start | bytes 786440 | tf_op jit(solution)/shard_map/ppermute | solution.py:234
  13.5 1.2 %collective-permute-done = bf16[2,256,256]{2,1,0:T(8,128)(2,1)S(1)} collective-permute-done((bf16[2,256,256]{2,1,0:T(8,128)(2,1)S(1)}, bf16[2,256,256]{2,1,0:T(8,128)(2,1)S(1)}, u32[]{:S(2)}, u32[]{:S(2)}) %collective-permute-start) | collective-permute-done | bytes 262176 | tf_op jit(solution)/shard_map/ppermute | solution.py:234
  14.7 0.1 convert_add_fusion
  14.8 2.9 %collective-permute-start.1 = (bf16[256,256]{1,0:T(8,128)(2,1)S(1)}, bf16[256,256]{1,0:T(8,128)(2,1)S(1)}, u32[]{:S(2)}, u32[]{:S(2)}) collective-permute-start(bf16[256,256]{1,0:T(8,128)(2,1)S(1)} %fusion), channel_id=1, source_target_pairs={{0,8},{4,12},{8,0},{12,4},{1,9},{5,13},{9,1},{13,5},{2,10},{6,14},... | collective-permute-start | bytes 393224 | tf_op jit(solution)/shard_map/ppermute | solution.py:240
  17.7 3.8 %collective-permute-done.1 = bf16[256,256]{1,0:T(8,128)(2,1)S(1)} collective-permute-done((bf16[256,256]{1,0:T(8,128)(2,1)S(1)}, bf16[256,256]{1,0:T(8,128)(2,1)S(1)}, u32[]{:S(2)}, u32[]{:S(2)}) %collective-permute-start.1) | collective-permute-done | bytes 131104 | tf_op jit(solution)/shard_map/ppermute | solution.py:240
  21.6 3.9 %collective-permute-start.4 = (bf16[64,256]{1,0:T(8,128)(2,1)S(1)}, bf16[64,256]{1,0:T(8,128)(2,1)S(1)}, u32[]{:S(2)}, u32[]{:S(2)}) collective-permute-start(bf16[64,256]{1,0:T(8,128)(2,1)S(1)} %get-tuple-element.10), channel_id=1, source_target_pairs={{0,3},{1,0},{2,1},{3,2},{4,7},{5,4},{6,5},{7,6},{8,11},{9,8},{10,9... | collective-permute-start | bytes 98312 | tf_op jit(solution)/shard_map/ppermute | solution.py:246
  25.5 0.0 collective-permute-start.3
  25.5 1.0 %collective-permute-start.2 = (bf16[64,256]{1,0:T(8,128)(2,1)S(1)}, bf16[64,256]{1,0:T(8,128)(2,1)S(1)}, u32[]{:S(2)}, u32[]{:S(2)}) collective-permute-start(bf16[64,256]{1,0:T(8,128)(2,1)S(1)} %get-tuple-element.9), channel_id=1, source_target_pairs={{0,1},{1,2},{2,3},{3,0},{4,5},{5,6},{6,7},{7,4},{8,9},{9,10},{10,1... | collective-permute-start | bytes 98312 | tf_op jit(solution)/shard_map/ppermute | solution.py:246
  26.5 0.6 %collective-permute-done.4 = bf16[64,256]{1,0:T(8,128)(2,1)S(1)} collective-permute-done((bf16[64,256]{1,0:T(8,128)(2,1)S(1)}, bf16[64,256]{1,0:T(8,128)(2,1)S(1)}, u32[]{:S(2)}, u32[]{:S(2)}) %collective-permute-start.4) | collective-permute-done | bytes 32800 | tf_op jit(solution)/shard_map/ppermute | solution.py:246
  27.1 3.2 %collective-permute-done.3 = bf16[64,256]{1,0:T(8,128)(2,1)S(1)} collective-permute-done((bf16[64,256]{1,0:T(8,128)(2,1)S(1)}, bf16[64,256]{1,0:T(8,128)(2,1)S(1)}, u32[]{:S(2)}, u32[]{:S(2)}) %collective-permute-start.3) | collective-permute-done | bytes 32800 | tf_op jit(solution)/shard_map/ppermute | solution.py:246
  30.3 0.9 %collective-permute-done.2 = bf16[64,256]{1,0:T(8,128)(2,1)S(1)} collective-permute-done((bf16[64,256]{1,0:T(8,128)(2,1)S(1)}, bf16[64,256]{1,0:T(8,128)(2,1)S(1)}, u32[]{:S(2)}, u32[]{:S(2)}) %collective-permute-start.2) | collective-permute-done | bytes 32800 | tf_op jit(solution)/shard_map/ppermute | solution.py:246
  31.2 0.6 %fusion.3 = f32[256,64]{0,1:T(8,128)} fusion(bf16[64,256]{1,0:T(8,128)(2,1)S(1)} %collective-permute-done.4, bf16[64,256]{1,0:T(8,128)(2,1)S(1)} %collective-permute-done.3, bf16[64,256]{1,0:T(8,128)(2,1)S(1)} %collective-permute-done.2, f32[4,64,256]{2,1,0:T(8,128)S(1)} %bitcast.27, s32[]{:T(128)S(6)} %select_n.47), kind=kLoop, calls=%fused_computation.7 | loop fusion | flops 98304 | bytes 229380 | tf_op jit(solution)/shard_map/transpose | solution.py:247
  (3 shorter events, 0.1 us)
Async XLA Ops:
  0.7 0.9 %copy-start = (bf16[16,3,1024]{2,0,1:T(8,128)(2,1)S(1)}, bf16[16,3,1024]{2,0,1:T(8,128)(2,1)}, u32[]{:S(2)}) copy-start(bf16[16,3,1024]{2,0,1:T(8,128)(2,1)} %param.4) | copy-start | bytes 294916
  13.0 1.7 %collective-permute-start = (bf16[2,256,256]{2,1,0:T(8,128)(2,1)S(1)}, bf16[2,256,256]{2,1,0:T(8,128)(2,1)S(1)}, u32[]{:S(2)}, u32[]{:S(2)}) collective-permute-start(bf16[2,256,256]{2,1,0:T(8,128)(2,1)S(1)} %get-tuple-element.8), channel_id=1, source_target_pairs={{0,4},{4,0},{8,12},{12,8},{1,5},{5,1},{9,13},{13,9},{2,6},{6,2},{1... | collective-permute-start | bytes 786440 | tf_op jit(solution)/shard_map/ppermute | solution.py:234
  14.8 6.7 %collective-permute-start.1 = (bf16[256,256]{1,0:T(8,128)(2,1)S(1)}, bf16[256,256]{1,0:T(8,128)(2,1)S(1)}, u32[]{:S(2)}, u32[]{:S(2)}) collective-permute-start(bf16[256,256]{1,0:T(8,128)(2,1)S(1)} %fusion), channel_id=1, source_target_pairs={{0,8},{4,12},{8,0},{12,4},{1,9},{5,13},{9,1},{13,5},{2,10},{6,14},... | collective-permute-start | bytes 393224 | tf_op jit(solution)/shard_map/ppermute | solution.py:240
  21.6 5.5 %collective-permute-start.4 = (bf16[64,256]{1,0:T(8,128)(2,1)S(1)}, bf16[64,256]{1,0:T(8,128)(2,1)S(1)}, u32[]{:S(2)}, u32[]{:S(2)}) collective-permute-start(bf16[64,256]{1,0:T(8,128)(2,1)S(1)} %get-tuple-element.10), channel_id=1, source_target_pairs={{0,3},{1,0},{2,1},{3,2},{4,7},{5,4},{6,5},{7,6},{8,11},{9,8},{10,9... | collective-permute-start | bytes 98312 | tf_op jit(solution)/shard_map/ppermute | solution.py:246
  25.5 4.8 %collective-permute-start.3 = (bf16[64,256]{1,0:T(8,128)(2,1)S(1)}, bf16[64,256]{1,0:T(8,128)(2,1)S(1)}, u32[]{:S(2)}, u32[]{:S(2)}) collective-permute-start(bf16[64,256]{1,0:T(8,128)(2,1)S(1)} %get-tuple-element.11), channel_id=1, source_target_pairs={{0,2},{1,3},{2,0},{3,1},{4,6},{5,7},{6,4},{7,5},{8,10},{9,11},{10,... | collective-permute-start | bytes 98312 | tf_op jit(solution)/shard_map/ppermute | solution.py:246
  25.5 5.7 %collective-permute-start.2 = (bf16[64,256]{1,0:T(8,128)(2,1)S(1)}, bf16[64,256]{1,0:T(8,128)(2,1)S(1)}, u32[]{:S(2)}, u32[]{:S(2)}) collective-permute-start(bf16[64,256]{1,0:T(8,128)(2,1)S(1)} %get-tuple-element.9), channel_id=1, source_target_pairs={{0,1},{1,2},{2,3},{3,0},{4,5},{5,6},{6,7},{7,4},{8,9},{9,10},{10,1... | collective-permute-start | bytes 98312 | tf_op jit(solution)/shard_map/ppermute | solution.py:246

commit v14 on v13

--- a/solution.py
+++ b/solution.py
@@ -240,9 +240,14 @@
         result = result + lax.ppermute(block.astype(jnp.bfloat16), "tm", perm).astype(jnp.float32)
     mine = result.reshape(chan, result.shape[0] // chan, result.shape[1])
     result = lax.dynamic_index_in_dim(mine, z, 0, keepdims=False)
+    paired = chan & (chan - 1) == 0
+
+    def partner(place, step):
+        return place ^ step if paired else (place + step) % chan
+
     for step in range(1, chan):
-        block = lax.dynamic_index_in_dim(mine, (z + step) % chan, 0, keepdims=False)
-        perm = [(i, (i + step) % chan) for i in range(chan)]
+        block = lax.dynamic_index_in_dim(mine, partner(z, step), 0, keepdims=False)
+        perm = [(i, partner(i, step)) for i in range(chan)]
         result = result + lax.ppermute(block.astype(jnp.bfloat16), "chan", perm).astype(jnp.float32)
     return result.T
 

time: 32 us -> 31.1 us (0.972)
  waiting for transfers between devices: 9.66 us -> 9.13 us
  starting transfers between devices: 8.34 us -> 8.02 us
    ppermute x3, waiting for transfers between devices: 4.7 us -> 4.17 us  [body(): lax.ppermute(block.astype(jnp.bfloat16), 'chan', perm).astype(jnp.float32)]
    ppermute x3, starting transfers between devices: 4.93 us -> 4.54 us  [body(): lax.ppermute(block.astype(jnp.bfloat16), 'chan', perm).astype(jnp.float32)]
  transfers between devices with their start and end apart: 5 -> 5, of which waited for: 5 -> 4; matrix products, arithmetic and copies ran while one was open for 0% -> 0% of each run, Pallas kernels for 0% -> 0%
where the time goes in v14:
time: 31.1 us; the launch traced here: 31 us
  Pallas kernels  11.4 us (37%)
  waiting for transfers between devices  9.13 us (29%)
  starting transfers between devices  8.02 us (26%)
  other arithmetic  1.43 us (5%)
  local copies, waits for them, and re-layouts  0.94 us (3%)
    pallas_call x1, Pallas kernels, correlate(): pl.pallas_call(functools.partial(correlate_kernel, window=window, batch=b...  11.4 us
    ppermute x3, starting transfers between devices, body(): lax.ppermute(block.astype(jnp.bfloat16), 'chan', perm).astype(jnp.float32)  4.54 us
    ppermute x3, waiting for transfers between devices, body(): lax.ppermute(block.astype(jnp.bfloat16), 'chan', perm).astype(jnp.float32)  4.17 us
    ppermute x1, waiting for transfers between devices, body(): lax.ppermute(block.astype(jnp.bfloat16), 'tm', perm).astype(jnp.float32)  3.8 us
    ppermute x1, starting transfers between devices, body(): lax.ppermute(block.astype(jnp.bfloat16), 'tm', perm).astype(jnp.float32)  2.95 us
    ppermute x1, waiting for transfers between devices, body(): got = lax.ppermute(send, 'tm', [(i, i ^ 1) for i in range(tm)])  1.16 us
    unnamed x2, local copies, waits for them, and re-layouts  0.89 us
    concatenate x1, other arithmetic, body(): jnp.concatenate([moveouts.T, uptime.T])  0.71 us
  transfers between devices with their start and end apart: 5, of which 4 were waited for; matrix products, arithmetic and copies ran while one was open for 0% of the time, Pallas kernels for 0%

profile of v14, /device:TPU:0, one launch (start us, length us, event | category | flops | bytes accessed | tf_op | source)
XLA Modules:
  0.0 31.0 jit_solution(4658682201996153302)
XLA Ops:
  0.0 0.7 %pad_add_fusion.numbers_ref = s32[5,16]{1,0:T(8,128)S(1)} fusion(s32[2,16]{1,0:T(2,128)} %bitcast.29, s32[3,16]{1,0:T(4,128)} %bitcast.28), kind=kLoop, calls=%fused_computation.14 | loop fusion | flops 80 | bytes 640 | tf_op jit(solution)/shard_map/concatenate | solution.py:232
  0.7 0.0 copy-start
  0.7 0.9 %copy-done = bf16[16,3,1024]{2,0,1:T(8,128)(2,1)S(1)} copy-done((bf16[16,3,1024]{2,0,1:T(8,128)(2,1)S(1)}, bf16[16,3,1024]{2,0,1:T(8,128)(2,1)}, u32[]{:S(2)}) %copy-start) | copy-done | bytes 98328
  1.6 11.4 %correlate.1 = (bf16[2,256,256]{2,1,0:T(8,128)(2,1)S(1)}, f32[2,256,256]{2,1,0:T(8,128)S(1)}) custom-call(s32[1]{0:T(128)} %bitcast.place_ref, s32[5,16]{1,0:T(8,128)S(1)} %pad_add_fusion.numbers_ref, bf16[3,16,1024]{2,1,0:T(8,128)(2,1)S(1)} %bitcast.25, bf16[16,3,200,256]{3,2,1,0:T(8,128)(2,1)} %templates_ref.1), custom_call_target="tpu_custom_call" | custom-call | tf_op jit(solution)/shard_map/correlate/pallas_call | solution.py:200
  13.0 0.5 %collective-permute-start = (bf16[2,256,256]{2,1,0:T(8,128)(2,1)S(1)}, bf16[2,256,256]{2,1,0:T(8,128)(2,1)S(1)}, u32[]{:S(2)}, u32[]{:S(2)}) collective-permute-start(bf16[2,256,256]{2,1,0:T(8,128)(2,1)S(1)} %get-tuple-element.8), channel_id=1, source_target_pairs={{0,4},{4,0},{8,12},{12,8},{1,5},{5,1},{9,13},{13,9},{2,6},{6,2},{1... | collective-permute-start | bytes 786440 | tf_op jit(solution)/shard_map/ppermute | solution.py:234
  13.5 1.2 %collective-permute-done = bf16[2,256,256]{2,1,0:T(8,128)(2,1)S(1)} collective-permute-done((bf16[2,256,256]{2,1,0:T(8,128)(2,1)S(1)}, bf16[2,256,256]{2,1,0:T(8,128)(2,1)S(1)}, u32[]{:S(2)}, u32[]{:S(2)}) %collective-permute-start) | collective-permute-done | bytes 262176 | tf_op jit(solution)/shard_map/ppermute | solution.py:234
  14.7 0.1 convert_add_fusion
  14.8 3.0 %collective-permute-start.1 = (bf16[256,256]{1,0:T(8,128)(2,1)S(1)}, bf16[256,256]{1,0:T(8,128)(2,1)S(1)}, u32[]{:S(2)}, u32[]{:S(2)}) collective-permute-start(bf16[256,256]{1,0:T(8,128)(2,1)S(1)} %fusion), channel_id=1, source_target_pairs={{0,8},{4,12},{8,0},{12,4},{1,9},{5,13},{9,1},{13,5},{2,10},{6,14},... | collective-permute-start | bytes 393224 | tf_op jit(solution)/shard_map/ppermute | solution.py:240
  17.7 3.8 %collective-permute-done.1 = bf16[256,256]{1,0:T(8,128)(2,1)S(1)} collective-permute-done((bf16[256,256]{1,0:T(8,128)(2,1)S(1)}, bf16[256,256]{1,0:T(8,128)(2,1)S(1)}, u32[]{:S(2)}, u32[]{:S(2)}) %collective-permute-start.1) | collective-permute-done | bytes 131104 | tf_op jit(solution)/shard_map/ppermute | solution.py:240
  21.6 3.9 %collective-permute-start.4 = (bf16[64,256]{1,0:T(8,128)(2,1)S(1)}, bf16[64,256]{1,0:T(8,128)(2,1)S(1)}, u32[]{:S(2)}, u32[]{:S(2)}) collective-permute-start(bf16[64,256]{1,0:T(8,128)(2,1)S(1)} %get-tuple-element.10), channel_id=1, source_target_pairs={{0,3},{1,2},{2,1},{3,0},{4,7},{5,6},{6,5},{7,4},{8,11},{9,10},{10,... | collective-permute-start | bytes 98312 | tf_op jit(solution)/shard_map/ppermute | solution.py:251
  25.5 0.0 collective-permute-start.3
  25.5 0.6 %collective-permute-start.2 = (bf16[64,256]{1,0:T(8,128)(2,1)S(1)}, bf16[64,256]{1,0:T(8,128)(2,1)S(1)}, u32[]{:S(2)}, u32[]{:S(2)}) collective-permute-start(bf16[64,256]{1,0:T(8,128)(2,1)S(1)} %get-tuple-element.9), channel_id=1, source_target_pairs={{0,1},{1,0},{2,3},{3,2},{4,5},{5,4},{6,7},{7,6},{8,9},{9,8},{10,11... | collective-permute-start | bytes 98312 | tf_op jit(solution)/shard_map/ppermute | solution.py:251
  26.1 1.6 %collective-permute-done.4 = bf16[64,256]{1,0:T(8,128)(2,1)S(1)} collective-permute-done((bf16[64,256]{1,0:T(8,128)(2,1)S(1)}, bf16[64,256]{1,0:T(8,128)(2,1)S(1)}, u32[]{:S(2)}, u32[]{:S(2)}) %collective-permute-start.4) | collective-permute-done | bytes 32800 | tf_op jit(solution)/shard_map/ppermute | solution.py:251
  27.8 2.5 %collective-permute-done.3 = bf16[64,256]{1,0:T(8,128)(2,1)S(1)} collective-permute-done((bf16[64,256]{1,0:T(8,128)(2,1)S(1)}, bf16[64,256]{1,0:T(8,128)(2,1)S(1)}, u32[]{:S(2)}, u32[]{:S(2)}) %collective-permute-start.3) | collective-permute-done | bytes 32800 | tf_op jit(solution)/shard_map/ppermute | solution.py:251
  30.3 0.0 collective-permute-done.2
  30.3 0.6 %fusion.3 = f32[256,64]{0,1:T(8,128)} fusion(bf16[64,256]{1,0:T(8,128)(2,1)S(1)} %collective-permute-done.4, bf16[64,256]{1,0:T(8,128)(2,1)S(1)} %collective-permute-done.3, bf16[64,256]{1,0:T(8,128)(2,1)S(1)} %collective-permute-done.2, f32[4,64,256]{2,1,0:T(8,128)S(1)} %bitcast.27, s32[]{:T(128)S(6)} %select_n.35), kind=kLoop, calls=%fused_computation.7 | loop fusion | flops 98304 | bytes 229380 | tf_op jit(solution)/shard_map/transpose | solution.py:252
  (3 shorter events, 0.1 us)
Async XLA Ops:
  0.7 0.9 %copy-start = (bf16[16,3,1024]{2,0,1:T(8,128)(2,1)S(1)}, bf16[16,3,1024]{2,0,1:T(8,128)(2,1)}, u32[]{:S(2)}) copy-start(bf16[16,3,1024]{2,0,1:T(8,128)(2,1)} %param.4) | copy-start | bytes 294916
  13.0 1.7 %collective-permute-start = (bf16[2,256,256]{2,1,0:T(8,128)(2,1)S(1)}, bf16[2,256,256]{2,1,0:T(8,128)(2,1)S(1)}, u32[]{:S(2)}, u32[]{:S(2)}) collective-permute-start(bf16[2,256,256]{2,1,0:T(8,128)(2,1)S(1)} %get-tuple-element.8), channel_id=1, source_target_pairs={{0,4},{4,0},{8,12},{12,8},{1,5},{5,1},{9,13},{13,9},{2,6},{6,2},{1... | collective-permute-start | bytes 786440 | tf_op jit(solution)/shard_map/ppermute | solution.py:234
  14.8 6.8 %collective-permute-start.1 = (bf16[256,256]{1,0:T(8,128)(2,1)S(1)}, bf16[256,256]{1,0:T(8,128)(2,1)S(1)}, u32[]{:S(2)}, u32[]{:S(2)}) collective-permute-start(bf16[256,256]{1,0:T(8,128)(2,1)S(1)} %fusion), channel_id=1, source_target_pairs={{0,8},{4,12},{8,0},{12,4},{1,9},{5,13},{9,1},{13,5},{2,10},{6,14},... | collective-permute-start | bytes 393224 | tf_op jit(solution)/shard_map/ppermute | solution.py:240
  21.6 6.2 %collective-permute-start.4 = (bf16[64,256]{1,0:T(8,128)(2,1)S(1)}, bf16[64,256]{1,0:T(8,128)(2,1)S(1)}, u32[]{:S(2)}, u32[]{:S(2)}) collective-permute-start(bf16[64,256]{1,0:T(8,128)(2,1)S(1)} %get-tuple-element.10), channel_id=1, source_target_pairs={{0,3},{1,2},{2,1},{3,0},{4,7},{5,6},{6,5},{7,4},{8,11},{9,10},{10,... | collective-permute-start | bytes 98312 | tf_op jit(solution)/shard_map/ppermute | solution.py:251
  25.5 4.8 %collective-permute-start.3 = (bf16[64,256]{1,0:T(8,128)(2,1)S(1)}, bf16[64,256]{1,0:T(8,128)(2,1)S(1)}, u32[]{:S(2)}, u32[]{:S(2)}) collective-permute-start(bf16[64,256]{1,0:T(8,128)(2,1)S(1)} %get-tuple-element.11), channel_id=1, source_target_pairs={{0,2},{1,3},{2,0},{3,1},{4,6},{5,7},{6,4},{7,5},{8,10},{9,11},{10,... | collective-permute-start | bytes 98312 | tf_op jit(solution)/shard_map/ppermute | solution.py:251
  25.5 4.8 %collective-permute-start.2 = (bf16[64,256]{1,0:T(8,128)(2,1)S(1)}, bf16[64,256]{1,0:T(8,128)(2,1)S(1)}, u32[]{:S(2)}, u32[]{:S(2)}) collective-permute-start(bf16[64,256]{1,0:T(8,128)(2,1)S(1)} %get-tuple-element.9), channel_id=1, source_target_pairs={{0,1},{1,0},{2,3},{3,2},{4,5},{5,4},{6,7},{7,6},{8,9},{9,8},{10,11... | collective-permute-start | bytes 98312 | tf_op jit(solution)/shard_map/ppermute | solution.py:251

commit v15 on v14

--- a/solution.py
+++ b/solution.py
@@ -60,11 +60,12 @@
     masked[:, :lead] = jnp.zeros((rows, lead), jnp.float32)
     shifted[...] = jnp.zeros(shifted.shape, jnp.float32)
     total[...] = jnp.zeros(total.shape, total.dtype)
-    for ref in (bank, bank_a, bank_b, windows_b):
-        ref[...] = jnp.zeros(ref.shape, ref.dtype)
+    bank[...] = jnp.zeros(bank.shape, bank.dtype)
     depth = batch * components * groups * GROUP
     if windows_a.shape[0] > depth:
-        windows_a[depth:, :] = jnp.zeros((windows_a.shape[0] - depth, length), windows_a.dtype)
+        for windows in (windows_a, windows_b):
+            rest = (windows.shape[0] - depth, length)
+            windows[depth:, :] = jnp.zeros(rest, windows.dtype)
     offsets = lax.broadcasted_iota(jnp.int32, (stations, LANES), 1)
     which = lax.broadcasted_iota(jnp.int32, (stations, LANES), 0)
     mirror = LANES - 1 - lax.broadcasted_iota(jnp.int32, (up(stations, 8), LANES), 1)
@@ -138,7 +139,7 @@
             unit = (values * lax.rsqrt(squares + 1e-06)).astype(jnp.bfloat16)
             bank[m * groups * GROUP:m * groups * GROUP + window, :] = unit
         turned[...] = bank[...].T
-        left = list(range(0, length, width))
+        left = list(range(0, length, width)) if pending else []
         share = up(len(left), len(places)) // len(places)
         for m in range(len(places)):
             for a in range(min(groups, LANES // GROUP)):
@@ -151,24 +152,27 @@
                 multiply(n, *pending)
             left = left[share:]
 
+    a, b = (windows_a, bank_a), (windows_b, bank_b)
+    fetch(0).wait()
+    build(0, *a, None)
+
     def two_batches(i, carry):
-        @pl.when(2 * i < batches)
+        fetch(2 * i + 1).wait()
+        build(2 * i + 1, *b, a)
+
+        @pl.when(2 * i + 2 < batches)
         def _():
-            fetch(2 * i).wait()
-
-        build(jnp.minimum(2 * i, batches - 1), windows_a, bank_a, (windows_b, bank_b))
-
-        @pl.when(2 * i < batches)
-        def _():
-            @pl.when(2 * i + 1 < batches)
-            def _():
-                fetch(2 * i + 1).wait()
-
-            build(jnp.minimum(2 * i + 1, batches - 1), windows_b, bank_b, (windows_a, bank_a))
-
-        return carry
-
-    lax.fori_loop(0, batches // 2 + 1, two_batches, 0)
+            fetch(2 * i + 2).wait()
+
+        build(jnp.minimum(2 * i + 2, batches - 1), *a, b)
+        return carry
+
+    if batches > 1:
+        lax.fori_loop(0, batches // 2, two_batches, 0)
+    if batches % 2:
+        for n in range(0, length, width):
+            multiply(n, *a)
+
     core = place_ref[0] % 2
     hops, region = keep_ref.shape[0], keep_ref.shape[1]
     flip = LANES - 1 - lax.broadcasted_iota(jnp.int32, (LANES, LANES), 1)

time: 31.1 us -> 30.6 us (0.984)
  Pallas kernels: 11.4 us -> 10.8 us
    pallas_call x1, Pallas kernels: 11.4 us -> 10.8 us  [correlate(): pl.pallas_call(functools.partial(correlate_kernel, window=window, batch=b...]
where the time goes in v15:
time: 30.6 us; the launch traced here: 30.4 us
  Pallas kernels  10.8 us (35%)
  waiting for transfers between devices  9.13 us (30%)
  starting transfers between devices  8 us (26%)
  other arithmetic  1.43 us (5%)
  local copies, waits for them, and re-layouts  0.94 us (3%)
    pallas_call x1, Pallas kernels, correlate(): pl.pallas_call(functools.partial(correlate_kernel, window=window, batch=b...  10.8 us
    ppermute x3, starting transfers between devices, body(): lax.ppermute(block.astype(jnp.bfloat16), 'chan', perm).astype(jnp.float32)  4.55 us
    ppermute x3, waiting for transfers between devices, body(): lax.ppermute(block.astype(jnp.bfloat16), 'chan', perm).astype(jnp.float32)  4.17 us
    ppermute x1, waiting for transfers between devices, body(): lax.ppermute(block.astype(jnp.bfloat16), 'tm', perm).astype(jnp.float32)  3.8 us
    ppermute x1, starting transfers between devices, body(): lax.ppermute(block.astype(jnp.bfloat16), 'tm', perm).astype(jnp.float32)  2.93 us
    ppermute x1, waiting for transfers between devices, body(): got = lax.ppermute(send, 'tm', [(i, i ^ 1) for i in range(tm)])  1.16 us
    unnamed x2, local copies, waits for them, and re-layouts  0.89 us
    concatenate x1, other arithmetic, body(): jnp.concatenate([moveouts.T, uptime.T])  0.71 us
  transfers between devices with their start and end apart: 5, of which 4 were waited for; matrix products, arithmetic and copies ran while one was open for 0% of the time, Pallas kernels for 0%

profile of v15, /device:TPU:0, one launch (start us, length us, event | category | flops | bytes accessed | tf_op | source)
XLA Modules:
  0.0 30.4 jit_solution(11663312765967991069)
XLA Ops:
  0.0 0.7 %pad_add_fusion.numbers_ref = s32[5,16]{1,0:T(8,128)S(1)} fusion(s32[2,16]{1,0:T(2,128)} %bitcast.29, s32[3,16]{1,0:T(4,128)} %bitcast.28), kind=kLoop, calls=%fused_computation.14 | loop fusion | flops 80 | bytes 640 | tf_op jit(solution)/shard_map/concatenate | solution.py:236
  0.7 0.0 copy-start
  0.7 0.9 %copy-done = bf16[16,3,1024]{2,0,1:T(8,128)(2,1)S(1)} copy-done((bf16[16,3,1024]{2,0,1:T(8,128)(2,1)S(1)}, bf16[16,3,1024]{2,0,1:T(8,128)(2,1)}, u32[]{:S(2)}) %copy-start) | copy-done | bytes 98328
  1.6 10.8 %correlate.1 = (bf16[2,256,256]{2,1,0:T(8,128)(2,1)S(1)}, f32[2,256,256]{2,1,0:T(8,128)S(1)}) custom-call(s32[1]{0:T(128)} %bitcast.place_ref, s32[5,16]{1,0:T(8,128)S(1)} %pad_add_fusion.numbers_ref, bf16[3,16,1024]{2,1,0:T(8,128)(2,1)S(1)} %bitcast.25, bf16[16,3,200,256]{3,2,1,0:T(8,128)(2,1)} %templates_ref.1), custom_call_target="tpu_custom_call" | custom-call | tf_op jit(solution)/shard_map/correlate/pallas_call | solution.py:204
  12.4 0.5 %collective-permute-start = (bf16[2,256,256]{2,1,0:T(8,128)(2,1)S(1)}, bf16[2,256,256]{2,1,0:T(8,128)(2,1)S(1)}, u32[]{:S(2)}, u32[]{:S(2)}) collective-permute-start(bf16[2,256,256]{2,1,0:T(8,128)(2,1)S(1)} %get-tuple-element.8), channel_id=1, source_target_pairs={{0,4},{4,0},{8,12},{12,8},{1,5},{5,1},{9,13},{13,9},{2,6},{6,2},{1... | collective-permute-start | bytes 786440 | tf_op jit(solution)/shard_map/ppermute | solution.py:238
  13.0 1.2 %collective-permute-done = bf16[2,256,256]{2,1,0:T(8,128)(2,1)S(1)} collective-permute-done((bf16[2,256,256]{2,1,0:T(8,128)(2,1)S(1)}, bf16[2,256,256]{2,1,0:T(8,128)(2,1)S(1)}, u32[]{:S(2)}, u32[]{:S(2)}) %collective-permute-start) | collective-permute-done | bytes 262176 | tf_op jit(solution)/shard_map/ppermute | solution.py:238
  14.1 0.1 convert_add_fusion
  14.2 2.9 %collective-permute-start.1 = (bf16[256,256]{1,0:T(8,128)(2,1)S(1)}, bf16[256,256]{1,0:T(8,128)(2,1)S(1)}, u32[]{:S(2)}, u32[]{:S(2)}) collective-permute-start(bf16[256,256]{1,0:T(8,128)(2,1)S(1)} %fusion), channel_id=1, source_target_pairs={{0,8},{4,12},{8,0},{12,4},{1,9},{5,13},{9,1},{13,5},{2,10},{6,14},... | collective-permute-start | bytes 393224 | tf_op jit(solution)/shard_map/ppermute | solution.py:244
  17.1 3.8 %collective-permute-done.1 = bf16[256,256]{1,0:T(8,128)(2,1)S(1)} collective-permute-done((bf16[256,256]{1,0:T(8,128)(2,1)S(1)}, bf16[256,256]{1,0:T(8,128)(2,1)S(1)}, u32[]{:S(2)}, u32[]{:S(2)}) %collective-permute-start.1) | collective-permute-done | bytes 131104 | tf_op jit(solution)/shard_map/ppermute | solution.py:244
  21.0 3.9 %collective-permute-start.4 = (bf16[64,256]{1,0:T(8,128)(2,1)S(1)}, bf16[64,256]{1,0:T(8,128)(2,1)S(1)}, u32[]{:S(2)}, u32[]{:S(2)}) collective-permute-start(bf16[64,256]{1,0:T(8,128)(2,1)S(1)} %get-tuple-element.10), channel_id=1, source_target_pairs={{0,3},{1,2},{2,1},{3,0},{4,7},{5,6},{6,5},{7,4},{8,11},{9,10},{10,... | collective-permute-start | bytes 98312 | tf_op jit(solution)/shard_map/ppermute | solution.py:255
  24.9 0.0 collective-permute-start.3
  24.9 0.6 %collective-permute-start.2 = (bf16[64,256]{1,0:T(8,128)(2,1)S(1)}, bf16[64,256]{1,0:T(8,128)(2,1)S(1)}, u32[]{:S(2)}, u32[]{:S(2)}) collective-permute-start(bf16[64,256]{1,0:T(8,128)(2,1)S(1)} %get-tuple-element.9), channel_id=1, source_target_pairs={{0,1},{1,0},{2,3},{3,2},{4,5},{5,4},{6,7},{7,6},{8,9},{9,8},{10,11... | collective-permute-start | bytes 98312 | tf_op jit(solution)/shard_map/ppermute | solution.py:255
  25.5 1.6 %collective-permute-done.4 = bf16[64,256]{1,0:T(8,128)(2,1)S(1)} collective-permute-done((bf16[64,256]{1,0:T(8,128)(2,1)S(1)}, bf16[64,256]{1,0:T(8,128)(2,1)S(1)}, u32[]{:S(2)}, u32[]{:S(2)}) %collective-permute-start.4) | collective-permute-done | bytes 32800 | tf_op jit(solution)/shard_map/ppermute | solution.py:255
  27.2 2.5 %collective-permute-done.3 = bf16[64,256]{1,0:T(8,128)(2,1)S(1)} collective-permute-done((bf16[64,256]{1,0:T(8,128)(2,1)S(1)}, bf16[64,256]{1,0:T(8,128)(2,1)S(1)}, u32[]{:S(2)}, u32[]{:S(2)}) %collective-permute-start.3) | collective-permute-done | bytes 32800 | tf_op jit(solution)/shard_map/ppermute | solution.py:255
  29.7 0.0 collective-permute-done.2
  29.7 0.6 %fusion.3 = f32[256,64]{0,1:T(8,128)} fusion(bf16[64,256]{1,0:T(8,128)(2,1)S(1)} %collective-permute-done.4, bf16[64,256]{1,0:T(8,128)(2,1)S(1)} %collective-permute-done.3, bf16[64,256]{1,0:T(8,128)(2,1)S(1)} %collective-permute-done.2, f32[4,64,256]{2,1,0:T(8,128)S(1)} %bitcast.27, s32[]{:T(128)S(6)} %select_n.35), kind=kLoop, calls=%fused_computation.7 | loop fusion | flops 98304 | bytes 229380 | tf_op jit(solution)/shard_map/transpose | solution.py:256
  (3 shorter events, 0.1 us)
Async XLA Ops:
  0.7 0.9 %copy-start = (bf16[16,3,1024]{2,0,1:T(8,128)(2,1)S(1)}, bf16[16,3,1024]{2,0,1:T(8,128)(2,1)}, u32[]{:S(2)}) copy-start(bf16[16,3,1024]{2,0,1:T(8,128)(2,1)} %param.4) | copy-start | bytes 294916
  12.4 1.7 %collective-permute-start = (bf16[2,256,256]{2,1,0:T(8,128)(2,1)S(1)}, bf16[2,256,256]{2,1,0:T(8,128)(2,1)S(1)}, u32[]{:S(2)}, u32[]{:S(2)}) collective-permute-start(bf16[2,256,256]{2,1,0:T(8,128)(2,1)S(1)} %get-tuple-element.8), channel_id=1, source_target_pairs={{0,4},{4,0},{8,12},{12,8},{1,5},{5,1},{9,13},{13,9},{2,6},{6,2},{1... | collective-permute-start | bytes 786440 | tf_op jit(solution)/shard_map/ppermute | solution.py:238
  14.2 6.7 %collective-permute-start.1 = (bf16[256,256]{1,0:T(8,128)(2,1)S(1)}, bf16[256,256]{1,0:T(8,128)(2,1)S(1)}, u32[]{:S(2)}, u32[]{:S(2)}) collective-permute-start(bf16[256,256]{1,0:T(8,128)(2,1)S(1)} %fusion), channel_id=1, source_target_pairs={{0,8},{4,12},{8,0},{12,4},{1,9},{5,13},{9,1},{13,5},{2,10},{6,14},... | collective-permute-start | bytes 393224 | tf_op jit(solution)/shard_map/ppermute | solution.py:244
  21.0 6.2 %collective-permute-start.4 = (bf16[64,256]{1,0:T(8,128)(2,1)S(1)}, bf16[64,256]{1,0:T(8,128)(2,1)S(1)}, u32[]{:S(2)}, u32[]{:S(2)}) collective-permute-start(bf16[64,256]{1,0:T(8,128)(2,1)S(1)} %get-tuple-element.10), channel_id=1, source_target_pairs={{0,3},{1,2},{2,1},{3,0},{4,7},{5,6},{6,5},{7,4},{8,11},{9,10},{10,... | collective-permute-start | bytes 98312 | tf_op jit(solution)/shard_map/ppermute | solution.py:255
  24.9 4.8 %collective-permute-start.3 = (bf16[64,256]{1,0:T(8,128)(2,1)S(1)}, bf16[64,256]{1,0:T(8,128)(2,1)S(1)}, u32[]{:S(2)}, u32[]{:S(2)}) collective-permute-start(bf16[64,256]{1,0:T(8,128)(2,1)S(1)} %get-tuple-element.11), channel_id=1, source_target_pairs={{0,2},{1,3},{2,0},{3,1},{4,6},{5,7},{6,4},{7,5},{8,10},{9,11},{10,... | collective-permute-start | bytes 98312 | tf_op jit(solution)/shard_map/ppermute | solution.py:255
  24.9 4.8 %collective-permute-start.2 = (bf16[64,256]{1,0:T(8,128)(2,1)S(1)}, bf16[64,256]{1,0:T(8,128)(2,1)S(1)}, u32[]{:S(2)}, u32[]{:S(2)}) collective-permute-start(bf16[64,256]{1,0:T(8,128)(2,1)S(1)} %get-tuple-element.9), channel_id=1, source_target_pairs={{0,1},{1,0},{2,3},{3,2},{4,5},{5,4},{6,7},{7,6},{8,9},{9,8},{10,11... | collective-permute-start | bytes 98312 | tf_op jit(solution)/shard_map/ppermute | solution.py:255

commit v16 on v15

--- a/solution.py
+++ b/solution.py
@@ -105,7 +105,8 @@
             shifted[pl.ds(c, 1), :] = row[:, LANES:]
         return carry
 
-    lax.fori_loop(0, stations // burst, shift_some, 0)
+    fetch(0).wait()
+    shift_some(0, 0)
     chunk = rows
 
     def energy_some(i, carry):
@@ -115,7 +116,7 @@
         factor[at, :] = lax.rsqrt(jnp.maximum(energy, 1.0))
         return carry
 
-    lax.fori_loop(0, rows // chunk, energy_some, 0)
+    energy_some(0, 0)
     width = min(2 * LANES, length)
 
     def multiply(n, windows, turned):
@@ -153,7 +154,6 @@
             left = left[share:]
 
     a, b = (windows_a, bank_a), (windows_b, bank_b)
-    fetch(0).wait()
     build(0, *a, None)
 
     def two_batches(i, carry):

time: 30.6 us -> 31.4 us (1.026)
  Pallas kernels: 10.8 us -> 11.7 us
    pallas_call x1, Pallas kernels: 10.8 us -> 11.7 us  [correlate(): pl.pallas_call(functools.partial(correlate_kernel, window=window, batch=b...]
where the time goes in v16:
time: 31.4 us; the launch traced here: 31.2 us
  Pallas kernels  11.7 us (37%)
  waiting for transfers between devices  9.13 us (29%)
  starting transfers between devices  8 us (25%)
  other arithmetic  1.43 us (5%)
  local copies, waits for them, and re-layouts  0.94 us (3%)
    pallas_call x1, Pallas kernels, correlate(): pl.pallas_call(functools.partial(correlate_kernel, window=window, batch=b...  11.7 us
    ppermute x3, starting transfers between devices, body(): lax.ppermute(block.astype(jnp.bfloat16), 'chan', perm).astype(jnp.float32)  4.56 us
    ppermute x3, waiting for transfers between devices, body(): lax.ppermute(block.astype(jnp.bfloat16), 'chan', perm).astype(jnp.float32)  4.17 us
    ppermute x1, waiting for transfers between devices, body(): lax.ppermute(block.astype(jnp.bfloat16), 'tm', perm).astype(jnp.float32)  3.8 us
    ppermute x1, starting transfers between devices, body(): lax.ppermute(block.astype(jnp.bfloat16), 'tm', perm).astype(jnp.float32)  2.92 us
    ppermute x1, waiting for transfers between devices, body(): got = lax.ppermute(send, 'tm', [(i, i ^ 1) for i in range(tm)])  1.16 us
    unnamed x2, local copies, waits for them, and re-layouts  0.89 us
    concatenate x1, other arithmetic, body(): jnp.concatenate([moveouts.T, uptime.T])  0.71 us
  transfers between devices with their start and end apart: 5, of which 4 were waited for; matrix products, arithmetic and copies ran while one was open for 0% of the time, Pallas kernels for 0%

profile of v16, /device:TPU:0, one launch (start us, length us, event | category | flops | bytes accessed | tf_op | source)
XLA Modules:
  0.0 31.2 jit_solution(8411150320979690915)
XLA Ops:
  0.0 0.7 %pad_add_fusion.numbers_ref = s32[5,16]{1,0:T(8,128)S(1)} fusion(s32[2,16]{1,0:T(2,128)} %bitcast.29, s32[3,16]{1,0:T(4,128)} %bitcast.28), kind=kLoop, calls=%fused_computation.14 | loop fusion | flops 80 | bytes 640 | tf_op jit(solution)/shard_map/concatenate | solution.py:236
  0.7 0.0 copy-start
  0.7 0.9 %copy-done = bf16[16,3,1024]{2,0,1:T(8,128)(2,1)S(1)} copy-done((bf16[16,3,1024]{2,0,1:T(8,128)(2,1)S(1)}, bf16[16,3,1024]{2,0,1:T(8,128)(2,1)}, u32[]{:S(2)}) %copy-start) | copy-done | bytes 98328
  1.6 11.7 %correlate.1 = (bf16[2,256,256]{2,1,0:T(8,128)(2,1)S(1)}, f32[2,256,256]{2,1,0:T(8,128)S(1)}) custom-call(s32[1]{0:T(128)} %bitcast.place_ref, s32[5,16]{1,0:T(8,128)S(1)} %pad_add_fusion.numbers_ref, bf16[3,16,1024]{2,1,0:T(8,128)(2,1)S(1)} %bitcast.25, bf16[16,3,200,256]{3,2,1,0:T(8,128)(2,1)} %templates_ref.1), custom_call_target="tpu_custom_call" | custom-call | tf_op jit(solution)/shard_map/correlate/pallas_call | solution.py:204
  13.3 0.5 %collective-permute-start = (bf16[2,256,256]{2,1,0:T(8,128)(2,1)S(1)}, bf16[2,256,256]{2,1,0:T(8,128)(2,1)S(1)}, u32[]{:S(2)}, u32[]{:S(2)}) collective-permute-start(bf16[2,256,256]{2,1,0:T(8,128)(2,1)S(1)} %get-tuple-element.8), channel_id=1, source_target_pairs={{0,4},{4,0},{8,12},{12,8},{1,5},{5,1},{9,13},{13,9},{2,6},{6,2},{1... | collective-permute-start | bytes 786440 | tf_op jit(solution)/shard_map/ppermute | solution.py:238
  13.8 1.2 %collective-permute-done = bf16[2,256,256]{2,1,0:T(8,128)(2,1)S(1)} collective-permute-done((bf16[2,256,256]{2,1,0:T(8,128)(2,1)S(1)}, bf16[2,256,256]{2,1,0:T(8,128)(2,1)S(1)}, u32[]{:S(2)}, u32[]{:S(2)}) %collective-permute-start) | collective-permute-done | bytes 262176 | tf_op jit(solution)/shard_map/ppermute | solution.py:238
  15.0 0.1 convert_add_fusion
  15.1 2.9 %collective-permute-start.1 = (bf16[256,256]{1,0:T(8,128)(2,1)S(1)}, bf16[256,256]{1,0:T(8,128)(2,1)S(1)}, u32[]{:S(2)}, u32[]{:S(2)}) collective-permute-start(bf16[256,256]{1,0:T(8,128)(2,1)S(1)} %fusion), channel_id=1, source_target_pairs={{0,8},{4,12},{8,0},{12,4},{1,9},{5,13},{9,1},{13,5},{2,10},{6,14},... | collective-permute-start | bytes 393224 | tf_op jit(solution)/shard_map/ppermute | solution.py:244
  18.0 3.8 %collective-permute-done.1 = bf16[256,256]{1,0:T(8,128)(2,1)S(1)} collective-permute-done((bf16[256,256]{1,0:T(8,128)(2,1)S(1)}, bf16[256,256]{1,0:T(8,128)(2,1)S(1)}, u32[]{:S(2)}, u32[]{:S(2)}) %collective-permute-start.1) | collective-permute-done | bytes 131104 | tf_op jit(solution)/shard_map/ppermute | solution.py:244
  21.9 3.9 %collective-permute-start.4 = (bf16[64,256]{1,0:T(8,128)(2,1)S(1)}, bf16[64,256]{1,0:T(8,128)(2,1)S(1)}, u32[]{:S(2)}, u32[]{:S(2)}) collective-permute-start(bf16[64,256]{1,0:T(8,128)(2,1)S(1)} %get-tuple-element.10), channel_id=1, source_target_pairs={{0,3},{1,2},{2,1},{3,0},{4,7},{5,6},{6,5},{7,4},{8,11},{9,10},{10,... | collective-permute-start | bytes 98312 | tf_op jit(solution)/shard_map/ppermute | solution.py:255
  25.8 0.0 collective-permute-start.3
  25.8 0.6 %collective-permute-start.2 = (bf16[64,256]{1,0:T(8,128)(2,1)S(1)}, bf16[64,256]{1,0:T(8,128)(2,1)S(1)}, u32[]{:S(2)}, u32[]{:S(2)}) collective-permute-start(bf16[64,256]{1,0:T(8,128)(2,1)S(1)} %get-tuple-element.9), channel_id=1, source_target_pairs={{0,1},{1,0},{2,3},{3,2},{4,5},{5,4},{6,7},{7,6},{8,9},{9,8},{10,11... | collective-permute-start | bytes 98312 | tf_op jit(solution)/shard_map/ppermute | solution.py:255
  26.4 1.6 %collective-permute-done.4 = bf16[64,256]{1,0:T(8,128)(2,1)S(1)} collective-permute-done((bf16[64,256]{1,0:T(8,128)(2,1)S(1)}, bf16[64,256]{1,0:T(8,128)(2,1)S(1)}, u32[]{:S(2)}, u32[]{:S(2)}) %collective-permute-start.4) | collective-permute-done | bytes 32800 | tf_op jit(solution)/shard_map/ppermute | solution.py:255
  28.1 2.5 %collective-permute-done.3 = bf16[64,256]{1,0:T(8,128)(2,1)S(1)} collective-permute-done((bf16[64,256]{1,0:T(8,128)(2,1)S(1)}, bf16[64,256]{1,0:T(8,128)(2,1)S(1)}, u32[]{:S(2)}, u32[]{:S(2)}) %collective-permute-start.3) | collective-permute-done | bytes 32800 | tf_op jit(solution)/shard_map/ppermute | solution.py:255
  30.6 0.0 collective-permute-done.2
  30.6 0.6 %fusion.3 = f32[256,64]{0,1:T(8,128)} fusion(bf16[64,256]{1,0:T(8,128)(2,1)S(1)} %collective-permute-done.4, bf16[64,256]{1,0:T(8,128)(2,1)S(1)} %collective-permute-done.3, bf16[64,256]{1,0:T(8,128)(2,1)S(1)} %collective-permute-done.2, f32[4,64,256]{2,1,0:T(8,128)S(1)} %bitcast.27, s32[]{:T(128)S(6)} %select_n.35), kind=kLoop, calls=%fused_computation.7 | loop fusion | flops 98304 | bytes 229380 | tf_op jit(solution)/shard_map/transpose | solution.py:256
  (3 shorter events, 0.1 us)
Async XLA Ops:
  0.7 0.9 %copy-start = (bf16[16,3,1024]{2,0,1:T(8,128)(2,1)S(1)}, bf16[16,3,1024]{2,0,1:T(8,128)(2,1)}, u32[]{:S(2)}) copy-start(bf16[16,3,1024]{2,0,1:T(8,128)(2,1)} %param.4) | copy-start | bytes 294916
  13.3 1.7 %collective-permute-start = (bf16[2,256,256]{2,1,0:T(8,128)(2,1)S(1)}, bf16[2,256,256]{2,1,0:T(8,128)(2,1)S(1)}, u32[]{:S(2)}, u32[]{:S(2)}) collective-permute-start(bf16[2,256,256]{2,1,0:T(8,128)(2,1)S(1)} %get-tuple-element.8), channel_id=1, source_target_pairs={{0,4},{4,0},{8,12},{12,8},{1,5},{5,1},{9,13},{13,9},{2,6},{6,2},{1... | collective-permute-start | bytes 786440 | tf_op jit(solution)/shard_map/ppermute | solution.py:238
  15.1 6.7 %collective-permute-start.1 = (bf16[256,256]{1,0:T(8,128)(2,1)S(1)}, bf16[256,256]{1,0:T(8,128)(2,1)S(1)}, u32[]{:S(2)}, u32[]{:S(2)}) collective-permute-start(bf16[256,256]{1,0:T(8,128)(2,1)S(1)} %fusion), channel_id=1, source_target_pairs={{0,8},{4,12},{8,0},{12,4},{1,9},{5,13},{9,1},{13,5},{2,10},{6,14},... | collective-permute-start | bytes 393224 | tf_op jit(solution)/shard_map/ppermute | solution.py:244
  21.9 6.2 %collective-permute-start.4 = (bf16[64,256]{1,0:T(8,128)(2,1)S(1)}, bf16[64,256]{1,0:T(8,128)(2,1)S(1)}, u32[]{:S(2)}, u32[]{:S(2)}) collective-permute-start(bf16[64,256]{1,0:T(8,128)(2,1)S(1)} %get-tuple-element.10), channel_id=1, source_target_pairs={{0,3},{1,2},{2,1},{3,0},{4,7},{5,6},{6,5},{7,4},{8,11},{9,10},{10,... | collective-permute-start | bytes 98312 | tf_op jit(solution)/shard_map/ppermute | solution.py:255
  25.8 4.8 %collective-permute-start.3 = (bf16[64,256]{1,0:T(8,128)(2,1)S(1)}, bf16[64,256]{1,0:T(8,128)(2,1)S(1)}, u32[]{:S(2)}, u32[]{:S(2)}) collective-permute-start(bf16[64,256]{1,0:T(8,128)(2,1)S(1)} %get-tuple-element.11), channel_id=1, source_target_pairs={{0,2},{1,3},{2,0},{3,1},{4,6},{5,7},{6,4},{7,5},{8,10},{9,11},{10,... | collective-permute-start | bytes 98312 | tf_op jit(solution)/shard_map/ppermute | solution.py:255
  25.8 4.8 %collective-permute-start.2 = (bf16[64,256]{1,0:T(8,128)(2,1)S(1)}, bf16[64,256]{1,0:T(8,128)(2,1)S(1)}, u32[]{:S(2)}, u32[]{:S(2)}) collective-permute-start(bf16[64,256]{1,0:T(8,128)(2,1)S(1)} %get-tuple-element.9), channel_id=1, source_target_pairs={{0,1},{1,0},{2,3},{3,2},{4,5},{5,4},{6,7},{7,6},{8,9},{9,8},{10,11... | collective-permute-start | bytes 98312 | tf_op jit(solution)/shard_map/ppermute | solution.py:255

commit v17 on v15

--- a/solution.py
+++ b/solution.py
@@ -55,7 +55,7 @@
         return carry
 
     batches = stations // batch
-    lax.fori_loop(0, batches, start, 0)
+    fetch(0).start()
 
     masked[:, :lead] = jnp.zeros((rows, lead), jnp.float32)
     shifted[...] = jnp.zeros(shifted.shape, jnp.float32)
@@ -106,6 +106,7 @@
         return carry
 
     lax.fori_loop(0, stations // burst, shift_some, 0)
+    lax.fori_loop(1, batches, start, 0)
     chunk = rows
 
     def energy_some(i, carry):

time: 30.6 us -> 30.5 us (level)
  no operation moved by 1% of the time
where the time goes in v17:
time: 30.5 us; the launch traced here: 30.4 us
  Pallas kernels  10.8 us (35%)
  waiting for transfers between devices  9.13 us (30%)
  starting transfers between devices  7.99 us (26%)
  other arithmetic  1.43 us (5%)
  local copies, waits for them, and re-layouts  0.94 us (3%)
    pallas_call x1, Pallas kernels, correlate(): pl.pallas_call(functools.partial(correlate_kernel, window=window, batch=b...  10.8 us
    ppermute x3, starting transfers between devices, body(): lax.ppermute(block.astype(jnp.bfloat16), 'chan', perm).astype(jnp.float32)  4.55 us
    ppermute x3, waiting for transfers between devices, body(): lax.ppermute(block.astype(jnp.bfloat16), 'chan', perm).astype(jnp.float32)  4.17 us
    ppermute x1, waiting for transfers between devices, body(): lax.ppermute(block.astype(jnp.bfloat16), 'tm', perm).astype(jnp.float32)  3.8 us
    ppermute x1, starting transfers between devices, body(): lax.ppermute(block.astype(jnp.bfloat16), 'tm', perm).astype(jnp.float32)  2.93 us
    ppermute x1, waiting for transfers between devices, body(): got = lax.ppermute(send, 'tm', [(i, i ^ 1) for i in range(tm)])  1.16 us
    unnamed x2, local copies, waits for them, and re-layouts  0.89 us
    concatenate x1, other arithmetic, body(): jnp.concatenate([moveouts.T, uptime.T])  0.71 us
  transfers between devices with their start and end apart: 5, of which 4 were waited for; matrix products, arithmetic and copies ran while one was open for 0% of the time, Pallas kernels for 0%

profile of v17, /device:TPU:0, one launch (start us, length us, event | category | flops | bytes accessed | tf_op | source)
XLA Modules:
  0.0 30.4 jit_solution(13271436518708233900)
XLA Ops:
  0.0 0.7 %pad_add_fusion.numbers_ref = s32[5,16]{1,0:T(8,128)S(1)} fusion(s32[2,16]{1,0:T(2,128)} %bitcast.29, s32[3,16]{1,0:T(4,128)} %bitcast.28), kind=kLoop, calls=%fused_computation.14 | loop fusion | flops 80 | bytes 640 | tf_op jit(solution)/shard_map/concatenate | solution.py:237
  0.7 0.0 copy-start
  0.7 0.9 %copy-done = bf16[16,3,1024]{2,0,1:T(8,128)(2,1)S(1)} copy-done((bf16[16,3,1024]{2,0,1:T(8,128)(2,1)S(1)}, bf16[16,3,1024]{2,0,1:T(8,128)(2,1)}, u32[]{:S(2)}) %copy-start) | copy-done | bytes 98328
  1.6 10.8 %correlate.1 = (bf16[2,256,256]{2,1,0:T(8,128)(2,1)S(1)}, f32[2,256,256]{2,1,0:T(8,128)S(1)}) custom-call(s32[1]{0:T(128)} %bitcast.place_ref, s32[5,16]{1,0:T(8,128)S(1)} %pad_add_fusion.numbers_ref, bf16[3,16,1024]{2,1,0:T(8,128)(2,1)S(1)} %bitcast.25, bf16[16,3,200,256]{3,2,1,0:T(8,128)(2,1)} %templates_ref.1), custom_call_target="tpu_custom_call" | custom-call | tf_op jit(solution)/shard_map/correlate/pallas_call | solution.py:205
  12.4 0.5 %collective-permute-start = (bf16[2,256,256]{2,1,0:T(8,128)(2,1)S(1)}, bf16[2,256,256]{2,1,0:T(8,128)(2,1)S(1)}, u32[]{:S(2)}, u32[]{:S(2)}) collective-permute-start(bf16[2,256,256]{2,1,0:T(8,128)(2,1)S(1)} %get-tuple-element.8), channel_id=1, source_target_pairs={{0,4},{4,0},{8,12},{12,8},{1,5},{5,1},{9,13},{13,9},{2,6},{6,2},{1... | collective-permute-start | bytes 786440 | tf_op jit(solution)/shard_map/ppermute | solution.py:239
  13.0 1.2 %collective-permute-done = bf16[2,256,256]{2,1,0:T(8,128)(2,1)S(1)} collective-permute-done((bf16[2,256,256]{2,1,0:T(8,128)(2,1)S(1)}, bf16[2,256,256]{2,1,0:T(8,128)(2,1)S(1)}, u32[]{:S(2)}, u32[]{:S(2)}) %collective-permute-start) | collective-permute-done | bytes 262176 | tf_op jit(solution)/shard_map/ppermute | solution.py:239
  14.1 0.1 convert_add_fusion
  14.2 2.9 %collective-permute-start.1 = (bf16[256,256]{1,0:T(8,128)(2,1)S(1)}, bf16[256,256]{1,0:T(8,128)(2,1)S(1)}, u32[]{:S(2)}, u32[]{:S(2)}) collective-permute-start(bf16[256,256]{1,0:T(8,128)(2,1)S(1)} %fusion), channel_id=1, source_target_pairs={{0,8},{4,12},{8,0},{12,4},{1,9},{5,13},{9,1},{13,5},{2,10},{6,14},... | collective-permute-start | bytes 393224 | tf_op jit(solution)/shard_map/ppermute | solution.py:245
  17.1 3.8 %collective-permute-done.1 = bf16[256,256]{1,0:T(8,128)(2,1)S(1)} collective-permute-done((bf16[256,256]{1,0:T(8,128)(2,1)S(1)}, bf16[256,256]{1,0:T(8,128)(2,1)S(1)}, u32[]{:S(2)}, u32[]{:S(2)}) %collective-permute-start.1) | collective-permute-done | bytes 131104 | tf_op jit(solution)/shard_map/ppermute | solution.py:245
  21.0 3.9 %collective-permute-start.4 = (bf16[64,256]{1,0:T(8,128)(2,1)S(1)}, bf16[64,256]{1,0:T(8,128)(2,1)S(1)}, u32[]{:S(2)}, u32[]{:S(2)}) collective-permute-start(bf16[64,256]{1,0:T(8,128)(2,1)S(1)} %get-tuple-element.10), channel_id=1, source_target_pairs={{0,3},{1,2},{2,1},{3,0},{4,7},{5,6},{6,5},{7,4},{8,11},{9,10},{10,... | collective-permute-start | bytes 98312 | tf_op jit(solution)/shard_map/ppermute | solution.py:256
  24.9 0.0 collective-permute-start.3
  24.9 0.6 %collective-permute-start.2 = (bf16[64,256]{1,0:T(8,128)(2,1)S(1)}, bf16[64,256]{1,0:T(8,128)(2,1)S(1)}, u32[]{:S(2)}, u32[]{:S(2)}) collective-permute-start(bf16[64,256]{1,0:T(8,128)(2,1)S(1)} %get-tuple-element.9), channel_id=1, source_target_pairs={{0,1},{1,0},{2,3},{3,2},{4,5},{5,4},{6,7},{7,6},{8,9},{9,8},{10,11... | collective-permute-start | bytes 98312 | tf_op jit(solution)/shard_map/ppermute | solution.py:256
  25.5 1.6 %collective-permute-done.4 = bf16[64,256]{1,0:T(8,128)(2,1)S(1)} collective-permute-done((bf16[64,256]{1,0:T(8,128)(2,1)S(1)}, bf16[64,256]{1,0:T(8,128)(2,1)S(1)}, u32[]{:S(2)}, u32[]{:S(2)}) %collective-permute-start.4) | collective-permute-done | bytes 32800 | tf_op jit(solution)/shard_map/ppermute | solution.py:256
  27.2 2.5 %collective-permute-done.3 = bf16[64,256]{1,0:T(8,128)(2,1)S(1)} collective-permute-done((bf16[64,256]{1,0:T(8,128)(2,1)S(1)}, bf16[64,256]{1,0:T(8,128)(2,1)S(1)}, u32[]{:S(2)}, u32[]{:S(2)}) %collective-permute-start.3) | collective-permute-done | bytes 32800 | tf_op jit(solution)/shard_map/ppermute | solution.py:256
  29.7 0.0 collective-permute-done.2
  29.7 0.6 %fusion.3 = f32[256,64]{0,1:T(8,128)} fusion(bf16[64,256]{1,0:T(8,128)(2,1)S(1)} %collective-permute-done.4, bf16[64,256]{1,0:T(8,128)(2,1)S(1)} %collective-permute-done.3, bf16[64,256]{1,0:T(8,128)(2,1)S(1)} %collective-permute-done.2, f32[4,64,256]{2,1,0:T(8,128)S(1)} %bitcast.27, s32[]{:T(128)S(6)} %select_n.35), kind=kLoop, calls=%fused_computation.7 | loop fusion | flops 98304 | bytes 229380 | tf_op jit(solution)/shard_map/transpose | solution.py:257
  (3 shorter events, 0.1 us)
Async XLA Ops:
  0.7 0.9 %copy-start = (bf16[16,3,1024]{2,0,1:T(8,128)(2,1)S(1)}, bf16[16,3,1024]{2,0,1:T(8,128)(2,1)}, u32[]{:S(2)}) copy-start(bf16[16,3,1024]{2,0,1:T(8,128)(2,1)} %param.4) | copy-start | bytes 294916
  12.4 1.7 %collective-permute-start = (bf16[2,256,256]{2,1,0:T(8,128)(2,1)S(1)}, bf16[2,256,256]{2,1,0:T(8,128)(2,1)S(1)}, u32[]{:S(2)}, u32[]{:S(2)}) collective-permute-start(bf16[2,256,256]{2,1,0:T(8,128)(2,1)S(1)} %get-tuple-element.8), channel_id=1, source_target_pairs={{0,4},{4,0},{8,12},{12,8},{1,5},{5,1},{9,13},{13,9},{2,6},{6,2},{1... | collective-permute-start | bytes 786440 | tf_op jit(solution)/shard_map/ppermute | solution.py:239
  14.2 6.7 %collective-permute-start.1 = (bf16[256,256]{1,0:T(8,128)(2,1)S(1)}, bf16[256,256]{1,0:T(8,128)(2,1)S(1)}, u32[]{:S(2)}, u32[]{:S(2)}) collective-permute-start(bf16[256,256]{1,0:T(8,128)(2,1)S(1)} %fusion), channel_id=1, source_target_pairs={{0,8},{4,12},{8,0},{12,4},{1,9},{5,13},{9,1},{13,5},{2,10},{6,14},... | collective-permute-start | bytes 393224 | tf_op jit(solution)/shard_map/ppermute | solution.py:245
  21.0 6.2 %collective-permute-start.4 = (bf16[64,256]{1,0:T(8,128)(2,1)S(1)}, bf16[64,256]{1,0:T(8,128)(2,1)S(1)}, u32[]{:S(2)}, u32[]{:S(2)}) collective-permute-start(bf16[64,256]{1,0:T(8,128)(2,1)S(1)} %get-tuple-element.10), channel_id=1, source_target_pairs={{0,3},{1,2},{2,1},{3,0},{4,7},{5,6},{6,5},{7,4},{8,11},{9,10},{10,... | collective-permute-start | bytes 98312 | tf_op jit(solution)/shard_map/ppermute | solution.py:256
  24.9 4.8 %collective-permute-start.3 = (bf16[64,256]{1,0:T(8,128)(2,1)S(1)}, bf16[64,256]{1,0:T(8,128)(2,1)S(1)}, u32[]{:S(2)}, u32[]{:S(2)}) collective-permute-start(bf16[64,256]{1,0:T(8,128)(2,1)S(1)} %get-tuple-element.11), channel_id=1, source_target_pairs={{0,2},{1,3},{2,0},{3,1},{4,6},{5,7},{6,4},{7,5},{8,10},{9,11},{10,... | collective-permute-start | bytes 98312 | tf_op jit(solution)/shard_map/ppermute | solution.py:256
  24.9 4.8 %collective-permute-start.2 = (bf16[64,256]{1,0:T(8,128)(2,1)S(1)}, bf16[64,256]{1,0:T(8,128)(2,1)S(1)}, u32[]{:S(2)}, u32[]{:S(2)}) collective-permute-start(bf16[64,256]{1,0:T(8,128)(2,1)S(1)} %get-tuple-element.9), channel_id=1, source_target_pairs={{0,1},{1,0},{2,3},{3,2},{4,5},{5,4},{6,7},{7,6},{8,9},{9,8},{10,11... | collective-permute-start | bytes 98312 | tf_op jit(solution)/shard_map/ppermute | solution.py:256

commit v18 on v17

--- a/solution.py
+++ b/solution.py
@@ -117,7 +117,7 @@
         return carry
 
     lax.fori_loop(0, rows // chunk, energy_some, 0)
-    width = min(2 * LANES, length)
+    width = min(4 * LANES, length)
 
     def multiply(n, windows, turned):
         total[:, n:n + width] += jnp.dot(

time: 30.5 us -> 30.5 us (level)
  no operation moved by 1% of the time
where the time goes in v18:
time: 30.5 us; the launch traced here: 30.4 us
  Pallas kernels  10.8 us (35%)
  waiting for transfers between devices  9.13 us (30%)
  starting transfers between devices  8 us (26%)
  other arithmetic  1.43 us (5%)
  local copies, waits for them, and re-layouts  0.94 us (3%)
    pallas_call x1, Pallas kernels, correlate(): pl.pallas_call(functools.partial(correlate_kernel, window=window, batch=b...  10.8 us
    ppermute x3, starting transfers between devices, body(): lax.ppermute(block.astype(jnp.bfloat16), 'chan', perm).astype(jnp.float32)  4.56 us
    ppermute x3, waiting for transfers between devices, body(): lax.ppermute(block.astype(jnp.bfloat16), 'chan', perm).astype(jnp.float32)  4.17 us
    ppermute x1, waiting for transfers between devices, body(): lax.ppermute(block.astype(jnp.bfloat16), 'tm', perm).astype(jnp.float32)  3.8 us
    ppermute x1, starting transfers between devices, body(): lax.ppermute(block.astype(jnp.bfloat16), 'tm', perm).astype(jnp.float32)  2.92 us
    ppermute x1, waiting for transfers between devices, body(): got = lax.ppermute(send, 'tm', [(i, i ^ 1) for i in range(tm)])  1.16 us
    unnamed x2, local copies, waits for them, and re-layouts  0.89 us
    concatenate x1, other arithmetic, body(): jnp.concatenate([moveouts.T, uptime.T])  0.71 us
  transfers between devices with their start and end apart: 5, of which 4 were waited for; matrix products, arithmetic and copies ran while one was open for 0% of the time, Pallas kernels for 0%

profile of v18, /device:TPU:0, one launch (start us, length us, event | category | flops | bytes accessed | tf_op | source)
XLA Modules:
  0.0 30.4 jit_solution(13271436518708233900)
XLA Ops:
  0.0 0.7 %pad_add_fusion.numbers_ref = s32[5,16]{1,0:T(8,128)S(1)} fusion(s32[2,16]{1,0:T(2,128)} %bitcast.29, s32[3,16]{1,0:T(4,128)} %bitcast.28), kind=kLoop, calls=%fused_computation.14 | loop fusion | flops 80 | bytes 640 | tf_op jit(solution)/shard_map/concatenate | solution.py:237
  0.7 0.0 copy-start
  0.7 0.9 %copy-done = bf16[16,3,1024]{2,0,1:T(8,128)(2,1)S(1)} copy-done((bf16[16,3,1024]{2,0,1:T(8,128)(2,1)S(1)}, bf16[16,3,1024]{2,0,1:T(8,128)(2,1)}, u32[]{:S(2)}) %copy-start) | copy-done | bytes 98328
  1.6 10.8 %correlate.1 = (bf16[2,256,256]{2,1,0:T(8,128)(2,1)S(1)}, f32[2,256,256]{2,1,0:T(8,128)S(1)}) custom-call(s32[1]{0:T(128)} %bitcast.place_ref, s32[5,16]{1,0:T(8,128)S(1)} %pad_add_fusion.numbers_ref, bf16[3,16,1024]{2,1,0:T(8,128)(2,1)S(1)} %bitcast.25, bf16[16,3,200,256]{3,2,1,0:T(8,128)(2,1)} %templates_ref.1), custom_call_target="tpu_custom_call" | custom-call | tf_op jit(solution)/shard_map/correlate/pallas_call | solution.py:205
  12.4 0.5 %collective-permute-start = (bf16[2,256,256]{2,1,0:T(8,128)(2,1)S(1)}, bf16[2,256,256]{2,1,0:T(8,128)(2,1)S(1)}, u32[]{:S(2)}, u32[]{:S(2)}) collective-permute-start(bf16[2,256,256]{2,1,0:T(8,128)(2,1)S(1)} %get-tuple-element.8), channel_id=1, source_target_pairs={{0,4},{4,0},{8,12},{12,8},{1,5},{5,1},{9,13},{13,9},{2,6},{6,2},{1... | collective-permute-start | bytes 786440 | tf_op jit(solution)/shard_map/ppermute | solution.py:239
  13.0 1.2 %collective-permute-done = bf16[2,256,256]{2,1,0:T(8,128)(2,1)S(1)} collective-permute-done((bf16[2,256,256]{2,1,0:T(8,128)(2,1)S(1)}, bf16[2,256,256]{2,1,0:T(8,128)(2,1)S(1)}, u32[]{:S(2)}, u32[]{:S(2)}) %collective-permute-start) | collective-permute-done | bytes 262176 | tf_op jit(solution)/shard_map/ppermute | solution.py:239
  14.1 0.1 convert_add_fusion
  14.2 2.9 %collective-permute-start.1 = (bf16[256,256]{1,0:T(8,128)(2,1)S(1)}, bf16[256,256]{1,0:T(8,128)(2,1)S(1)}, u32[]{:S(2)}, u32[]{:S(2)}) collective-permute-start(bf16[256,256]{1,0:T(8,128)(2,1)S(1)} %fusion), channel_id=1, source_target_pairs={{0,8},{4,12},{8,0},{12,4},{1,9},{5,13},{9,1},{13,5},{2,10},{6,14},... | collective-permute-start | bytes 393224 | tf_op jit(solution)/shard_map/ppermute | solution.py:245
  17.1 3.8 %collective-permute-done.1 = bf16[256,256]{1,0:T(8,128)(2,1)S(1)} collective-permute-done((bf16[256,256]{1,0:T(8,128)(2,1)S(1)}, bf16[256,256]{1,0:T(8,128)(2,1)S(1)}, u32[]{:S(2)}, u32[]{:S(2)}) %collective-permute-start.1) | collective-permute-done | bytes 131104 | tf_op jit(solution)/shard_map/ppermute | solution.py:245
  21.0 3.9 %collective-permute-start.4 = (bf16[64,256]{1,0:T(8,128)(2,1)S(1)}, bf16[64,256]{1,0:T(8,128)(2,1)S(1)}, u32[]{:S(2)}, u32[]{:S(2)}) collective-permute-start(bf16[64,256]{1,0:T(8,128)(2,1)S(1)} %get-tuple-element.10), channel_id=1, source_target_pairs={{0,3},{1,2},{2,1},{3,0},{4,7},{5,6},{6,5},{7,4},{8,11},{9,10},{10,... | collective-permute-start | bytes 98312 | tf_op jit(solution)/shard_map/ppermute | solution.py:256
  24.9 0.0 collective-permute-start.3
  24.9 0.6 %collective-permute-start.2 = (bf16[64,256]{1,0:T(8,128)(2,1)S(1)}, bf16[64,256]{1,0:T(8,128)(2,1)S(1)}, u32[]{:S(2)}, u32[]{:S(2)}) collective-permute-start(bf16[64,256]{1,0:T(8,128)(2,1)S(1)} %get-tuple-element.9), channel_id=1, source_target_pairs={{0,1},{1,0},{2,3},{3,2},{4,5},{5,4},{6,7},{7,6},{8,9},{9,8},{10,11... | collective-permute-start | bytes 98312 | tf_op jit(solution)/shard_map/ppermute | solution.py:256
  25.5 1.6 %collective-permute-done.4 = bf16[64,256]{1,0:T(8,128)(2,1)S(1)} collective-permute-done((bf16[64,256]{1,0:T(8,128)(2,1)S(1)}, bf16[64,256]{1,0:T(8,128)(2,1)S(1)}, u32[]{:S(2)}, u32[]{:S(2)}) %collective-permute-start.4) | collective-permute-done | bytes 32800 | tf_op jit(solution)/shard_map/ppermute | solution.py:256
  27.2 2.5 %collective-permute-done.3 = bf16[64,256]{1,0:T(8,128)(2,1)S(1)} collective-permute-done((bf16[64,256]{1,0:T(8,128)(2,1)S(1)}, bf16[64,256]{1,0:T(8,128)(2,1)S(1)}, u32[]{:S(2)}, u32[]{:S(2)}) %collective-permute-start.3) | collective-permute-done | bytes 32800 | tf_op jit(solution)/shard_map/ppermute | solution.py:256
  29.7 0.0 collective-permute-done.2
  29.7 0.6 %fusion.3 = f32[256,64]{0,1:T(8,128)} fusion(bf16[64,256]{1,0:T(8,128)(2,1)S(1)} %collective-permute-done.4, bf16[64,256]{1,0:T(8,128)(2,1)S(1)} %collective-permute-done.3, bf16[64,256]{1,0:T(8,128)(2,1)S(1)} %collective-permute-done.2, f32[4,64,256]{2,1,0:T(8,128)S(1)} %bitcast.27, s32[]{:T(128)S(6)} %select_n.35), kind=kLoop, calls=%fused_computation.7 | loop fusion | flops 98304 | bytes 229380 | tf_op jit(solution)/shard_map/transpose | solution.py:257
  (3 shorter events, 0.1 us)
Async XLA Ops:
  0.7 0.9 %copy-start = (bf16[16,3,1024]{2,0,1:T(8,128)(2,1)S(1)}, bf16[16,3,1024]{2,0,1:T(8,128)(2,1)}, u32[]{:S(2)}) copy-start(bf16[16,3,1024]{2,0,1:T(8,128)(2,1)} %param.4) | copy-start | bytes 294916
  12.4 1.7 %collective-permute-start = (bf16[2,256,256]{2,1,0:T(8,128)(2,1)S(1)}, bf16[2,256,256]{2,1,0:T(8,128)(2,1)S(1)}, u32[]{:S(2)}, u32[]{:S(2)}) collective-permute-start(bf16[2,256,256]{2,1,0:T(8,128)(2,1)S(1)} %get-tuple-element.8), channel_id=1, source_target_pairs={{0,4},{4,0},{8,12},{12,8},{1,5},{5,1},{9,13},{13,9},{2,6},{6,2},{1... | collective-permute-start | bytes 786440 | tf_op jit(solution)/shard_map/ppermute | solution.py:239
  14.2 6.7 %collective-permute-start.1 = (bf16[256,256]{1,0:T(8,128)(2,1)S(1)}, bf16[256,256]{1,0:T(8,128)(2,1)S(1)}, u32[]{:S(2)}, u32[]{:S(2)}) collective-permute-start(bf16[256,256]{1,0:T(8,128)(2,1)S(1)} %fusion), channel_id=1, source_target_pairs={{0,8},{4,12},{8,0},{12,4},{1,9},{5,13},{9,1},{13,5},{2,10},{6,14},... | collective-permute-start | bytes 393224 | tf_op jit(solution)/shard_map/ppermute | solution.py:245
  21.0 6.2 %collective-permute-start.4 = (bf16[64,256]{1,0:T(8,128)(2,1)S(1)}, bf16[64,256]{1,0:T(8,128)(2,1)S(1)}, u32[]{:S(2)}, u32[]{:S(2)}) collective-permute-start(bf16[64,256]{1,0:T(8,128)(2,1)S(1)} %get-tuple-element.10), channel_id=1, source_target_pairs={{0,3},{1,2},{2,1},{3,0},{4,7},{5,6},{6,5},{7,4},{8,11},{9,10},{10,... | collective-permute-start | bytes 98312 | tf_op jit(solution)/shard_map/ppermute | solution.py:256
  24.9 4.8 %collective-permute-start.3 = (bf16[64,256]{1,0:T(8,128)(2,1)S(1)}, bf16[64,256]{1,0:T(8,128)(2,1)S(1)}, u32[]{:S(2)}, u32[]{:S(2)}) collective-permute-start(bf16[64,256]{1,0:T(8,128)(2,1)S(1)} %get-tuple-element.11), channel_id=1, source_target_pairs={{0,2},{1,3},{2,0},{3,1},{4,6},{5,7},{6,4},{7,5},{8,10},{9,11},{10,... | collective-permute-start | bytes 98312 | tf_op jit(solution)/shard_map/ppermute | solution.py:256
  24.9 4.8 %collective-permute-start.2 = (bf16[64,256]{1,0:T(8,128)(2,1)S(1)}, bf16[64,256]{1,0:T(8,128)(2,1)S(1)}, u32[]{:S(2)}, u32[]{:S(2)}) collective-permute-start(bf16[64,256]{1,0:T(8,128)(2,1)S(1)} %get-tuple-element.9), channel_id=1, source_target_pairs={{0,1},{1,0},{2,3},{3,2},{4,5},{5,4},{6,7},{7,6},{8,9},{9,8},{10,11... | collective-permute-start | bytes 98312 | tf_op jit(solution)/shard_map/ppermute | solution.py:256

commit v19 on v17

--- a/solution.py
+++ b/solution.py
@@ -107,16 +107,10 @@
 
     lax.fori_loop(0, stations // burst, shift_some, 0)
     lax.fori_loop(1, batches, start, 0)
-    chunk = rows
-
-    def energy_some(i, carry):
-        at = pl.ds(pl.multiple_of(i * chunk, 8), chunk)
-        values = shifted[at, :]
+    for g in range(0, rows, 8):
+        values = shifted[g:g + 8, :]
         energy = window_sum(values * values, window)[:, margin:]
-        factor[at, :] = lax.rsqrt(jnp.maximum(energy, 1.0))
-        return carry
-
-    lax.fori_loop(0, rows // chunk, energy_some, 0)
+        factor[g:g + 8, :] = lax.rsqrt(jnp.maximum(energy, 1.0))
     width = min(2 * LANES, length)
 
     def multiply(n, windows, turned):

time: 30.5 us -> 30.5 us (level)
  no operation moved by 1% of the time
where the time goes in v19:
time: 30.5 us; the launch traced here: 30.4 us
  Pallas kernels  10.8 us (35%)
  waiting for transfers between devices  9.13 us (30%)
  starting transfers between devices  8 us (26%)
  other arithmetic  1.43 us (5%)
  local copies, waits for them, and re-layouts  0.94 us (3%)
    pallas_call x1, Pallas kernels, correlate(): pl.pallas_call(functools.partial(correlate_kernel, window=window, batch=b...  10.8 us
    ppermute x3, starting transfers between devices, body(): lax.ppermute(block.astype(jnp.bfloat16), 'chan', perm).astype(jnp.float32)  4.56 us
    ppermute x3, waiting for transfers between devices, body(): lax.ppermute(block.astype(jnp.bfloat16), 'chan', perm).astype(jnp.float32)  4.17 us
    ppermute x1, waiting for transfers between devices, body(): lax.ppermute(block.astype(jnp.bfloat16), 'tm', perm).astype(jnp.float32)  3.8 us
    ppermute x1, starting transfers between devices, body(): lax.ppermute(block.astype(jnp.bfloat16), 'tm', perm).astype(jnp.float32)  2.93 us
    ppermute x1, waiting for transfers between devices, body(): got = lax.ppermute(send, 'tm', [(i, i ^ 1) for i in range(tm)])  1.16 us
    unnamed x2, local copies, waits for them, and re-layouts  0.89 us
    concatenate x1, other arithmetic, body(): jnp.concatenate([moveouts.T, uptime.T])  0.71 us
  transfers between devices with their start and end apart: 5, of which 4 were waited for; matrix products, arithmetic and copies ran while one was open for 0% of the time, Pallas kernels for 0%

profile of v19, /device:TPU:0, one launch (start us, length us, event | category | flops | bytes accessed | tf_op | source)
XLA Modules:
  0.0 30.4 jit_solution(10751402740502882533)
XLA Ops:
  0.0 0.7 %pad_add_fusion.numbers_ref = s32[5,16]{1,0:T(8,128)S(1)} fusion(s32[2,16]{1,0:T(2,128)} %bitcast.29, s32[3,16]{1,0:T(4,128)} %bitcast.28), kind=kLoop, calls=%fused_computation.14 | loop fusion | flops 80 | bytes 640 | tf_op jit(solution)/shard_map/concatenate | solution.py:231
  0.7 0.0 copy-start
  0.7 0.9 %copy-done = bf16[16,3,1024]{2,0,1:T(8,128)(2,1)S(1)} copy-done((bf16[16,3,1024]{2,0,1:T(8,128)(2,1)S(1)}, bf16[16,3,1024]{2,0,1:T(8,128)(2,1)}, u32[]{:S(2)}) %copy-start) | copy-done | bytes 98328
  1.6 10.8 %correlate.1 = (bf16[2,256,256]{2,1,0:T(8,128)(2,1)S(1)}, f32[2,256,256]{2,1,0:T(8,128)S(1)}) custom-call(s32[1]{0:T(128)} %bitcast.place_ref, s32[5,16]{1,0:T(8,128)S(1)} %pad_add_fusion.numbers_ref, bf16[3,16,1024]{2,1,0:T(8,128)(2,1)S(1)} %bitcast.25, bf16[16,3,200,256]{3,2,1,0:T(8,128)(2,1)} %templates_ref.1), custom_call_target="tpu_custom_call" | custom-call | tf_op jit(solution)/shard_map/correlate/pallas_call | solution.py:199
  12.4 0.5 %collective-permute-start = (bf16[2,256,256]{2,1,0:T(8,128)(2,1)S(1)}, bf16[2,256,256]{2,1,0:T(8,128)(2,1)S(1)}, u32[]{:S(2)}, u32[]{:S(2)}) collective-permute-start(bf16[2,256,256]{2,1,0:T(8,128)(2,1)S(1)} %get-tuple-element.8), channel_id=1, source_target_pairs={{0,4},{4,0},{8,12},{12,8},{1,5},{5,1},{9,13},{13,9},{2,6},{6,2},{1... | collective-permute-start | bytes 786440 | tf_op jit(solution)/shard_map/ppermute | solution.py:233
  12.9 1.2 %collective-permute-done = bf16[2,256,256]{2,1,0:T(8,128)(2,1)S(1)} collective-permute-done((bf16[2,256,256]{2,1,0:T(8,128)(2,1)S(1)}, bf16[2,256,256]{2,1,0:T(8,128)(2,1)S(1)}, u32[]{:S(2)}, u32[]{:S(2)}) %collective-permute-start) | collective-permute-done | bytes 262176 | tf_op jit(solution)/shard_map/ppermute | solution.py:233
  14.1 0.1 convert_add_fusion
  14.2 2.9 %collective-permute-start.1 = (bf16[256,256]{1,0:T(8,128)(2,1)S(1)}, bf16[256,256]{1,0:T(8,128)(2,1)S(1)}, u32[]{:S(2)}, u32[]{:S(2)}) collective-permute-start(bf16[256,256]{1,0:T(8,128)(2,1)S(1)} %fusion), channel_id=1, source_target_pairs={{0,8},{4,12},{8,0},{12,4},{1,9},{5,13},{9,1},{13,5},{2,10},{6,14},... | collective-permute-start | bytes 393224 | tf_op jit(solution)/shard_map/ppermute | solution.py:239
  17.1 3.8 %collective-permute-done.1 = bf16[256,256]{1,0:T(8,128)(2,1)S(1)} collective-permute-done((bf16[256,256]{1,0:T(8,128)(2,1)S(1)}, bf16[256,256]{1,0:T(8,128)(2,1)S(1)}, u32[]{:S(2)}, u32[]{:S(2)}) %collective-permute-start.1) | collective-permute-done | bytes 131104 | tf_op jit(solution)/shard_map/ppermute | solution.py:239
  21.0 3.9 %collective-permute-start.4 = (bf16[64,256]{1,0:T(8,128)(2,1)S(1)}, bf16[64,256]{1,0:T(8,128)(2,1)S(1)}, u32[]{:S(2)}, u32[]{:S(2)}) collective-permute-start(bf16[64,256]{1,0:T(8,128)(2,1)S(1)} %get-tuple-element.10), channel_id=1, source_target_pairs={{0,3},{1,2},{2,1},{3,0},{4,7},{5,6},{6,5},{7,4},{8,11},{9,10},{10,... | collective-permute-start | bytes 98312 | tf_op jit(solution)/shard_map/ppermute | solution.py:250
  24.9 0.0 collective-permute-start.3
  24.9 0.6 %collective-permute-start.2 = (bf16[64,256]{1,0:T(8,128)(2,1)S(1)}, bf16[64,256]{1,0:T(8,128)(2,1)S(1)}, u32[]{:S(2)}, u32[]{:S(2)}) collective-permute-start(bf16[64,256]{1,0:T(8,128)(2,1)S(1)} %get-tuple-element.9), channel_id=1, source_target_pairs={{0,1},{1,0},{2,3},{3,2},{4,5},{5,4},{6,7},{7,6},{8,9},{9,8},{10,11... | collective-permute-start | bytes 98312 | tf_op jit(solution)/shard_map/ppermute | solution.py:250
  25.5 1.6 %collective-permute-done.4 = bf16[64,256]{1,0:T(8,128)(2,1)S(1)} collective-permute-done((bf16[64,256]{1,0:T(8,128)(2,1)S(1)}, bf16[64,256]{1,0:T(8,128)(2,1)S(1)}, u32[]{:S(2)}, u32[]{:S(2)}) %collective-permute-start.4) | collective-permute-done | bytes 32800 | tf_op jit(solution)/shard_map/ppermute | solution.py:250
  27.2 2.5 %collective-permute-done.3 = bf16[64,256]{1,0:T(8,128)(2,1)S(1)} collective-permute-done((bf16[64,256]{1,0:T(8,128)(2,1)S(1)}, bf16[64,256]{1,0:T(8,128)(2,1)S(1)}, u32[]{:S(2)}, u32[]{:S(2)}) %collective-permute-start.3) | collective-permute-done | bytes 32800 | tf_op jit(solution)/shard_map/ppermute | solution.py:250
  29.7 0.0 collective-permute-done.2
  29.7 0.6 %fusion.3 = f32[256,64]{0,1:T(8,128)} fusion(bf16[64,256]{1,0:T(8,128)(2,1)S(1)} %collective-permute-done.4, bf16[64,256]{1,0:T(8,128)(2,1)S(1)} %collective-permute-done.3, bf16[64,256]{1,0:T(8,128)(2,1)S(1)} %collective-permute-done.2, f32[4,64,256]{2,1,0:T(8,128)S(1)} %bitcast.27, s32[]{:T(128)S(6)} %select_n.35), kind=kLoop, calls=%fused_computation.7 | loop fusion | flops 98304 | bytes 229380 | tf_op jit(solution)/shard_map/transpose | solution.py:251
  (3 shorter events, 0.1 us)
Async XLA Ops:
  0.7 0.9 %copy-start = (bf16[16,3,1024]{2,0,1:T(8,128)(2,1)S(1)}, bf16[16,3,1024]{2,0,1:T(8,128)(2,1)}, u32[]{:S(2)}) copy-start(bf16[16,3,1024]{2,0,1:T(8,128)(2,1)} %param.4) | copy-start | bytes 294916
  12.4 1.7 %collective-permute-start = (bf16[2,256,256]{2,1,0:T(8,128)(2,1)S(1)}, bf16[2,256,256]{2,1,0:T(8,128)(2,1)S(1)}, u32[]{:S(2)}, u32[]{:S(2)}) collective-permute-start(bf16[2,256,256]{2,1,0:T(8,128)(2,1)S(1)} %get-tuple-element.8), channel_id=1, source_target_pairs={{0,4},{4,0},{8,12},{12,8},{1,5},{5,1},{9,13},{13,9},{2,6},{6,2},{1... | collective-permute-start | bytes 786440 | tf_op jit(solution)/shard_map/ppermute | solution.py:233
  14.2 6.7 %collective-permute-start.1 = (bf16[256,256]{1,0:T(8,128)(2,1)S(1)}, bf16[256,256]{1,0:T(8,128)(2,1)S(1)}, u32[]{:S(2)}, u32[]{:S(2)}) collective-permute-start(bf16[256,256]{1,0:T(8,128)(2,1)S(1)} %fusion), channel_id=1, source_target_pairs={{0,8},{4,12},{8,0},{12,4},{1,9},{5,13},{9,1},{13,5},{2,10},{6,14},... | collective-permute-start | bytes 393224 | tf_op jit(solution)/shard_map/ppermute | solution.py:239
  21.0 6.2 %collective-permute-start.4 = (bf16[64,256]{1,0:T(8,128)(2,1)S(1)}, bf16[64,256]{1,0:T(8,128)(2,1)S(1)}, u32[]{:S(2)}, u32[]{:S(2)}) collective-permute-start(bf16[64,256]{1,0:T(8,128)(2,1)S(1)} %get-tuple-element.10), channel_id=1, source_target_pairs={{0,3},{1,2},{2,1},{3,0},{4,7},{5,6},{6,5},{7,4},{8,11},{9,10},{10,... | collective-permute-start | bytes 98312 | tf_op jit(solution)/shard_map/ppermute | solution.py:250
  24.9 4.8 %collective-permute-start.3 = (bf16[64,256]{1,0:T(8,128)(2,1)S(1)}, bf16[64,256]{1,0:T(8,128)(2,1)S(1)}, u32[]{:S(2)}, u32[]{:S(2)}) collective-permute-start(bf16[64,256]{1,0:T(8,128)(2,1)S(1)} %get-tuple-element.11), channel_id=1, source_target_pairs={{0,2},{1,3},{2,0},{3,1},{4,6},{5,7},{6,4},{7,5},{8,10},{9,11},{10,... | collective-permute-start | bytes 98312 | tf_op jit(solution)/shard_map/ppermute | solution.py:250
  24.9 4.8 %collective-permute-start.2 = (bf16[64,256]{1,0:T(8,128)(2,1)S(1)}, bf16[64,256]{1,0:T(8,128)(2,1)S(1)}, u32[]{:S(2)}, u32[]{:S(2)}) collective-permute-start(bf16[64,256]{1,0:T(8,128)(2,1)S(1)} %get-tuple-element.9), channel_id=1, source_target_pairs={{0,1},{1,0},{2,3},{3,2},{4,5},{5,4},{6,7},{7,6},{8,9},{9,8},{10,11... | collective-permute-start | bytes 98312 | tf_op jit(solution)/shard_map/ppermute | solution.py:250
